TPU v7x, 256 devices: a whole 4x4x8 slice. The times are simulated.
256 devices in a mesh: gx: 32 (over z, y_hi, core), gy: 8 (over y_lo, x).
Axes of the slice: x: 4, y: 4 (y_hi: 2, y_lo: 2; y = y_hi * 2 + y_lo), z: 8, core: 2. Of those that a mesh axis runs over, the one named last changes fastest.
Arguments:
- field: bfloat16 [256, 512, 256], P('gx', 'gy'), may hold values from -6 to 6
- norm_gain: float32 [2, 256], replicated, may hold values from 0.1 to 1.9
- inner_weight: bfloat16 [2, 256, 1024], replicated, may hold values from -0.375 to 0.375
- state_weight: bfloat16 [2, 256, 128], replicated, may hold values from -0.375 to 0.375
- step_weight: bfloat16 [2, 256, 8], replicated, may hold values from -0.375 to 0.375
- step_bias: float32 [2, 8], replicated, may hold values from -1 to 1
- decay_rate: float32 [2, 8], replicated, may hold values from 0.0005859375 to 0.05, as said below
- out_gain: float32 [2, 512], replicated, may hold values from 0.1 to 1.9
- out_weight: bfloat16 [2, 512, 256], replicated, may hold values from -0.25 to 0.25
Outputs:
- mixed: bfloat16 [256, 512, 256], P('gx', 'gy')
Inputs may be any that keep to these rules, and one draw needn't show every extreme that they name: `decay_rate`: decay rate of each layer's heads.
All inputs are finite; a program needn't handle non-finite values.
Results may differ from a plain program's by a relative error of at most 0.024.
Values may be sent and summed in bfloat16 or wider, within the bound.
No kernel may reach another device: no remote copies, remote signals or barrier semaphores. Data moves between devices by JAX's collectives and lax.ppermute only.
A program may use at most 64 MiB of HBM per device.

v0:
```python
import jax
import jax.numpy as jnp
from jax import lax
from jax.sharding import PartitionSpec as P

BLOCK = 64


EPSILON = 1e-05


def normalize(stream, gain):
    values = stream.astype(jnp.float32)
    scale = lax.rsqrt(jnp.mean(values * values, axis=-1, keepdims=True) + EPSILON)
    return (values * scale * gain).astype(jnp.bfloat16)


def project(normed, layer, weights):
    inner_weight, state_weight, step_weight, step_bias, decay_rate = weights[:5]
    length, lines, width = normed.shape
    heads = step_weight.shape[2]
    flat = normed.reshape(length * lines, width)
    inner = jnp.dot(flat, inner_weight[layer], preferred_element_type=jnp.float32)
    half = inner.shape[1] // 2
    gates = inner[:, :half].reshape(length, lines, half)
    inputs = (
        jax.nn.silu(inner[:, half:])
        .astype(jnp.bfloat16)
        .reshape(length, lines, heads, half // heads)
    )
    states = jnp.dot(flat, state_weight[layer], preferred_element_type=jnp.float32).astype(
        jnp.bfloat16
    )
    order = states.shape[1] // 2
    enter = states[:, :order].reshape(length, lines, order)
    leave = states[:, order:].reshape(length, lines, order)
    steps = jax.nn.softplus(
        jnp.dot(flat, step_weight[layer], preferred_element_type=jnp.float32) + step_bias[layer]
    )
    steps = steps.reshape(length, lines, heads)
    logdecay = -steps * decay_rate[layer]
    return (gates, (inputs, enter, leave, steps, logdecay))


def block_terms(inputs, enter, leave, steps, logdecay):
    span = inputs.shape[0]
    running = jnp.cumsum(logdecay, axis=0)
    scores = jnp.einsum("tmn,smn->mts", leave, enter, preferred_element_type=jnp.float32)
    across = jnp.transpose(running, (1, 2, 0))
    gap = across[:, :, :, None] - across[:, :, None, :]
    causal = jnp.arange(span)[:, None] >= jnp.arange(span)[None, :]
    decays = jnp.where(causal, jnp.exp(jnp.where(causal, gap, 0.0)), 0.0)
    mixing = (scores[:, None] * decays * jnp.transpose(steps, (1, 2, 0))[:, :, None, :]).astype(
        jnp.bfloat16
    )
    local_out = jnp.einsum("mhts,smhp->tmhp", mixing, inputs, preferred_element_type=jnp.float32)
    tail = jnp.exp(running[-1][None] - running) * steps
    carried = (inputs.astype(jnp.float32) * tail[..., None]).astype(jnp.bfloat16)
    end_state = jnp.einsum("smhp,smn->mhpn", carried, enter, preferred_element_type=jnp.float32)
    return (local_out, jnp.exp(running), jnp.exp(running[-1]), end_state)


def with_state(local_out, growth, leave, state):
    rounded = state.astype(jnp.bfloat16)
    incoming = jnp.einsum("tmn,mhpn->tmhp", leave, rounded, preferred_element_type=jnp.float32)
    return local_out + growth[..., None] * incoming


def to_blocks(array, count):
    span = array.shape[0] // count
    shaped = jnp.swapaxes(array.reshape((count, span) + array.shape[1:]), 0, 1)
    return shaped.reshape((span, count * array.shape[1]) + array.shape[2:])


def from_blocks(array, count):
    span = array.shape[0]
    lines = array.shape[1] // count
    shaped = jnp.swapaxes(array.reshape((span, count, lines) + array.shape[2:]), 0, 1)
    return shaped.reshape((count * span, lines) + array.shape[2:])


def chain_blocks(total, end_state):

    def advance(carry, item):
        factor, added = item
        return (factor[:, :, None, None] * carry + added, carry)

    _, states = lax.scan(advance, jnp.zeros_like(end_state[0]), (total, end_state))
    return states


def one_direction(arrays, count):
    pieces = [to_blocks(item, count) for item in arrays]
    local_out, growth, total, end_state = block_terms(*pieces)
    lines = arrays[0].shape[1]
    state = chain_blocks(
        total.reshape((count, lines) + total.shape[1:]),
        end_state.reshape((count, lines) + end_state.shape[1:]),
    )
    result = with_state(local_out, growth, pieces[2], state.reshape(end_state.shape))
    return from_blocks(result, count)


def line_mix(normed, layer, weights):
    out_gain, out_weight = (weights[5], weights[6])
    count = normed.shape[0] // BLOCK
    gates, arrays = project(normed, layer, weights)
    forward_out = one_direction(arrays, count)
    flipped = tuple((jnp.flip(item, 0) for item in arrays))
    backward_out = jnp.flip(one_direction(flipped, count), 0)
    length, lines = (gates.shape[0], gates.shape[1])
    gated = (forward_out + backward_out).reshape(gates.shape) * jax.nn.silu(gates)
    scale = lax.rsqrt(jnp.mean(gated * gated, axis=-1, keepdims=True) + EPSILON)
    rounded = (gated * scale * out_gain[layer]).astype(jnp.bfloat16)
    product = jnp.dot(
        rounded.reshape(length * lines, -1), out_weight[layer], preferred_element_type=jnp.float32
    )
    return product.reshape(length, lines, -1)


def on_device(
    field,
    norm_gain,
    inner_weight,
    state_weight,
    step_weight,
    step_bias,
    decay_rate,
    out_gain,
    out_weight,
):
    weights = (inner_weight, state_weight, step_weight, step_bias, decay_rate, out_gain, out_weight)
    normed = normalize(field, norm_gain[0])
    regrouped = lax.all_to_all(normed, "gx", split_axis=1, concat_axis=0, tiled=True)
    change = line_mix(regrouped, 0, weights)
    change = lax.all_to_all(
        change.astype(jnp.bfloat16), "gx", split_axis=0, concat_axis=1, tiled=True
    ).astype(change.dtype)
    stream = (field.astype(jnp.float32) + change).astype(jnp.bfloat16)
    normed = normalize(stream, norm_gain[1])
    regrouped = lax.all_to_all(normed, "gy", split_axis=0, concat_axis=1, tiled=True)
    change = line_mix(jnp.swapaxes(regrouped, 0, 1), 1, weights)
    change = lax.all_to_all(
        jnp.swapaxes(change, 0, 1).astype(jnp.bfloat16),
        "gy",
        split_axis=1,
        concat_axis=0,
        tiled=True,
    ).astype(jnp.float32)
    return (stream.astype(jnp.float32) + change).astype(jnp.bfloat16)


def solution(mesh):
    in_specs = (P("gx", "gy", None), P(), P(), P(), P(), P(), P(), P(), P())
    out_specs = P("gx", "gy", None)
    return jax.shard_map(
        on_device, mesh=mesh, in_specs=in_specs, out_specs=out_specs, check_vma=False
    )
```

profile of v0, /device:TPU:1, one launch (start us, length us, event | category | flops | bytes accessed | tf_op | source)
XLA Modules:
  0.0 281.7 jit_solution(1589744618820723215)
XLA Ops:
  4.4 12.8 %all-to-all-start = ((bf16[8,64,256]{2,0,1:T(8,128)(2,1)}), bf16[8,64,256]{2,0,1:T(8,128)(2,1)S(1)}, u32[]{:S(2)}, u32[]{:S(2)}) async-start(bf16[8,64,256]{2,0,1:T(8,128)(2,1)} %copy.242), calls=%async_computation | async-start | bytes 524288 | tf_op jit(solution)/shard_map/all_to_all | solution.py:134
  21.2 8.9 %all-to-all-done = bf16[8,64,256]{2,0,1:T(8,128)(2,1)S(1)} async-done(((bf16[8,64,256]{2,0,1:T(8,128)(2,1)}), bf16[8,64,256]{2,0,1:T(8,128)(2,1)S(1)}, u32[]{:S(2)}, u32[]{:S(2)}) %all-to-all-start) | async-done | bytes 262176 | tf_op jit(solution)/shard_map/all_to_all | solution.py:134
  33.4 2.4 reshape.387
  35.8 2.4 reshape_reshape.22
  43.0 6.3 %fusion.97 = f32[64,8,8]{2,1,0:T(8,128)S(1)} fusion(f32[64,8,8]{2,1,0:T(8,128)S(1)} %bitcast.430), kind=kOutput, calls=%fused_computation.171 | output fusion | flops 258048 | bytes 32768 | tf_op jit(solution)/shard_map/jit(cumsum)/reduce_window_sum | solution.py:47
  53.1 2.4 rev.36
  55.5 2.7 copy.259
  62.7 3.0 %fusion.14 = f32[8,8,64,64]{3,2,1,0:T(8,128)} fusion(bf16[64,8,64,1]{2,0,3,1:T(8,128)(2,1)S(1)} %bitcast.410, bf16[64,8,8,64]{0,3,2,1:T(8,128)(2,1)} %bitcast.380, f32[64,8,8]{0,2,1:T(8,128)} %copy.271), kind=kOutput, calls=%fused_computation.48 | convolution fusion | flops 34340864 | bytes 1654784 | tf_op jit(solution)/shard_map/smhp,smn->mhpn/dot_general | solution.py:59
  67.0 7.8 %while.53 = (s32[]{:T(128)}, f32[2,8,64,64]{3,2,1,0:T(8,128)S(1)}, bf16[4,2,8,64,64]{4,3,2,1,0:T(8,128)(2,1)}, f32[4,2,8]{2,1,0:T(2,128)S(1)}, f32[4,2,8,64,64]{4,3,2,1,0:T(8,128)}, /*index=5*/s32[]{:T(128)}, s32[]{:T(128)}) while((s32[]{:T(128)}, f32[2,8,64,64]{3,2,1,0:T(8,128)S(1)}, bf16[4,2,8,64,64]{4,3,2,1,0:T(8,128)(2,1)}, ...), condition=%wide.region_6.7_spmd.clone, body=%wide.region_5.6_spmd.clone.sunk | while | flops 262147 | bytes 1311520 | solution.py:88
  82.1 2.2 fusion.10
  86.1 3.1 %copy.272 = f32[4,64,2,8,64]{4,3,2,1,0:T(8,128)} copy(f32[4,64,2,8,64]{1,4,3,2,0:T(8,128)} %bitcast.374) | data formatting | bytes 2097152 | tf_op jit(solution)/shard_map/transpose | solution.py:78
  91.0 6.3 %fusion.96 = f32[64,8,8]{2,1,0:T(8,128)S(1)} fusion(f32[64,8,8]{2,1,0:T(8,128)S(1)} %copy.251), kind=kOutput, calls=%fused_computation.170 | output fusion | flops 258048 | bytes 32768 | tf_op jit(solution)/shard_map/jit(cumsum)/reduce_window_sum | solution.py:47
  98.9 2.7 copy.244
  101.7 3.0 %fusion.13 = f32[8,8,64,64]{3,2,1,0:T(8,128)} fusion(bf16[64,8,64,1]{2,0,3,1:T(8,128)(2,1)S(1)} %bitcast.414, bf16[64,8,8,64]{0,3,2,1:T(8,128)(2,1)} %bitcast.382, f32[64,8,8]{0,2,1:T(8,128)S(1)} %copy-done.21), kind=kOutput, calls=%fused_computation.47 | convolution fusion | flops 34340864 | bytes 1654784 | tf_op jit(solution)/shard_map/smhp,smn->mhpn/dot_general | solution.py:59
  105.9 7.8 %while.52 = (s32[]{:T(128)}, f32[2,8,64,64]{3,2,1,0:T(8,128)S(1)}, bf16[4,2,8,64,64]{4,3,2,1,0:T(8,128)(2,1)}, f32[4,2,8]{2,1,0:T(2,128)S(1)}, f32[4,2,8,64,64]{4,3,2,1,0:T(8,128)}, /*index=5*/s32[]{:T(128)}, s32[]{:T(128)}) while((s32[]{:T(128)}, f32[2,8,64,64]{3,2,1,0:T(8,128)S(1)}, bf16[4,2,8,64,64]{4,3,2,1,0:T(8,128)(2,1)}, ...), condition=%wide.region_3.4_spmd.clone, body=%wide.region_2.3_spmd.clone.sunk | while | flops 262147 | bytes 1311520 | solution.py:88
  115.3 2.2 fusion.9
  119.3 3.2 %copy.258 = f32[4,64,2,8,64]{4,3,2,1,0:T(8,128)} copy(f32[4,64,2,8,64]{1,4,3,2,0:T(8,128)} %bitcast.375) | data formatting | bytes 2097152 | tf_op jit(solution)/shard_map/transpose | solution.py:78
  124.3 5.5 %multiply_reduce_fusion = (f32[256,2]{1,0:T(8,128)S(1)}, f32[256,2,8,64]{3,2,1,0:T(8,128)}) fusion(f32[256,2,8,64]{3,2,1,0:T(8,128)} %reshape.405, f32[256,2,8,64]{3,2,1,0:T(8,128)} %bitcast.373, f32[4,64,2,8,64]{4,3,2,1,0:T(8,128)} %copy.258), kind=kLoop, calls=%fused_computation.29 | loop fusion | flops 2096640 | bytes 4196352 | tf_op jit(solution)/shard_map/reduce_sum | solution.py:113
  135.9 16.9 %all_to_all.42 = bf16[256,2,256]{2,1,0:T(2,128)(2,1)S(1)} all-to-all(bf16[256,2,256]{2,1,0:T(2,128)(2,1)S(1)} %copy.274), channel_id=1, replica_groups=mesh['gx'=32,'gy'=8] {'gx'}, dimensions={0} | all-to-all | bytes 524288 | tf_op jit(solution)/shard_map/all_to_all | solution.py:136
  155.0 4.1 %all-to-all-start.2 = ((bf16[8,64,256]{2,1,0:T(8,128)(2,1)}), bf16[8,64,256]{2,1,0:T(8,128)(2,1)S(1)}, u32[]{:S(2)}, u32[]{:S(2)}) async-start(bf16[8,64,256]{2,1,0:T(8,128)(2,1)} %fusion.56), calls=%async_computation.2 | async-start | bytes 524288 | tf_op jit(solution)/shard_map/all_to_all | solution.py:141
  159.2 6.6 %all-to-all-done.2 = bf16[8,64,256]{2,1,0:T(8,128)(2,1)S(1)} async-done(((bf16[8,64,256]{2,1,0:T(8,128)(2,1)}), bf16[8,64,256]{2,1,0:T(8,128)(2,1)S(1)}, u32[]{:S(2)}, u32[]{:S(2)}) %all-to-all-start.2) | async-done | bytes 262176 | tf_op jit(solution)/shard_map/all_to_all | solution.py:141
  176.6 6.3 %fusion.67 = f32[64,8,8]{2,1,0:T(8,128)S(1)} fusion(f32[8,64,1,8]{3,0,1,2:T(8,128)S(1)} %copy.292), kind=kOutput, calls=%fused_computation.114 | output fusion | flops 258048 | bytes 32768 | tf_op jit(solution)/shard_map/jit(cumsum)/reduce_window_sum | solution.py:47
  185.7 2.2 rev.42
  195.0 19.0 %while.55 = (s32[]{:T(128)}, f32[1,8,64,64]{3,2,1,0:T(8,128)S(1)}, bf16[8,1,8,64,64]{4,3,2,1,0:T(8,128)(2,1)}, f32[8,1,8]{2,1,0:T(1,128)}, f32[8,1,8,64,64]{4,3,2,1,0:T(8,128)}, /*index=5*/s32[]{:T(128)}, s32[]{:T(128)}) while((s32[]{:T(128)}, f32[1,8,64,64]{3,2,1,0:T(8,128)S(1)}, bf16[8,1,8,64,64]{4,3,2,1,0:T(8,128)(2,1)}, ...), condition=%wide.region_14.15_spmd.clone, body=%wide.region_13.14_spmd.clone.sunk | while | flops 131075 | bytes 656064 | solution.py:88
  214.7 2.2 fusion.12
  217.3 2.6 copy.303
  224.7 6.3 %fusion.69 = f32[64,8,8]{2,1,0:T(8,128)S(1)} fusion(f32[8,64,1,8]{3,0,1,2:T(8,128)S(1)} %copy.279), kind=kOutput, calls=%fused_computation.116 | output fusion | flops 258048 | bytes 32768 | tf_op jit(solution)/shard_map/jit(cumsum)/reduce_window_sum | solution.py:47
  235.3 2.5 convolution_bitcast_fusion.1
  239.1 13.9 %while.54 = (s32[]{:T(128)}, f32[1,8,64,64]{3,2,1,0:T(8,128)S(1)}, bf16[8,1,8,64,64]{4,3,2,1,0:T(8,128)(2,1)}, f32[8,1,8]{2,1,0:T(1,128)S(1)}, f32[8,1,8,64,64]{4,3,2,1,0:T(8,128)}, /*index=5*/s32[]{:T(128)}, s32[]{:T(128)}) while((s32[]{:T(128)}, f32[1,8,64,64]{3,2,1,0:T(8,128)S(1)}, bf16[8,1,8,64,64]{4,3,2,1,0:T(8,128)(2,1)}, ...), condition=%wide.region_11.12_spmd.clone, body=%wide.region_10.11_spmd.clone.sunk | while | flops 131075 | bytes 656064 | solution.py:88
  258.7 2.6 copy.288
  263.4 2.4 add.156
  271.9 8.6 %all_to_all.43 = bf16[8,2,8192]{2,1,0:T(2,128)(2,1)S(1)} all-to-all(bf16[8,2,8192]{2,1,0:T(2,128)(2,1)S(1)} %reshape.442), channel_id=1, replica_groups=mesh['gx'=32,'gy'=8] {'gy'}, dimensions={0} | all-to-all | bytes 524288 | tf_op jit(solution)/shard_map/all_to_all | solution.py:143
  (265 shorter events, 148.0 us)
Async XLA Ops:
  4.4 25.7 %all-to-all-start = ((bf16[8,64,256]{2,0,1:T(8,128)(2,1)}), bf16[8,64,256]{2,0,1:T(8,128)(2,1)S(1)}, u32[]{:S(2)}, u32[]{:S(2)}) async-start(bf16[8,64,256]{2,0,1:T(8,128)(2,1)} %copy.242), calls=%async_computation | async-start | bytes 524288 | tf_op jit(solution)/shard_map/all_to_all | solution.py:134
  30.4 7.8 %copy-start.11 = (bf16[512,256]{1,0:T(8,128)(2,1)}, bf16[512,256]{1,0:T(8,128)(2,1)S(1)}, u32[]{:S(2)}) copy-start(bf16[512,256]{1,0:T(8,128)(2,1)S(1)} %reshape.377) | copy-start | bytes 786436
  33.4 4.8 %copy-start.30 = (bf16[2,256,8]{1,2,0:T(8,128)(2,1)S(1)}, bf16[2,256,8]{1,2,0:T(8,128)(2,1)}, u32[]{:S(2)}) copy-start(bf16[2,256,8]{1,2,0:T(8,128)(2,1)} %param.21) | copy-start | bytes 24580
  49.3 1.2 copy-start.5
  50.5 0.9 copy-start.10
  53.1 5.1 %copy-start.22 = (bf16[2,256,128]{2,1,0:T(8,128)(2,1)S(1)}, bf16[2,256,128]{2,1,0:T(8,128)(2,1)}, u32[]{:S(2)}) copy-start(bf16[2,256,128]{2,1,0:T(8,128)(2,1)} %param.20) | copy-start | bytes 393220
  62.7 4.3 %copy-start.14 = (bf16[64,4,2,64]{3,0,2,1:T(8,128)(2,1)}, bf16[64,4,2,64]{3,0,2,1:T(8,128)(2,1)S(1)}, u32[]{:S(2)}) copy-start(bf16[64,4,2,64]{3,0,2,1:T(8,128)(2,1)S(1)} %copy.263) | copy-start | bytes 196612
  75.8 8.5 %copy-start.12 = (bf16[512,64]{1,0:T(8,128)(2,1)}, bf16[512,64]{1,0:T(8,128)(2,1)S(1)}, u32[]{:S(2)}) copy-start(bf16[512,64]{1,0:T(8,128)(2,1)S(1)} %copy.245) | copy-start | bytes 196612
  82.1 2.3 copy-start.2
  82.1 2.3 copy-start.20
  98.9 2.7 copy-start.21
  105.9 7.8 %copy-start.13 = (bf16[512,64]{1,0:T(8,128)(2,1)S(1)}, bf16[512,64]{1,0:T(8,128)(2,1)}, u32[]{:S(2)}) copy-start(bf16[512,64]{1,0:T(8,128)(2,1)} %copy-done.12) | copy-start | bytes 196612
  105.9 9.4 %copy-start.25 = (pred[64,64]{1,0:T(8,128)(4,1)S(1)}, pred[64,64]{1,0:T(8,128)(4,1)}, u32[]{:S(2)}) copy-start(pred[64,64]{1,0:T(8,128)(4,1)} %iota_compare_fusion) | copy-start | bytes 12292
  115.3 2.2 copy-start.3
  119.3 3.2 %copy-start = (f32[512,512]{1,0:T(8,128)S(1)}, f32[512,512]{1,0:T(8,128)}, u32[]{:S(2)}) copy-start(f32[512,512]{1,0:T(8,128)} %get-tuple-element.286) | copy-start | bytes 3145732
  134.3 19.0 %copy-start.9 = (bf16[8,64,256]{2,1,0:T(8,128)(2,1)S(1)}, bf16[8,64,256]{2,1,0:T(8,128)(2,1)}, u32[]{:S(2)}) copy-start(bf16[8,64,256]{2,1,0:T(8,128)(2,1)} %param.17) | copy-start | bytes 786436
  135.6 18.6 %copy-start.27 = (f32[1,256]{1,0:T(1,128)S(1)}, f32[1,256]{1,0:T(1,128)}, u32[]{:S(2)}) copy-start(f32[1,256]{1,0:T(1,128)} %get-tuple-element.309) | copy-start | bytes 3076
  153.5 13.8 %copy-start.23 = (bf16[2,256,128]{2,1,0:T(8,128)(2,1)S(1)}, bf16[2,256,128]{2,1,0:T(8,128)(2,1)}, u32[]{:S(2)}) copy-start(bf16[2,256,128]{2,1,0:T(8,128)(2,1)} %param.20) | copy-start | bytes 393220
  154.2 13.3 %copy-start.28 = (f32[8]{0:T(128)S(1)}, f32[8]{0:T(128)}, u32[]{:S(2)}) copy-start(f32[8]{0:T(128)} %get-tuple-element.313) | copy-start | bytes 100
  154.2 13.3 %copy-start.29 = (f32[8]{0:T(128)S(1)}, f32[8]{0:T(128)}, u32[]{:S(2)}) copy-start(f32[8]{0:T(128)} %get-tuple-element.311) | copy-start | bytes 100
  154.2 13.3 %copy-start.31 = (bf16[2,256,8]{1,2,0:T(8,128)(2,1)S(1)}, bf16[2,256,8]{1,2,0:T(8,128)(2,1)}, u32[]{:S(2)}) copy-start(bf16[2,256,8]{1,2,0:T(8,128)(2,1)} %param.21) | copy-start | bytes 24580
  155.0 10.7 %all-to-all-start.2 = ((bf16[8,64,256]{2,1,0:T(8,128)(2,1)}), bf16[8,64,256]{2,1,0:T(8,128)(2,1)S(1)}, u32[]{:S(2)}, u32[]{:S(2)}) async-start(bf16[8,64,256]{2,1,0:T(8,128)(2,1)} %fusion.56), calls=%async_computation.2 | async-start | bytes 524288 | tf_op jit(solution)/shard_map/all_to_all | solution.py:141
  195.0 19.0 %copy-start.16 = (f32[64,8,8]{2,1,0:T(8,128)S(1)}, f32[64,8,8]{2,1,0:T(8,128)}, u32[]{:S(2)}) copy-start(f32[64,8,8]{2,1,0:T(8,128)} %get-tuple-element.287) | copy-start | bytes 49156
  195.0 19.2 %copy-start.19 = (bf16[512,64]{0,1:T(8,128)(2,1)S(1)}, bf16[512,64]{0,1:T(8,128)(2,1)}, u32[]{:S(2)}) copy-start(bf16[512,64]{0,1:T(8,128)(2,1)} %reverse.12) | copy-start | bytes 196612
  195.0 19.4 %copy-start.18 = (f32[8,64,1,8]{1,0,3,2:T(8,128)S(1)}, f32[8,64,1,8]{1,0,3,2:T(8,128)}, u32[]{:S(2)}) copy-start(f32[8,64,1,8]{1,0,3,2:T(8,128)} %copy-done.17) | copy-start | bytes 49156
  195.0 19.7 %copy-start.26 = (pred[64,64]{1,0:T(8,128)(4,1)S(1)}, pred[64,64]{1,0:T(8,128)(4,1)}, u32[]{:S(2)}) copy-start(pred[64,64]{1,0:T(8,128)(4,1)} %iota_compare_fusion) | copy-start | bytes 12292
  214.6 2.2 copy-start.4
  231.0 1.8 copy-start.6
  257.0 1.2 copy-start.1
  257.0 1.2 copy-start.15
  267.4 1.0 copy-start.24
  268.8 12.1 %copy-start.8 = (bf16[8,64,256]{2,1,0:T(8,128)(2,1)S(1)}, bf16[8,64,256]{2,1,0:T(8,128)(2,1)}, u32[]{:S(2)}) copy-start(bf16[8,64,256]{2,1,0:T(8,128)(2,1)} %copy-done.7) | copy-start | bytes 786436
  (2 other events, 1.3 us)
where the time goes:
time: 286 us; the launch traced here: 282 us
  local copies, waits for them, and re-layouts  99.1 us (35%)
  other arithmetic  92.2 us (32%)
  matrix products  31.1 us (11%)
  blocking collectives  25.5 us (9%)
  starting transfers between devices  16.9 us (6%)
  waiting for transfers between devices  15.5 us (5%)
    add x24, other arithmetic, advance(): return (factor[:, :, None, None] * carry + added, carry)  25.9 us
    another operation x4, other arithmetic, block_terms(): running = jnp.cumsum(logdecay, axis=0)  25.3 us
    dynamic_update_slice x24, other arithmetic, chain_blocks(): lax.scan(advance, jnp.zeros_like(end_state[0]), (total, end_state))  17.2 us
    all_to_all x1, blocking collectives, on_device(): lax.all_to_all(change.astype(jnp.bfloat16), 'gx', split_axis=0, concat_ax...  16.9 us
    all_to_all x1, starting transfers between devices, on_device(): lax.all_to_all(normed, 'gx', split_axis=1, concat_axis=0, tiled=True)  12.8 us
    transpose x4, local copies, waits for them, and re-layouts, from_blocks(): jnp.swapaxes(array.reshape((span, count, lines) + array.shape[2:]), 0, 1)  11.3 us
    dot_general x4, matrix products, block_terms(): jnp.einsum('smhp,smn->mhpn', carried, enter, preferred_element_type=jnp.f...  10.3 us
    all_to_all x1, waiting for transfers between devices, on_device(): lax.all_to_all(normed, 'gx', split_axis=1, concat_axis=0, tiled=True)  8.89 us
  transfers between devices with their start and end apart: 2, of which 2 were waited for; matrix products, arithmetic and copies ran while one was open for 1% of the time, Pallas kernels for 0%

commit v1 on v0

v1 whole, which is shorter than its diff:
```python
import functools

import jax
import jax.numpy as jnp
import numpy as np
from jax import lax
from jax.experimental import pallas as pl
from jax.experimental.pallas import tpu as pltpu
from jax.sharding import PartitionSpec as P

EPSILON = 1e-05
CHUNK = 128
HEADS = 8
SIZE = 64
ORDER = 64
INNER = HEADS * SIZE
F32 = jnp.float32
BF16 = jnp.bfloat16


def spread_matrix():
    rows = np.arange(CHUNK)
    cols = np.arange(INNER)
    blocks = []
    for q in range(5):
        blocks.append((rows[:, None] // 16 == q) & (rows[:, None] % 8 == cols[None] // SIZE))
    cols = np.arange(HEADS * 2 * ORDER)
    kind = 5 + (cols % (2 * ORDER)) // ORDER
    blocks.append(
        (rows[:, None] // 16 == kind[None]) & (rows[:, None] % 8 == cols[None] // (2 * ORDER))
    )
    return np.concatenate(blocks, 1).astype(np.float32)


def sum_matrix():
    s = np.arange(CHUNK)
    below = (s[:, None] < s[None, :]) + 0.5 * (s[:, None] == s[None, :])
    return np.concatenate([below, np.ones((CHUNK, CHUNK))], 1).astype(np.float32)


def gather_matrix():
    i = np.arange(2 * CHUNK)
    source = 2 * (i % CHUNK) + i // CHUNK
    return (source[:, None] == np.arange(2 * CHUNK)[None, :]).astype(np.float32)


def dot(a, b, dims=((1,), (0,))):
    return lax.dot_general(a, b, (dims, ((), ())), preferred_element_type=F32)


def silu(v):
    return 0.5 * v * (1.0 + jnp.tanh(0.5 * v))


def column(row):
    n = row.shape[1]
    square = lax.broadcasted_iota(jnp.int32, (n, n), 0) == lax.broadcasted_iota(
        jnp.int32, (n, n), 1
    )
    return jnp.sum(jnp.where(square, jnp.broadcast_to(row, (n, n)), 0.0), 1, keepdims=True)


def layer_kernel(
    layer,
    lines,
    interleaved,
    x_ref,
    norm_ref,
    inner_ref,
    state_ref,
    step_ref,
    bias_ref,
    rate_ref,
    gain_ref,
    out_w_ref,
    spread_ref,
    sums_ref,
    perm_ref,
    o_ref,
):
    tokens = x_ref.shape[0]
    chunks = tokens // CHUNK
    per_line = chunks // lines
    raw = x_ref[...]
    if interleaved:
        perm = perm_ref[...]
        parts = [
            dot(perm, raw[256 * a : 256 * a + 256]) for a in range(tokens // 256)
        ]
        h = jnp.concatenate(
            [p[CHUNK * l : CHUNK * l + CHUNK] for l in range(2) for p in parts], 0
        )
    else:
        h = raw.astype(F32)
    scale = lax.rsqrt(jnp.mean(h * h, axis=1, keepdims=True) + EPSILON)
    normed = (h * scale * norm_ref[layer : layer + 1, :]).astype(BF16)

    inner = inner_ref[0]
    state_w = state_ref[0]
    gates = dot(normed, inner[:, :INNER])
    inputs = silu(dot(normed, inner[:, INNER:])).astype(BF16)
    leave_w = state_w[:, ORDER:]
    leave2 = dot(normed, jnp.concatenate([leave_w, leave_w], 1)).astype(BF16)
    enter_t = dot(state_w, normed, ((0,), (1,)))[:ORDER].astype(BF16)
    raw_steps = dot(step_ref[0], normed, ((0,), (1,))) + column(bias_ref[layer : layer + 1, :])
    steps = jnp.maximum(raw_steps, 0.0) + jnp.log1p(jnp.exp(-jnp.abs(raw_steps)))
    decay = -steps * column(rate_ref[layer : layer + 1, :])
    steps = jnp.concatenate([steps[:, CHUNK * k : CHUNK * k + CHUNK] for k in range(chunks)], 0)
    decay = jnp.concatenate([decay[:, CHUNK * k : CHUNK * k + CHUNK] for k in range(chunks)], 0)
    first = decay.astype(BF16)
    rest = decay - first.astype(F32)
    second = rest.astype(BF16)
    third = (rest - second.astype(F32)).astype(BF16)
    summed = dot(jnp.concatenate([first, second, third], 0), sums_ref[...])
    n = HEADS * chunks
    summed = summed[:n] + summed[n : 2 * n] + summed[2 * n :]
    mid = summed[:, :CHUNK]
    whole = summed[:, CHUNK:]
    lead = jnp.exp(mid)
    tail = jnp.exp(whole - mid)
    entry = steps * jnp.exp(-0.5 * decay)
    growth = jnp.exp(0.5 * decay)
    total = jnp.exp(whole)
    quantities = (entry, entry * tail, entry * lead, growth, total, lead, tail)

    t_pos = lax.broadcasted_iota(jnp.int32, (CHUNK, CHUNK), 0)
    s_pos = lax.broadcasted_iota(jnp.int32, (CHUNK, CHUNK), 1)
    double = jnp.where(t_pos == s_pos, 2.0, 1.0)
    first_half = s_pos < SIZE
    spread_b = spread_ref[...]

    columns = []
    wides = []
    ends_f = []
    ends_b = []
    totals = []
    for k in range(chunks):
        rows = slice(CHUNK * k, CHUNK * k + CHUNK)
        own = slice(HEADS * k, HEADS * k + HEADS)
        pieces = []
        for q in quantities:
            upper = q[own].astype(BF16).astype(F32)
            pieces += [upper, q[own] - upper]
        pieces += [mid[own], jnp.zeros((HEADS, CHUNK), F32)]
        turned = jnp.transpose(jnp.concatenate(pieces, 0))
        columns.append(turned[:, 14 * HEADS : 15 * HEADS])
        wide = dot(turned.astype(BF16), spread_b)
        x = inputs[rows].astype(F32)
        entered = (x * wide[:, :INNER]).astype(BF16)
        carried_f = (x * wide[:, INNER : 2 * INNER]).astype(BF16)
        carried_b = (x * wide[:, 2 * INNER : 3 * INNER]).astype(BF16)
        e_t = enter_t[:, rows]
        ends_f.append(dot(e_t, carried_f))
        ends_b.append(dot(e_t, carried_b))
        totals.append(wide[0:1, 4 * INNER : 5 * INNER])
        wides.append((entered, wide[:, 3 * INNER : 4 * INNER], wide[:, 5 * INNER :]))

    states_f = [None] * chunks
    states_b = [None] * chunks
    zero = jnp.zeros((ORDER, INNER), F32)
    for line in range(lines):
        state = zero
        for k in range(line * per_line, (line + 1) * per_line):
            states_f[k] = state.astype(BF16)
            state = totals[k] * state + ends_f[k]
        state = zero
        for k in reversed(range(line * per_line, (line + 1) * per_line)):
            states_b[k] = state.astype(BF16)
            state = totals[k] * state + ends_b[k]

    results = []
    for k in range(chunks):
        rows = slice(CHUNK * k, CHUNK * k + CHUNK)
        entered, grow, sides = wides[k]
        right = jnp.concatenate([entered, states_f[k], states_b[k]], 0)
        leave = leave2[rows]
        scores = dot(leave[:, :ORDER], enter_t[:, rows]) * double
        leave = leave.astype(F32)
        mixed = []
        for pair in range(HEADS // 2):
            lefts = []
            for head in (2 * pair, 2 * pair + 1):
                gap = columns[k][:, head : head + 1] - mid[HEADS * k + head : HEADS * k + head + 1]
                mixing = (scores * jnp.exp(-jnp.abs(gap))).astype(BF16)
                side = (leave * sides[:, CHUNK * head : CHUNK * head + CHUNK]).astype(BF16)
                lefts.append(jnp.concatenate([mixing, side], 1))
            both = dot(
                jnp.concatenate(lefts, 0), right[:, CHUNK * pair : CHUNK * pair + CHUNK]
            )
            mixed.append(jnp.where(first_half, both[:CHUNK], both[CHUNK:]))
        gated = jnp.concatenate(mixed, 1) * grow * silu(gates[rows])
        scale = lax.rsqrt(jnp.mean(gated * gated, axis=1, keepdims=True) + EPSILON)
        rounded = (gated * scale * gain_ref[layer : layer + 1, :]).astype(BF16)
        results.append((h[rows] + dot(rounded, out_w_ref[0])).astype(BF16))

    if interleaved:
        perm = perm_ref[...]
        half = tokens // 256
        for a in range(half):
            o_ref[256 * a : 256 * a + 256, :] = dot(
                perm, jnp.concatenate([results[a], results[half + a]], 0), ((0,), (0,))
            ).astype(BF16)
    else:
        for k in range(chunks):
            o_ref[CHUNK * k : CHUNK * k + CHUNK, :] = results[k]


def mix(x, layer, lines, interleaved, weights):
    norm_gain, inner_weight, state_weight, step_weight, step_bias, decay_rate, out_gain, out_weight = weights
    whole = lambda a: pl.BlockSpec(a.shape, lambda i: (0,) * a.ndim)
    part = lambda a: pl.BlockSpec((1,) + a.shape[1:], lambda i: (layer, 0, 0))
    consts = (
        jnp.asarray(spread_matrix(), BF16),
        jnp.asarray(sum_matrix(), BF16),
        jnp.asarray(gather_matrix(), BF16),
    )
    return pl.pallas_call(
        functools.partial(layer_kernel, layer, lines, interleaved),
        grid=(1,),
        out_shape=jax.ShapeDtypeStruct(x.shape, BF16),
        in_specs=[
            whole(x),
            whole(norm_gain),
            part(inner_weight),
            part(state_weight),
            part(step_weight),
            whole(step_bias),
            whole(decay_rate),
            whole(out_gain),
            part(out_weight),
        ]
        + [whole(c) for c in consts],
        out_specs=whole(x),
        compiler_params=pltpu.CompilerParams(vmem_limit_bytes=40 * 1024 * 1024),
        name=f"mix_layer_{layer}",
    )(
        x,
        norm_gain,
        inner_weight,
        state_weight,
        step_weight,
        step_bias,
        decay_rate,
        out_gain,
        out_weight,
        *consts,
    )


def on_device(gx, gy, field, *weights):
    nx, ny, width = field.shape
    lines = ny // gx
    sent = jnp.swapaxes(field.reshape(nx, gx, lines, width), 0, 1).reshape(gx, nx * lines, width)
    taken = lax.all_to_all(sent, "gx", 0, 0, tiled=True).reshape(gx * nx * lines, width)
    stream = mix(taken, 0, lines, True, weights)
    taken = lax.all_to_all(
        stream.reshape(gx * nx, lines, width), ("gx", "gy"), 0, 0, tiled=True
    )
    taken = jnp.swapaxes(taken.reshape(gx, gy, lines, width), 0, 1)
    stream = mix(taken.reshape(gy * gx * lines, width), 1, 1, False, weights)
    return lax.all_to_all(stream.reshape(gy, ny, width), "gy", 0, 0, tiled=True)


def solution(mesh):
    in_specs = (P("gx", "gy", None), P(), P(), P(), P(), P(), P(), P(), P())
    return jax.shard_map(
        functools.partial(on_device, mesh.shape["gx"], mesh.shape["gy"]),
        mesh=mesh,
        in_specs=in_specs,
        out_specs=P("gx", "gy", None),
        check_vma=False,
    )
```

time: 286 us -> 72.7 us (0.25); the launches traced: 282 us -> 72.3 us
  other arithmetic: 92.2 us -> 0 us
  local copies, waits for them, and re-layouts: 99.1 us -> 6.94 us
  matrix products: 31.1 us -> 0 us
  Pallas kernels: 0 us -> 8.06 us
  blocking collectives: 25.5 us -> 32.3 us
  starting transfers between devices: 16.9 us -> 12.9 us
  waiting for transfers between devices: 15.5 us -> 12 us
    dot_general x24 -> x0, matrix products: 31.1 us -> none  [the longest x4 10.3 us: block_terms(): jnp.einsum('smhp,smn->mhpn', carried, enter, preferred_element_type=jnp.f...]
    add x25 -> x0, other arithmetic: 28.3 us -> none  [the longest x24 25.9 us: advance(): return (factor[:, :, None, None] * carry + added, carry)]
    another operation x4 -> x0, other arithmetic: 25.3 us -> none  [block_terms(): running = jnp.cumsum(logdecay, axis=0)]
    transpose x21 -> x2, local copies, waits for them, and re-layouts: 25.2 us -> 0.45 us  [the longest x1 0.27 us: on_device(): taken = jnp.swapaxes(taken.reshape(gx, gy, lines, width), 0, 1)]
    dynamic_update_slice x24 -> x0, other arithmetic: 17.2 us -> none  [chain_blocks(): lax.scan(advance, jnp.zeros_like(end_state[0]), (total, end_state))]
    another operation x15 -> x0, local copies, waits for them, and re-layouts: 16.7 us -> none
    reshape x18 -> x4, local copies, waits for them, and re-layouts: 18.5 us -> 2.15 us  [the longest x1 1.14 us: on_device(): field.reshape(nx, gx, lines, width)]
    mul x29 -> x0, local copies, waits for them, and re-layouts: 10.3 us -> none  [the longest x24 5.04 us: advance(): return (factor[:, :, None, None] * carry + added, carry)]
  transfers between devices with their start and end apart: 2 -> 1, of which waited for: 2 -> 1; matrix products, arithmetic and copies ran while one was open for 1% -> 1% of each run, Pallas kernels for 0% -> 0%
where the time goes in v1:
time: 72.7 us; the launch traced here: 72.3 us
  blocking collectives  32.3 us (44%)
  starting transfers between devices  12.9 us (18%)
  waiting for transfers between devices  12 us (17%)
  Pallas kernels  8.06 us (11%)
  local copies, waits for them, and re-layouts  6.94 us (10%)
    all_to_all x1, blocking collectives, on_device(): lax.all_to_all(stream.reshape(gx * nx, lines, width), ('gx', 'gy'), 0, 0,...  21.7 us
    all_to_all x1, starting transfers between devices, on_device(): lax.all_to_all(sent, 'gx', 0, 0, tiled=True).reshape(gx * nx * lines, width)  12.9 us
    all_to_all x1, waiting for transfers between devices, on_device(): lax.all_to_all(sent, 'gx', 0, 0, tiled=True).reshape(gx * nx * lines, width)  12 us
    all_to_all x1, blocking collectives, on_device(): return lax.all_to_all(stream.reshape(gy, ny, width), 'gy', 0, 0, tiled=True)  10.5 us
    pallas_call x2, Pallas kernels, mix(): pl.pallas_call(functools.partial(layer_kernel, layer, lines, interleaved)...  8.06 us
    unnamed x26, local copies, waits for them, and re-layouts  4.31 us
  transfers between devices with their start and end apart: 1, of which 1 were waited for; matrix products, arithmetic and copies ran while one was open for 1% of the time, Pallas kernels for 0%

profile of v1, /device:TPU:1, one launch (start us, length us, event | category | flops | bytes accessed | tf_op | source)
XLA Modules:
  0.0 72.3 jit_solution(12164036081901950447)
XLA Ops:
  0.0 1.1 %reshape.21 = bf16[8,32,2,256]{3,2,1,0:T(2,128)(2,1)S(1)} reshape(bf16[8,64,256]{2,1,0:T(8,128)(2,1)} %param.15) | data formatting | bytes 524288 | tf_op jit(solution)/shard_map/reshape | solution.py:253
  1.1 0.0 copy-start.1
  1.2 0.2 copy.24
  1.3 0.8 %reshape.22 = bf16[32,16,256]{2,1,0:T(8,128)(2,1)} reshape(bf16[32,8,2,256]{3,2,1,0:T(2,128)(2,1)S(1)} %copy.24) | data formatting | bytes 524288 | tf_op jit(solution)/shard_map/reshape | solution.py:253
  2.2 12.9 %all-to-all-start = ((bf16[32,16,256]{2,1,0:T(8,128)(2,1)}), bf16[32,16,256]{2,1,0:T(8,128)(2,1)S(1)}, u32[]{:S(2)}, u32[]{:S(2)}) async-start(bf16[32,16,256]{2,1,0:T(8,128)(2,1)} %reshape.22), calls=%async_computation | async-start | bytes 524288 | tf_op jit(solution)/shard_map/all_to_all | solution.py:254
  15.0 0.0 copy-start.4
  15.1 0.0 copy-start.8
  15.1 0.0 copy-start.9
  15.1 0.0 copy-start.11
  15.1 0.9 %copy.25.step_ref = bf16[2,256,8]{2,1,0:T(8,128)(2,1)S(1)} copy(bf16[2,256,8]{1,2,0:T(8,128)(2,1)} %param.19) | data formatting | bytes 16384 | tf_op args[4]
  16.0 0.0 copy-start.10
  16.0 12.0 %all-to-all-done = bf16[32,16,256]{2,1,0:T(8,128)(2,1)S(1)} async-done(((bf16[32,16,256]{2,1,0:T(8,128)(2,1)}), bf16[32,16,256]{2,1,0:T(8,128)(2,1)S(1)}, u32[]{:S(2)}, u32[]{:S(2)}) %all-to-all-start) | async-done | bytes 262176 | tf_op jit(solution)/shard_map/all_to_all | solution.py:254
  28.0 0.0 copy-done
  28.0 0.0 copy-done.1
  28.0 0.0 copy-done.5
  28.0 0.0 copy-done.4
  28.0 0.0 copy-done.8
  28.0 0.0 copy-start.2
  28.1 1.0 %copy-done.2 = bf16[2,512,256]{2,1,0:T(8,128)(2,1)S(1)} copy-done((bf16[2,512,256]{2,1,0:T(8,128)(2,1)S(1)}, bf16[2,512,256]{2,1,0:T(8,128)(2,1)}, u32[]{:S(2)}) %copy-start.2) | copy-done | bytes 524312
  29.1 0.8 %copy-done.6 = bf16[128,256]{1,0:T(8,128)(2,1)S(1)} copy-done((bf16[128,256]{1,0:T(8,128)(2,1)S(1)}, bf16[128,256]{1,0:T(8,128)(2,1)}, u32[]{:S(2)}) %copy-start.6) | copy-done | bytes 65560
  29.9 4.2 %mix_layer_0.1 = bf16[512,256]{1,0:T(8,128)(2,1)S(1)} custom-call(bf16[512,256]{1,0:T(8,128)(2,1)S(1)} %bitcast.8, f32[2,256]{1,0:T(2,128)S(1)} %copy-done.9, bf16[2,256,1024]{2,1,0:T(8,128)(2,1)S(1)} %copy-done, bf16[2,256,128]{2,1,0:T(8,128)(2,1)S(1)} %copy-done.4, bf16[2,256,8]{2,1,0:T(8,128)(2,1)S(1)} %copy.25.step_ref, f32[2,8]{1,0:T(2,128)S(1)} %copy-done.10, ...), custom_call_target="tpu_custom_call" | custom-call | tf_op jit(solution)/shard_map/mix_layer_0/pallas_call | solution.py:217
  34.1 0.1 reshape.24
  34.2 21.7 %all_to_all.15 = bf16[256,2,256]{2,1,0:T(2,128)(2,1)S(1)} all-to-all(bf16[256,2,256]{2,1,0:T(2,128)(2,1)S(1)} %reshape.24), channel_id=1, replica_groups=mesh['gx'=32,'gy'=8] {'gx','gy'}, dimensions={0} | all-to-all | bytes 524288 | tf_op jit(solution)/shard_map/all_to_all | solution.py:256
  56.0 0.0 copy-start.3
  56.0 0.3 copy.27
  56.3 0.0 copy-start.7
  56.3 0.1 reshape.26.x_ref
  56.4 0.6 copy-done.3
  57.0 0.1 copy-done.7
  57.2 3.9 %mix_layer_1.1 = bf16[512,256]{1,0:T(8,128)(2,1)S(1)} custom-call(bf16[512,256]{1,0:T(8,128)(2,1)S(1)} %reshape.26.x_ref, f32[2,256]{1,0:T(2,128)S(1)} %copy-done.9, bf16[2,256,1024]{2,1,0:T(8,128)(2,1)S(1)} %copy-done, bf16[2,256,128]{2,1,0:T(8,128)(2,1)S(1)} %copy-done.4, bf16[2,256,8]{2,1,0:T(8,128)(2,1)S(1)} %copy.25.step_ref, f32[2,8]{1,0:T(2,128)S(1)} %copy-done.10, ...), custom_call_target="tpu_custom_call" | custom-call | tf_op jit(solution)/shard_map/mix_layer_1/pallas_call | solution.py:217
  61.1 10.5 %all_to_all.16 = bf16[8,64,256]{2,1,0:T(8,128)(2,1)S(1)} all-to-all(bf16[8,64,256]{2,1,0:T(8,128)(2,1)S(1)} %bitcast.9), channel_id=1, replica_groups=mesh['gx'=32,'gy'=8] {'gy'}, dimensions={0} | all-to-all | bytes 524288 | tf_op jit(solution)/shard_map/all_to_all | solution.py:261
  71.6 0.7 copy.32
  (7 shorter events, 0.0 us)
Async XLA Ops:
  0.0 28.0 %copy-start = (bf16[2,256,1024]{2,1,0:T(8,128)(2,1)S(1)}, bf16[2,256,1024]{2,1,0:T(8,128)(2,1)}, u32[]{:S(2)}) copy-start(bf16[2,256,1024]{2,1,0:T(8,128)(2,1)} %inner_ref.3) | copy-start | bytes 3145732
  1.1 26.8 %copy-start.1 = (bf16[128,3584]{1,0:T(8,128)(2,1)S(1)}, bf16[128,3584]{1,0:T(8,128)(2,1)}, u32[]{:S(2)}) copy-start(bf16[128,3584]{1,0:T(8,128)(2,1)} %constant.6.clone.spread_ref) | copy-start | bytes 2752516
  2.2 25.8 %copy-start.5 = (bf16[256,256]{1,0:T(8,128)(2,1)S(1)}, bf16[256,256]{1,0:T(8,128)(2,1)}, u32[]{:S(2)}) copy-start(bf16[256,256]{1,0:T(8,128)(2,1)} %constant.8.clone.perm_ref) | copy-start | bytes 393220
  2.2 25.8 %all-to-all-start = ((bf16[32,16,256]{2,1,0:T(8,128)(2,1)}), bf16[32,16,256]{2,1,0:T(8,128)(2,1)S(1)}, u32[]{:S(2)}, u32[]{:S(2)}) async-start(bf16[32,16,256]{2,1,0:T(8,128)(2,1)} %reshape.22), calls=%async_computation | async-start | bytes 524288 | tf_op jit(solution)/shard_map/all_to_all | solution.py:254
  15.0 12.9 %copy-start.4 = (bf16[2,256,128]{2,1,0:T(8,128)(2,1)S(1)}, bf16[2,256,128]{2,1,0:T(8,128)(2,1)}, u32[]{:S(2)}) copy-start(bf16[2,256,128]{2,1,0:T(8,128)(2,1)} %state_ref.3) | copy-start | bytes 393220
  15.1 12.9 %copy-start.8 = (f32[2,512]{1,0:T(2,128)S(1)}, f32[2,512]{1,0:T(2,128)}, u32[]{:S(2)}) copy-start(f32[2,512]{1,0:T(2,128)} %gain_ref.3) | copy-start | bytes 12292
  15.1 12.9 %copy-start.9 = (f32[2,256]{1,0:T(2,128)S(1)}, f32[2,256]{1,0:T(2,128)}, u32[]{:S(2)}) copy-start(f32[2,256]{1,0:T(2,128)} %norm_ref.3) | copy-start | bytes 6148
  15.1 12.9 %copy-start.11 = (f32[2,8]{1,0:T(2,128)S(1)}, f32[2,8]{1,0:T(2,128)}, u32[]{:S(2)}) copy-start(f32[2,8]{1,0:T(2,128)} %rate_ref.3) | copy-start | bytes 196
  16.0 12.0 %copy-start.10 = (f32[2,8]{1,0:T(2,128)S(1)}, f32[2,8]{1,0:T(2,128)}, u32[]{:S(2)}) copy-start(f32[2,8]{1,0:T(2,128)} %bias_ref.3) | copy-start | bytes 196
  28.0 1.0 %copy-start.2 = (bf16[2,512,256]{2,1,0:T(8,128)(2,1)S(1)}, bf16[2,512,256]{2,1,0:T(8,128)(2,1)}, u32[]{:S(2)}) copy-start(bf16[2,512,256]{2,1,0:T(8,128)(2,1)} %out_w_ref.3) | copy-start | bytes 1572868
  29.1 0.8 %copy-start.6 = (bf16[128,256]{1,0:T(8,128)(2,1)S(1)}, bf16[128,256]{1,0:T(8,128)(2,1)}, u32[]{:S(2)}) copy-start(bf16[128,256]{1,0:T(8,128)(2,1)} %constant.7.clone.sums_ref) | copy-start | bytes 196612
  56.0 1.0 %copy-start.3 = (bf16[2,512,256]{2,1,0:T(8,128)(2,1)S(1)}, bf16[2,512,256]{2,1,0:T(8,128)(2,1)}, u32[]{:S(2)}) copy-start(bf16[2,512,256]{2,1,0:T(8,128)(2,1)} %out_w_ref.3) | copy-start | bytes 1572868
  56.3 0.9 %copy-start.7 = (bf16[128,256]{1,0:T(8,128)(2,1)S(1)}, bf16[128,256]{1,0:T(8,128)(2,1)}, u32[]{:S(2)}) copy-start(bf16[128,256]{1,0:T(8,128)(2,1)} %constant.7.clone.sums_ref) | copy-start | bytes 196612

commit v2 on v1

--- a/solution.py
+++ b/solution.py
@@ -22,26 +22,40 @@
     rows = np.arange(CHUNK)
     cols = np.arange(INNER)
     blocks = []
-    for q in range(5):
+    for q in range(4):
         blocks.append((rows[:, None] // 16 == q) & (rows[:, None] % 8 == cols[None] // SIZE))
     cols = np.arange(HEADS * 2 * ORDER)
-    kind = 5 + (cols % (2 * ORDER)) // ORDER
+    kind = 4 + (cols % (2 * ORDER)) // ORDER
     blocks.append(
         (rows[:, None] // 16 == kind[None]) & (rows[:, None] % 8 == cols[None] // (2 * ORDER))
     )
     return np.concatenate(blocks, 1).astype(np.float32)
 
 
+def positions(rows, cols):
+    return (
+        lax.broadcasted_iota(jnp.int32, (rows, cols), 0),
+        lax.broadcasted_iota(jnp.int32, (rows, cols), 1),
+    )
+
+
 def sum_matrix():
-    s = np.arange(CHUNK)
-    below = (s[:, None] < s[None, :]) + 0.5 * (s[:, None] == s[None, :])
-    return np.concatenate([below, np.ones((CHUNK, CHUNK))], 1).astype(np.float32)
-
-
-def gather_matrix():
-    i = np.arange(2 * CHUNK)
-    source = 2 * (i % CHUNK) + i // CHUNK
-    return (source[:, None] == np.arange(2 * CHUNK)[None, :]).astype(np.float32)
+    s, t = positions(CHUNK, CHUNK)
+    below = jnp.where(s < t, 1.0, jnp.where(s == t, 0.5, 0.0))
+    return jnp.concatenate([below, jnp.ones((CHUNK, CHUNK), F32)], 1).astype(BF16)
+
+
+def gather_matrix(source):
+    i, j = positions(2 * CHUNK, 2 * CHUNK)
+    return jnp.where(source(i // CHUNK, i % CHUNK) == j, 1.0, 0.0).astype(BF16)
+
+
+def arriving(line, x):
+    return 16 * (x // 8) + 8 * line + x % 8
+
+
+def leaving(line, x):
+    return 2 * x + line
 
 
 def dot(a, b, dims=((1,), (0,))):
@@ -72,18 +86,20 @@
     bias_ref,
     rate_ref,
     gain_ref,
+    out_w_hbm,
+    spread_ref,
+    o_ref,
     out_w_ref,
-    spread_ref,
-    sums_ref,
-    perm_ref,
-    o_ref,
+    out_w_sem,
 ):
+    out_copy = pltpu.make_async_copy(out_w_hbm.at[layer], out_w_ref, out_w_sem)
+    out_copy.start()
     tokens = x_ref.shape[0]
     chunks = tokens // CHUNK
     per_line = chunks // lines
     raw = x_ref[...]
     if interleaved:
-        perm = perm_ref[...]
+        perm = gather_matrix(arriving)
         parts = [
             dot(perm, raw[256 * a : 256 * a + 256]) for a in range(tokens // 256)
         ]
@@ -111,7 +127,7 @@
     rest = decay - first.astype(F32)
     second = rest.astype(BF16)
     third = (rest - second.astype(F32)).astype(BF16)
-    summed = dot(jnp.concatenate([first, second, third], 0), sums_ref[...])
+    summed = dot(jnp.concatenate([first, second, third], 0), sum_matrix())
     n = HEADS * chunks
     summed = summed[:n] + summed[n : 2 * n] + summed[2 * n :]
     mid = summed[:, :CHUNK]
@@ -121,10 +137,9 @@
     entry = steps * jnp.exp(-0.5 * decay)
     growth = jnp.exp(0.5 * decay)
     total = jnp.exp(whole)
-    quantities = (entry, entry * tail, entry * lead, growth, total, lead, tail)
-
-    t_pos = lax.broadcasted_iota(jnp.int32, (CHUNK, CHUNK), 0)
-    s_pos = lax.broadcasted_iota(jnp.int32, (CHUNK, CHUNK), 1)
+    quantities = (entry, entry * tail, entry * lead, growth, lead, tail)
+
+    t_pos, s_pos = positions(CHUNK, CHUNK)
     double = jnp.where(t_pos == s_pos, 2.0, 1.0)
     first_half = s_pos < SIZE
     spread_b = spread_ref[...]
@@ -141,9 +156,9 @@
         for q in quantities:
             upper = q[own].astype(BF16).astype(F32)
             pieces += [upper, q[own] - upper]
-        pieces += [mid[own], jnp.zeros((HEADS, CHUNK), F32)]
+        pieces += [mid[own], jnp.zeros((3 * HEADS, CHUNK), F32)]
         turned = jnp.transpose(jnp.concatenate(pieces, 0))
-        columns.append(turned[:, 14 * HEADS : 15 * HEADS])
+        columns.append(turned[:, 12 * HEADS : 13 * HEADS])
         wide = dot(turned.astype(BF16), spread_b)
         x = inputs[rows].astype(F32)
         entered = (x * wide[:, :INNER]).astype(BF16)
@@ -152,8 +167,20 @@
         e_t = enter_t[:, rows]
         ends_f.append(dot(e_t, carried_f))
         ends_b.append(dot(e_t, carried_b))
-        totals.append(wide[0:1, 4 * INNER : 5 * INNER])
-        wides.append((entered, wide[:, 3 * INNER : 4 * INNER], wide[:, 5 * INNER :]))
+        totals.append(
+            jnp.concatenate(
+                [
+                    jnp.where(
+                        first_half[:1],
+                        total[HEADS * k + h : HEADS * k + h + 1],
+                        total[HEADS * k + h + 1 : HEADS * k + h + 2],
+                    )
+                    for h in range(0, HEADS, 2)
+                ],
+                1,
+            )
+        )
+        wides.append((entered, wide[:, 3 * INNER : 4 * INNER], wide[:, 4 * INNER :]))
 
     states_f = [None] * chunks
     states_b = [None] * chunks
@@ -168,6 +195,7 @@
             states_b[k] = state.astype(BF16)
             state = totals[k] * state + ends_b[k]
 
+    out_copy.wait()
     results = []
     for k in range(chunks):
         rows = slice(CHUNK * k, CHUNK * k + CHUNK)
@@ -191,10 +219,10 @@
         gated = jnp.concatenate(mixed, 1) * grow * silu(gates[rows])
         scale = lax.rsqrt(jnp.mean(gated * gated, axis=1, keepdims=True) + EPSILON)
         rounded = (gated * scale * gain_ref[layer : layer + 1, :]).astype(BF16)
-        results.append((h[rows] + dot(rounded, out_w_ref[0])).astype(BF16))
+        results.append((h[rows] + dot(rounded, out_w_ref[...])).astype(BF16))
 
     if interleaved:
-        perm = perm_ref[...]
+        perm = gather_matrix(leaving)
         half = tokens // 256
         for a in range(half):
             o_ref[256 * a : 256 * a + 256, :] = dot(
@@ -209,11 +237,7 @@
     norm_gain, inner_weight, state_weight, step_weight, step_bias, decay_rate, out_gain, out_weight = weights
     whole = lambda a: pl.BlockSpec(a.shape, lambda i: (0,) * a.ndim)
     part = lambda a: pl.BlockSpec((1,) + a.shape[1:], lambda i: (layer, 0, 0))
-    consts = (
-        jnp.asarray(spread_matrix(), BF16),
-        jnp.asarray(sum_matrix(), BF16),
-        jnp.asarray(gather_matrix(), BF16),
-    )
+    spread = jnp.asarray(spread_matrix(), BF16)
     return pl.pallas_call(
         functools.partial(layer_kernel, layer, lines, interleaved),
         grid=(1,),
@@ -227,10 +251,11 @@
             whole(step_bias),
             whole(decay_rate),
             whole(out_gain),
-            part(out_weight),
-        ]
-        + [whole(c) for c in consts],
+            pl.BlockSpec(memory_space=pl.ANY),
+            whole(spread),
+        ],
         out_specs=whole(x),
+        scratch_shapes=[pltpu.VMEM(out_weight.shape[1:], BF16), pltpu.SemaphoreType.DMA],
         compiler_params=pltpu.CompilerParams(vmem_limit_bytes=40 * 1024 * 1024),
         name=f"mix_layer_{layer}",
     )(
@@ -243,14 +268,14 @@
         decay_rate,
         out_gain,
         out_weight,
-        *consts,
+        spread,
     )
 
 
 def on_device(gx, gy, field, *weights):
     nx, ny, width = field.shape
     lines = ny // gx
-    sent = jnp.swapaxes(field.reshape(nx, gx, lines, width), 0, 1).reshape(gx, nx * lines, width)
+    sent = jnp.swapaxes(field, 0, 1).reshape(gx, lines * nx, width)
     taken = lax.all_to_all(sent, "gx", 0, 0, tiled=True).reshape(gx * nx * lines, width)
     stream = mix(taken, 0, lines, True, weights)
     taken = lax.all_to_all(

time: 72.7 us -> 72.8 us (level)
    unnamed x26 -> x23, local copies, waits for them, and re-layouts: 4.31 us -> 6.57 us
    reshape x2 -> x0, local copies, waits for them, and re-layouts: 1.94 us -> none  [the longest x1 1.14 us: on_device(): field.reshape(nx, gx, lines, width)]
where the time goes in v2:
time: 72.8 us; the launch traced here: 72.4 us
  blocking collectives  32.3 us (44%)
  starting transfers between devices  12.8 us (18%)
  waiting for transfers between devices  12 us (16%)
  Pallas kernels  8.22 us (11%)
  local copies, waits for them, and re-layouts  7.08 us (10%)
    all_to_all x1, blocking collectives, on_device(): lax.all_to_all(stream.reshape(gx * nx, lines, width), ('gx', 'gy'), 0, 0,...  21.7 us
    all_to_all x1, starting transfers between devices, on_device(): lax.all_to_all(sent, 'gx', 0, 0, tiled=True).reshape(gx * nx * lines, width)  12.8 us
    all_to_all x1, waiting for transfers between devices, on_device(): lax.all_to_all(sent, 'gx', 0, 0, tiled=True).reshape(gx * nx * lines, width)  12 us
    all_to_all x1, blocking collectives, on_device(): return lax.all_to_all(stream.reshape(gy, ny, width), 'gy', 0, 0, tiled=True)  10.5 us
    pallas_call x2, Pallas kernels, mix(): pl.pallas_call(functools.partial(layer_kernel, layer, lines, interleaved)...  8.22 us
    unnamed x23, local copies, waits for them, and re-layouts  6.57 us
  transfers between devices with their start and end apart: 1, of which 1 were waited for; matrix products, arithmetic and copies ran while one was open for 1% of the time, Pallas kernels for 0%

profile of v2, /device:TPU:1, one launch (start us, length us, event | category | flops | bytes accessed | tf_op | source)
XLA Modules:
  0.0 72.4 jit_solution(10309566908589770602)
XLA Ops:
  0.0 0.0 copy-start
  0.0 1.9 %copy.19 = bf16[8,64,256]{2,0,1:T(8,128)(2,1)} copy(bf16[8,64,256]{2,1,0:T(8,128)(2,1)} %param.11) | data formatting | bytes 524288 | tf_op args[0]
  1.9 12.8 %all-to-all-start = ((bf16[32,16,256]{2,1,0:T(8,128)(2,1)}), bf16[32,16,256]{2,1,0:T(8,128)(2,1)S(1)}, u32[]{:S(2)}, u32[]{:S(2)}) async-start(bf16[32,16,256]{2,1,0:T(8,128)(2,1)} %bitcast.1), calls=%async_computation | async-start | bytes 524288 | tf_op jit(solution)/shard_map/all_to_all | solution.py:279
  14.7 0.0 copy-start.5
  14.7 0.0 copy-start.6
  14.7 0.0 copy-start.7
  14.7 0.0 copy-start.9
  14.7 0.9 %copy.20.step_ref = bf16[2,256,8]{2,1,0:T(8,128)(2,1)S(1)} copy(bf16[2,256,8]{1,2,0:T(8,128)(2,1)} %param.15) | data formatting | bytes 16384 | tf_op args[4]
  15.6 0.0 copy-start.8
  15.6 12.0 %all-to-all-done = bf16[32,16,256]{2,1,0:T(8,128)(2,1)S(1)} async-done(((bf16[32,16,256]{2,1,0:T(8,128)(2,1)}), bf16[32,16,256]{2,1,0:T(8,128)(2,1)S(1)}, u32[]{:S(2)}, u32[]{:S(2)}) %all-to-all-start) | async-done | bytes 262176 | tf_op jit(solution)/shard_map/all_to_all | solution.py:279
  27.6 0.0 copy-done
  27.6 0.0 copy-done.5
  27.6 0.0 copy-done.6
  27.6 0.0 copy-done.7
  27.6 0.0 copy-done.9
  27.6 0.0 copy-done.8
  27.6 0.0 copy-start.1
  27.6 1.1 %copy-done.1 = bf16[128,3072]{1,0:T(8,128)(2,1)S(1)} copy-done((bf16[128,3072]{1,0:T(8,128)(2,1)S(1)}, bf16[128,3072]{1,0:T(8,128)(2,1)}, u32[]{:S(2)}) %copy-start.1) | copy-done | bytes 786456
  28.8 0.0 copy-start.3
  28.8 1.0 %copy-done.3 = bf16[2,512,256]{2,1,0:T(8,128)(2,1)S(1)} copy-done((bf16[2,512,256]{2,1,0:T(8,128)(2,1)S(1)}, bf16[2,512,256]{2,1,0:T(8,128)(2,1)}, u32[]{:S(2)}) %copy-start.3) | copy-done | bytes 524312
  29.8 4.2 %mix_layer_0.1 = bf16[512,256]{1,0:T(8,128)(2,1)S(1)} custom-call(bf16[512,256]{1,0:T(8,128)(2,1)S(1)} %bitcast.10, f32[2,256]{1,0:T(2,128)S(1)} %copy-done.7, bf16[2,256,1024]{2,1,0:T(8,128)(2,1)S(1)} %copy-done, bf16[2,256,128]{2,1,0:T(8,128)(2,1)S(1)} %copy-done.5, bf16[2,256,8]{2,1,0:T(8,128)(2,1)S(1)} %copy.20.step_ref, f32[2,8]{1,0:T(2,128)S(1)} %copy-done.8, ...), custom_call_target="tpu_custom_call" | custom-call | tf_op jit(solution)/shard_map/mix_layer_0/pallas_call | solution.py:241
  34.1 0.1 reshape.20
  34.2 21.7 %all_to_all.15 = bf16[256,2,256]{2,1,0:T(2,128)(2,1)S(1)} all-to-all(bf16[256,2,256]{2,1,0:T(2,128)(2,1)S(1)} %reshape.20), channel_id=1, replica_groups=mesh['gx'=32,'gy'=8] {'gx','gy'}, dimensions={0} | all-to-all | bytes 524288 | tf_op jit(solution)/shard_map/all_to_all | solution.py:281
  55.9 0.0 copy-start.2
  55.9 0.0 copy-start.4
  56.0 0.3 copy.22
  56.2 0.1 reshape.22.x_ref
  56.3 0.7 copy-done.2
  57.0 0.1 copy-done.4
  57.2 4.0 %mix_layer_1.1 = bf16[512,256]{1,0:T(8,128)(2,1)S(1)} custom-call(bf16[512,256]{1,0:T(8,128)(2,1)S(1)} %reshape.22.x_ref, f32[2,256]{1,0:T(2,128)S(1)} %copy-done.7, bf16[2,256,1024]{2,1,0:T(8,128)(2,1)S(1)} %copy-done, bf16[2,256,128]{2,1,0:T(8,128)(2,1)S(1)} %copy-done.5, bf16[2,256,8]{2,1,0:T(8,128)(2,1)S(1)} %copy.20.step_ref, f32[2,8]{1,0:T(2,128)S(1)} %copy-done.8, ...), custom_call_target="tpu_custom_call" | custom-call | tf_op jit(solution)/shard_map/mix_layer_1/pallas_call | solution.py:241
  61.2 10.5 %all_to_all.16 = bf16[8,64,256]{2,1,0:T(8,128)(2,1)S(1)} all-to-all(bf16[8,64,256]{2,1,0:T(8,128)(2,1)S(1)} %bitcast.11), channel_id=1, replica_groups=mesh['gx'=32,'gy'=8] {'gy'}, dimensions={0} | all-to-all | bytes 524288 | tf_op jit(solution)/shard_map/all_to_all | solution.py:286
  71.7 0.7 copy.27
  (1 shorter events, 0.0 us)
Async XLA Ops:
  0.0 27.6 %copy-start = (bf16[2,256,1024]{2,1,0:T(8,128)(2,1)S(1)}, bf16[2,256,1024]{2,1,0:T(8,128)(2,1)}, u32[]{:S(2)}) copy-start(bf16[2,256,1024]{2,1,0:T(8,128)(2,1)} %inner_ref.3) | copy-start | bytes 3145732
  1.9 25.7 %all-to-all-start = ((bf16[32,16,256]{2,1,0:T(8,128)(2,1)}), bf16[32,16,256]{2,1,0:T(8,128)(2,1)S(1)}, u32[]{:S(2)}, u32[]{:S(2)}) async-start(bf16[32,16,256]{2,1,0:T(8,128)(2,1)} %bitcast.1), calls=%async_computation | async-start | bytes 524288 | tf_op jit(solution)/shard_map/all_to_all | solution.py:279
  14.7 12.9 %copy-start.5 = (bf16[2,256,128]{2,1,0:T(8,128)(2,1)S(1)}, bf16[2,256,128]{2,1,0:T(8,128)(2,1)}, u32[]{:S(2)}) copy-start(bf16[2,256,128]{2,1,0:T(8,128)(2,1)} %state_ref.3) | copy-start | bytes 393220
  14.7 12.9 %copy-start.6 = (f32[2,512]{1,0:T(2,128)S(1)}, f32[2,512]{1,0:T(2,128)}, u32[]{:S(2)}) copy-start(f32[2,512]{1,0:T(2,128)} %gain_ref.3) | copy-start | bytes 12292
  14.7 12.9 %copy-start.7 = (f32[2,256]{1,0:T(2,128)S(1)}, f32[2,256]{1,0:T(2,128)}, u32[]{:S(2)}) copy-start(f32[2,256]{1,0:T(2,128)} %norm_ref.3) | copy-start | bytes 6148
  14.7 12.9 %copy-start.9 = (f32[2,8]{1,0:T(2,128)S(1)}, f32[2,8]{1,0:T(2,128)}, u32[]{:S(2)}) copy-start(f32[2,8]{1,0:T(2,128)} %rate_ref.3) | copy-start | bytes 196
  15.6 12.0 %copy-start.8 = (f32[2,8]{1,0:T(2,128)S(1)}, f32[2,8]{1,0:T(2,128)}, u32[]{:S(2)}) copy-start(f32[2,8]{1,0:T(2,128)} %bias_ref.3) | copy-start | bytes 196
  27.6 1.1 %copy-start.1 = (bf16[128,3072]{1,0:T(8,128)(2,1)S(1)}, bf16[128,3072]{1,0:T(8,128)(2,1)}, u32[]{:S(2)}) copy-start(bf16[128,3072]{1,0:T(8,128)(2,1)} %constant.2.clone.spread_ref) | copy-start | bytes 2359300
  28.8 1.0 %copy-start.3 = (bf16[2,512,256]{2,1,0:T(8,128)(2,1)S(1)}, bf16[2,512,256]{2,1,0:T(8,128)(2,1)}, u32[]{:S(2)}) copy-start(bf16[2,512,256]{2,1,0:T(8,128)(2,1)} %out_w_hbm.3) | copy-start | bytes 1572868
  55.9 1.1 %copy-start.2 = (bf16[128,3072]{1,0:T(8,128)(2,1)S(1)}, bf16[128,3072]{1,0:T(8,128)(2,1)}, u32[]{:S(2)}) copy-start(bf16[128,3072]{1,0:T(8,128)(2,1)} %constant.2.clone.spread_ref) | copy-start | bytes 2359300
  55.9 1.2 %copy-start.4 = (bf16[2,512,256]{2,1,0:T(8,128)(2,1)S(1)}, bf16[2,512,256]{2,1,0:T(8,128)(2,1)}, u32[]{:S(2)}) copy-start(bf16[2,512,256]{2,1,0:T(8,128)(2,1)} %out_w_hbm.3) | copy-start | bytes 1572868

commit v3 on v2

v3 whole, which is shorter than its diff:
```python
import functools

import jax
import jax.numpy as jnp
from jax import lax
from jax.experimental import pallas as pl
from jax.experimental.pallas import tpu as pltpu
from jax.sharding import PartitionSpec as P

EPSILON = 1e-05
LOG2E = 1.4426950408889634
CHUNK = 128
HEADS = 8
SIZE = 64
ORDER = 64
INNER = HEADS * SIZE
F32 = jnp.float32
BF16 = jnp.bfloat16


def positions(rows, cols):
    return (
        lax.broadcasted_iota(jnp.int32, (rows, cols), 0),
        lax.broadcasted_iota(jnp.int32, (rows, cols), 1),
    )


def sum_matrix():
    s, t = positions(CHUNK, CHUNK)
    below = jnp.where(s < t, 1.0, jnp.where(s == t, 0.5, 0.0))
    return jnp.concatenate([below, jnp.ones((CHUNK, CHUNK), F32)], 1).astype(BF16)


def gather_matrix(source):
    i, j = positions(2 * CHUNK, 2 * CHUNK)
    return jnp.where(source(i // CHUNK, i % CHUNK) == j, 1.0, 0.0).astype(BF16)


def arriving(line, x):
    return 16 * (x // 8) + 8 * line + x % 8


def leaving(line, x):
    return 2 * x + line


def dot(a, b, dims=((1,), (0,))):
    return lax.dot_general(a, b, (dims, ((), ())), preferred_element_type=F32)


def silu(v):
    return 0.5 * v * (1.0 + jnp.tanh(0.5 * v))


def column(row):
    n = row.shape[1]
    square = lax.broadcasted_iota(jnp.int32, (n, n), 0) == lax.broadcasted_iota(
        jnp.int32, (n, n), 1
    )
    return jnp.sum(jnp.where(square, jnp.broadcast_to(row, (n, n)), 0.0), 1, keepdims=True)


def layer_kernel(
    layer,
    lines,
    interleaved,
    x_ref,
    norm_ref,
    inner_ref,
    state_ref,
    step_ref,
    bias_ref,
    rate_ref,
    gain_ref,
    out_w_hbm,
    o_ref,
    out_w_ref,
    out_w_sem,
):
    out_copy = pltpu.make_async_copy(out_w_hbm.at[layer], out_w_ref, out_w_sem)
    out_copy.start()
    tokens = x_ref.shape[0]
    chunks = tokens // CHUNK
    per_line = chunks // lines
    raw = x_ref[...]
    if interleaved:
        perm = gather_matrix(arriving)
        parts = [
            dot(perm, raw[256 * a : 256 * a + 256]) for a in range(tokens // 256)
        ]
        h = jnp.concatenate(
            [p[CHUNK * l : CHUNK * l + CHUNK] for l in range(2) for p in parts], 0
        )
    else:
        h = raw.astype(F32)
    scale = lax.rsqrt(jnp.mean(h * h, axis=1, keepdims=True) + EPSILON)
    normed = (h * scale * norm_ref[layer : layer + 1, :]).astype(BF16)

    weights = jnp.concatenate(
        [
            jnp.transpose(jnp.concatenate([inner_ref[0], state_ref[0]], 1)),
            step_ref[0],
            jnp.zeros_like(step_ref[0]),
        ],
        0,
    )
    projected = dot(weights, normed, ((1,), (1,)))
    gates = projected[:INNER]
    inputs = silu(projected[INNER : 2 * INNER]).astype(BF16)
    base = 2 * INNER
    enter = projected[base : base + ORDER].astype(BF16)
    leave = projected[base + ORDER : base + 2 * ORDER].astype(BF16)
    raw_steps = projected[base + 2 * ORDER : base + 2 * ORDER + HEADS]
    raw_steps = raw_steps + column(bias_ref[layer : layer + 1, :])
    steps = jnp.maximum(raw_steps, 0.0) + jnp.log1p(jnp.exp(-jnp.abs(raw_steps)))
    decay = -steps * column(rate_ref[layer : layer + 1, :])
    steps = jnp.concatenate([steps[:, CHUNK * k : CHUNK * k + CHUNK] for k in range(chunks)], 0)
    decay = jnp.concatenate([decay[:, CHUNK * k : CHUNK * k + CHUNK] for k in range(chunks)], 0)
    first = decay.astype(BF16)
    rest = decay - first.astype(F32)
    second = rest.astype(BF16)
    third = (rest - second.astype(F32)).astype(BF16)
    summed = dot(jnp.concatenate([first, second, third], 0), sum_matrix())
    n = HEADS * chunks
    summed = summed[:n] + summed[n : 2 * n] + summed[2 * n :]
    mid = summed[:, :CHUNK]
    whole = summed[:, CHUNK:]
    lead = jnp.exp(mid)
    tail = jnp.exp(whole - mid)
    entry = steps * jnp.exp(-0.5 * decay)
    entry_tail = entry * tail
    entry_lead = entry * lead
    growth = jnp.exp(0.5 * decay)
    total = jnp.exp(whole)
    mid2 = mid * LOG2E
    mid2_columns = jnp.transpose(
        jnp.concatenate([mid2, jnp.zeros((CHUNK - n, CHUNK), F32)], 0)
    )

    s_pos, t_pos = positions(CHUNK, CHUNK)
    double = jnp.where(s_pos == t_pos, 2.0, 1.0)
    ahead_half = t_pos < ORDER

    def span(k):
        return slice(CHUNK * k, CHUNK * k + CHUNK)

    def by_head(values, rows, k):
        return jnp.concatenate(
            [
                values[SIZE * h : SIZE * h + SIZE] * rows[HEADS * k + h : HEADS * k + h + 1]
                for h in range(HEADS)
            ],
            0,
        )

    entered = []
    carried_ahead = []
    carried_behind = []
    for k in range(chunks):
        x = inputs[:, span(k)].astype(F32)
        entered.append(by_head(x, entry, k).astype(BF16))
        carried_ahead.append(by_head(x, entry_tail, k).astype(BF16))
        carried_behind.append(by_head(x, entry_lead, k).astype(BF16))

    empty = jnp.zeros((ORDER, CHUNK), BF16)
    joined = [None] * chunks
    for line in range(lines):
        start = line * per_line
        states = [jnp.zeros((INNER, CHUNK), F32)]
        for j in range(per_line - 1):
            f, b = start + j, start + per_line - 1 - j
            sides = jnp.concatenate(
                [
                    jnp.concatenate([enter[:, span(f)], empty], 1),
                    jnp.concatenate([empty, enter[:, span(b)]], 1),
                ],
                0,
            )
            end = dot(
                jnp.concatenate([carried_ahead[f], carried_behind[b]], 1), sides, ((1,), (1,))
            )
            factor = jnp.where(
                ahead_half[:HEADS],
                total[HEADS * f : HEADS * f + HEADS],
                total[HEADS * b : HEADS * b + HEADS],
            )
            states.append(by_head(states[-1], factor, 0) + end)
        for j in range(per_line):
            mirror = states[per_line - 1 - j]
            ahead = jnp.concatenate([ahead_half] * (INNER // CHUNK), 0)
            joined[start + j] = jnp.where(ahead, states[j], mirror).astype(BF16)

    gain = jnp.transpose(
        jnp.broadcast_to(gain_ref[layer : layer + 1, :], (CHUNK, INNER))
    )
    rounded = []
    for k in range(chunks):
        left = jnp.concatenate([entered[k], joined[k]], 1)
        leave_k = leave[:, span(k)]
        scores = dot(enter[:, span(k)], leave_k, ((0,), (0,))) * double
        leave_k = leave_k.astype(F32)
        mixed = []
        for pair in range(HEADS // 2):
            rights = []
            for row in (HEADS * k + 2 * pair, HEADS * k + 2 * pair + 1):
                gap = mid2_columns[:, row : row + 1] - mid2[row : row + 1]
                mixing = (scores * jnp.exp2(-jnp.abs(gap))).astype(BF16)
                rights.append(
                    jnp.concatenate(
                        [
                            mixing,
                            (leave_k * lead[row : row + 1]).astype(BF16),
                            (leave_k * tail[row : row + 1]).astype(BF16),
                        ],
                        0,
                    )
                )
            both = dot(left[CHUNK * pair : CHUNK * pair + CHUNK], jnp.concatenate(rights, 1))
            mixed += [both[:SIZE, :CHUNK], both[SIZE:, CHUNK:]]
        gated = by_head(jnp.concatenate(mixed, 0), growth, k) * silu(gates[:, span(k)])
        scale = lax.rsqrt(jnp.mean(gated * gated, axis=0, keepdims=True) + EPSILON)
        rounded.append((gated * scale * gain).astype(BF16))

    out_copy.wait()
    results = []
    for k in range(chunks):
        change = dot(rounded[k], out_w_ref[...], ((0,), (0,)))
        results.append((h[span(k)] + change).astype(BF16))
    if interleaved:
        perm = gather_matrix(leaving)
        half = tokens // 256
        for a in range(half):
            o_ref[256 * a : 256 * a + 256, :] = dot(
                perm, jnp.concatenate([results[a], results[half + a]], 0), ((0,), (0,))
            ).astype(BF16)
    else:
        for k in range(chunks):
            o_ref[span(k), :] = results[k]


def mix(x, layer, lines, interleaved, weights):
    norm_gain, inner_weight, state_weight, step_weight, step_bias, decay_rate, out_gain, out_weight = weights
    whole = lambda a: pl.BlockSpec(a.shape, lambda i: (0,) * a.ndim)
    part = lambda a: pl.BlockSpec((1,) + a.shape[1:], lambda i: (layer, 0, 0))
    step_weight = jnp.swapaxes(step_weight, 1, 2)
    return pl.pallas_call(
        functools.partial(layer_kernel, layer, lines, interleaved),
        grid=(1,),
        out_shape=jax.ShapeDtypeStruct(x.shape, BF16),
        in_specs=[
            whole(x),
            whole(norm_gain),
            part(inner_weight),
            part(state_weight),
            part(step_weight),
            whole(step_bias),
            whole(decay_rate),
            whole(out_gain),
            pl.BlockSpec(memory_space=pltpu.HBM),
        ],
        out_specs=whole(x),
        scratch_shapes=[pltpu.VMEM(out_weight.shape[1:], BF16), pltpu.SemaphoreType.DMA],
        compiler_params=pltpu.CompilerParams(vmem_limit_bytes=40 * 1024 * 1024),
        name=f"mix_layer_{layer}",
    )(
        x,
        norm_gain,
        inner_weight,
        state_weight,
        step_weight,
        step_bias,
        decay_rate,
        out_gain,
        out_weight,
    )


def on_device(gx, gy, field, *weights):
    nx, ny, width = field.shape
    lines = ny // gx
    sent = jnp.swapaxes(field, 0, 1).reshape(gx, lines * nx, width)
    taken = lax.all_to_all(sent, "gx", 0, 0, tiled=True).reshape(gx * nx * lines, width)
    stream = mix(taken, 0, lines, True, weights)
    taken = lax.all_to_all(
        stream.reshape(gx * nx, lines, width), ("gx", "gy"), 0, 0, tiled=True
    )
    taken = jnp.swapaxes(taken.reshape(gx, gy, lines, width), 0, 1)
    stream = mix(taken.reshape(gy * gx * lines, width), 1, 1, False, weights)
    return lax.all_to_all(stream.reshape(gy, ny, width), "gy", 0, 0, tiled=True)


def solution(mesh):
    in_specs = (P("gx", "gy", None), P(), P(), P(), P(), P(), P(), P(), P())
    return jax.shard_map(
        functools.partial(on_device, mesh.shape["gx"], mesh.shape["gy"]),
        mesh=mesh,
        in_specs=in_specs,
        out_specs=P("gx", "gy", None),
        check_vma=False,
    )
```

time: 72.8 us -> 72.2 us (level)
  blocking collectives: 32.3 us -> 57.8 us
  starting transfers between devices: 12.8 us -> 0 us
  waiting for transfers between devices: 12 us -> 0 us
  Pallas kernels: 8.22 us -> 6.03 us
  local copies, waits for them, and re-layouts: 7.08 us -> 7.9 us
    all_to_all x0 -> x1, blocking collectives: none -> 25.5 us  [on_device(): lax.all_to_all(sent, 'gx', 0, 0, tiled=True).reshape(gx * nx * lines, width)]
    all_to_all x1 -> x0, starting transfers between devices: 12.8 us -> none  [on_device(): lax.all_to_all(sent, 'gx', 0, 0, tiled=True).reshape(gx * nx * lines, width)]
    all_to_all x1 -> x0, waiting for transfers between devices: 12 us -> none  [on_device(): lax.all_to_all(sent, 'gx', 0, 0, tiled=True).reshape(gx * nx * lines, width)]
    pallas_call x2, Pallas kernels: 8.22 us -> 6.03 us  [mix(): pl.pallas_call(functools.partial(layer_kernel, layer, lines, interleaved)...]
    unnamed x23 -> x28, local copies, waits for them, and re-layouts: 6.57 us -> 7.39 us
  transfers between devices with their start and end apart: 1 -> 0, of which waited for: 1 -> 0; matrix products, arithmetic and copies ran while one was open for 1% -> 0% of each run, Pallas kernels for 0% -> 0%
where the time goes in v3:
time: 72.2 us; the launch traced here: 71.8 us
  blocking collectives  57.8 us (80%)
  local copies, waits for them, and re-layouts  7.9 us (11%)
  Pallas kernels  6.03 us (8%)
    all_to_all x1, blocking collectives, on_device(): lax.all_to_all(sent, 'gx', 0, 0, tiled=True).reshape(gx * nx * lines, width)  25.5 us
    all_to_all x1, blocking collectives, on_device(): lax.all_to_all(stream.reshape(gx * nx, lines, width), ('gx', 'gy'), 0, 0,...  21.7 us
    all_to_all x1, blocking collectives, on_device(): return lax.all_to_all(stream.reshape(gy, ny, width), 'gy', 0, 0, tiled=True)  10.5 us
    unnamed x28, local copies, waits for them, and re-layouts  7.39 us
    pallas_call x2, Pallas kernels, mix(): pl.pallas_call(functools.partial(layer_kernel, layer, lines, interleaved)...  6.03 us

profile of v3, /device:TPU:1, one launch (start us, length us, event | category | flops | bytes accessed | tf_op | source)
XLA Modules:
  0.0 71.8 jit_solution(17731991204515689769)
XLA Ops:
  0.0 0.0 copy-start
  0.0 1.2 %copy.13 = bf16[8,64,256]{2,0,1:T(8,128)(2,1)S(1)} copy(bf16[8,64,256]{2,1,0:T(8,128)(2,1)} %param.9) | data formatting | bytes 524288 | tf_op args[0]
  1.2 0.0 copy-start.7
  1.2 25.5 %all_to_all.15 = bf16[32,16,256]{2,1,0:T(8,128)(2,1)S(1)} all-to-all(bf16[32,16,256]{2,1,0:T(8,128)(2,1)S(1)} %bitcast.16), channel_id=1, replica_groups=mesh['gx'=32,'gy'=8] {'gx'}, dimensions={0} | all-to-all | bytes 524288 | tf_op jit(solution)/shard_map/all_to_all | solution.py:282
  26.7 0.0 copy-start.10
  26.7 0.0 copy-done
  26.7 0.0 copy-done.7
  26.7 0.7 copy-done.10
  27.4 0.0 copy-start.1
  27.4 1.0 %copy-done.1 = bf16[2,512,256]{2,1,0:T(8,128)(2,1)S(1)} copy-done((bf16[2,512,256]{2,1,0:T(8,128)(2,1)S(1)}, bf16[2,512,256]{2,1,0:T(8,128)(2,1)}, u32[]{:S(2)}) %copy-start.1) | copy-done | bytes 524312
  28.4 0.9 %copy-done.3 = bf16[2,256,128]{2,1,0:T(8,128)(2,1)S(1)} copy-done((bf16[2,256,128]{2,1,0:T(8,128)(2,1)S(1)}, bf16[2,256,128]{2,1,0:T(8,128)(2,1)}, u32[]{:S(2)}) %copy-start.3) | copy-done | bytes 131096
  29.3 0.7 copy-done.5
  30.0 0.7 copy-done.8
  30.7 0.7 copy-done.11
  31.4 3.2 %mix_layer_0.1 = bf16[512,256]{1,0:T(8,128)(2,1)S(1)} custom-call(bf16[512,256]{1,0:T(8,128)(2,1)S(1)} %bitcast.11, f32[2,256]{1,0:T(2,128)S(1)} %copy-done.8, bf16[2,256,1024]{2,1,0:T(8,128)(2,1)S(1)} %copy-done, bf16[2,256,128]{2,1,0:T(8,128)(2,1)S(1)} %copy-done.3, bf16[2,8,256]{2,1,0:T(8,128)(2,1)S(1)} %bitcast.13, f32[2,8]{1,0:T(2,128)S(1)} %copy-done.10, ...), custom_call_target="tpu_custom_call" | custom-call | tf_op jit(solution)/shard_map/mix_layer_0/pallas_call | solution.py:246
  34.6 0.1 reshape.20
  34.7 21.7 %all_to_all.16 = bf16[256,2,256]{2,1,0:T(2,128)(2,1)S(1)} all-to-all(bf16[256,2,256]{2,1,0:T(2,128)(2,1)S(1)} %reshape.20), channel_id=1, replica_groups=mesh['gx'=32,'gy'=8] {'gx','gy'}, dimensions={0} | all-to-all | bytes 524288 | tf_op jit(solution)/shard_map/all_to_all | solution.py:284
  56.5 0.0 copy-start.2
  56.5 0.3 copy.15
  56.8 0.0 copy-start.4
  56.8 0.0 copy-start.6
  56.8 0.0 copy-start.9
  56.8 0.0 copy-start.12
  56.8 0.1 reshape.22.x_ref
  56.9 0.6 copy-done.2
  57.5 0.2 copy-done.4
  57.7 0.0 copy-done.6
  57.7 0.0 copy-done.9
  57.7 0.0 copy-done.12
  57.7 2.8 %mix_layer_1.1 = bf16[512,256]{1,0:T(8,128)(2,1)S(1)} custom-call(bf16[512,256]{1,0:T(8,128)(2,1)S(1)} %reshape.22.x_ref, f32[2,256]{1,0:T(2,128)S(1)} %copy-done.9, bf16[2,256,1024]{2,1,0:T(8,128)(2,1)S(1)} %copy-done, bf16[2,256,128]{2,1,0:T(8,128)(2,1)S(1)} %copy-done.4, bf16[2,8,256]{2,1,0:T(8,128)(2,1)S(1)} %bitcast.14, f32[2,8]{1,0:T(2,128)S(1)} %copy-done.10, ...), custom_call_target="tpu_custom_call" | custom-call | tf_op jit(solution)/shard_map/mix_layer_1/pallas_call | solution.py:246
  60.6 10.5 %all_to_all.17 = bf16[8,64,256]{2,1,0:T(8,128)(2,1)S(1)} all-to-all(bf16[8,64,256]{2,1,0:T(8,128)(2,1)S(1)} %bitcast.12), channel_id=1, replica_groups=mesh['gx'=32,'gy'=8] {'gy'}, dimensions={0} | all-to-all | bytes 524288 | tf_op jit(solution)/shard_map/all_to_all | solution.py:289
  71.1 0.7 copy.19
  (5 shorter events, 0.0 us)
Async XLA Ops:
  0.0 26.7 %copy-start = (bf16[2,256,1024]{2,1,0:T(8,128)(2,1)S(1)}, bf16[2,256,1024]{2,1,0:T(8,128)(2,1)}, u32[]{:S(2)}) copy-start(bf16[2,256,1024]{2,1,0:T(8,128)(2,1)} %inner_ref.3) | copy-start | bytes 3145732
  1.2 25.5 %copy-start.7 = (f32[2,512]{1,0:T(2,128)S(1)}, f32[2,512]{1,0:T(2,128)}, u32[]{:S(2)}) copy-start(f32[2,512]{1,0:T(2,128)} %gain_ref.3) | copy-start | bytes 12292
  26.7 0.7 copy-start.10
  27.4 1.0 %copy-start.1 = (bf16[2,512,256]{2,1,0:T(8,128)(2,1)S(1)}, bf16[2,512,256]{2,1,0:T(8,128)(2,1)}, u32[]{:S(2)}) copy-start(bf16[2,512,256]{2,1,0:T(8,128)(2,1)} %out_w_hbm.3) | copy-start | bytes 1572868
  28.4 0.9 %copy-start.3 = (bf16[2,256,128]{2,1,0:T(8,128)(2,1)S(1)}, bf16[2,256,128]{2,1,0:T(8,128)(2,1)}, u32[]{:S(2)}) copy-start(bf16[2,256,128]{2,1,0:T(8,128)(2,1)} %state_ref.3) | copy-start | bytes 393220
  29.3 0.7 copy-start.5
  30.0 0.7 copy-start.8
  30.7 0.7 copy-start.11
  56.5 1.0 %copy-start.2 = (bf16[2,512,256]{2,1,0:T(8,128)(2,1)S(1)}, bf16[2,512,256]{2,1,0:T(8,128)(2,1)}, u32[]{:S(2)}) copy-start(bf16[2,512,256]{2,1,0:T(8,128)(2,1)} %out_w_hbm.3) | copy-start | bytes 1572868
  56.8 0.9 %copy-start.4 = (bf16[2,256,128]{2,1,0:T(8,128)(2,1)S(1)}, bf16[2,256,128]{2,1,0:T(8,128)(2,1)}, u32[]{:S(2)}) copy-start(bf16[2,256,128]{2,1,0:T(8,128)(2,1)} %state_ref.3) | copy-start | bytes 393220
  56.8 0.9 %copy-start.6 = (bf16[2,256,8]{1,2,0:T(8,128)(2,1)S(1)}, bf16[2,256,8]{1,2,0:T(8,128)(2,1)}, u32[]{:S(2)}) copy-start(bf16[2,256,8]{1,2,0:T(8,128)(2,1)} %param.13) | copy-start | bytes 24580
  56.8 0.9 %copy-start.9 = (f32[2,256]{1,0:T(2,128)S(1)}, f32[2,256]{1,0:T(2,128)}, u32[]{:S(2)}) copy-start(f32[2,256]{1,0:T(2,128)} %norm_ref.3) | copy-start | bytes 6148
  56.8 0.9 %copy-start.12 = (f32[2,8]{1,0:T(2,128)S(1)}, f32[2,8]{1,0:T(2,128)}, u32[]{:S(2)}) copy-start(f32[2,8]{1,0:T(2,128)} %rate_ref.3) | copy-start | bytes 196

commit v4 on v3

--- a/solution.py
+++ b/solution.py
@@ -60,11 +60,7 @@
     return jnp.sum(jnp.where(square, jnp.broadcast_to(row, (n, n)), 0.0), 1, keepdims=True)
 
 
-def layer_kernel(
-    layer,
-    lines,
-    interleaved,
-    x_ref,
+def prepare_kernel(
     norm_ref,
     inner_ref,
     state_ref,
@@ -72,13 +68,55 @@
     bias_ref,
     rate_ref,
     gain_ref,
-    out_w_hbm,
-    o_ref,
     out_w_ref,
-    out_w_sem,
+    weights_ref,
+    out_ref,
+    small_ref,
 ):
-    out_copy = pltpu.make_async_copy(out_w_hbm.at[layer], out_w_ref, out_w_sem)
-    out_copy.start()
+    base = 2 * INNER + 2 * ORDER
+    for layer in range(2):
+        weights_ref[layer, : 2 * INNER, :] = jnp.transpose(inner_ref[layer])
+        weights_ref[layer, 2 * INNER : base, :] = jnp.transpose(state_ref[layer])
+        weights_ref[layer, base:, :] = jnp.concatenate(
+            [step_ref[layer], jnp.zeros_like(step_ref[layer])], 0
+        )
+        out_ref[layer] = out_w_ref[layer]
+        row = slice(layer, layer + 1)
+        wide = (HEADS, INNER)
+        small_ref[layer, :HEADS, :] = jnp.broadcast_to(column(bias_ref[row, :]), wide)
+        small_ref[layer, HEADS : 2 * HEADS, :] = jnp.broadcast_to(column(rate_ref[row, :]), wide)
+        norm = norm_ref[row, :]
+        small_ref[layer, 2 * HEADS :, :] = jnp.concatenate(
+            [
+                gain_ref[row, :],
+                jnp.concatenate([norm, norm], 1),
+                jnp.zeros((HEADS - 2, INNER), F32),
+            ],
+            0,
+        )
+
+
+def prepare(norm_gain, inner, state, step, bias, rate, gain, out_weight):
+    step = jnp.swapaxes(step, 1, 2)
+    rows = inner.shape[2] + state.shape[2] + 2 * HEADS
+    return pl.pallas_call(
+        prepare_kernel,
+        out_shape=(
+            jax.ShapeDtypeStruct((2, rows, inner.shape[1]), BF16),
+            jax.ShapeDtypeStruct(out_weight.shape, BF16),
+            jax.ShapeDtypeStruct((2, 3 * HEADS, INNER), F32),
+        ),
+        in_specs=[pl.BlockSpec(memory_space=pltpu.VMEM)] * 8,
+        out_specs=[pl.BlockSpec(memory_space=pltpu.VMEM)] * 3,
+        compiler_params=pltpu.CompilerParams(vmem_limit_bytes=16 * 1024 * 1024),
+        cost_estimate=pl.CostEstimate(flops=0, bytes_accessed=4 * 1024 * 1024, transcendentals=0),
+        name="prepare_weights",
+    )(norm_gain, inner, state, step, bias, rate, gain, out_weight)
+
+
+def layer_kernel(
+    layer, lines, interleaved, x_ref, weights_ref, out_w_ref, small_ref, o_ref
+):
     tokens = x_ref.shape[0]
     chunks = tokens // CHUNK
     per_line = chunks // lines
@@ -94,26 +132,18 @@
     else:
         h = raw.astype(F32)
     scale = lax.rsqrt(jnp.mean(h * h, axis=1, keepdims=True) + EPSILON)
-    normed = (h * scale * norm_ref[layer : layer + 1, :]).astype(BF16)
-
-    weights = jnp.concatenate(
-        [
-            jnp.transpose(jnp.concatenate([inner_ref[0], state_ref[0]], 1)),
-            step_ref[0],
-            jnp.zeros_like(step_ref[0]),
-        ],
-        0,
-    )
-    projected = dot(weights, normed, ((1,), (1,)))
+    normed = (h * scale * small_ref[layer, 2 * HEADS + 1 : 2 * HEADS + 2, : h.shape[1]]).astype(BF16)
+
+    projected = dot(weights_ref[layer], normed, ((1,), (1,)))
     gates = projected[:INNER]
     inputs = silu(projected[INNER : 2 * INNER]).astype(BF16)
     base = 2 * INNER
     enter = projected[base : base + ORDER].astype(BF16)
     leave = projected[base + ORDER : base + 2 * ORDER].astype(BF16)
     raw_steps = projected[base + 2 * ORDER : base + 2 * ORDER + HEADS]
-    raw_steps = raw_steps + column(bias_ref[layer : layer + 1, :])
+    raw_steps = raw_steps + small_ref[layer, :HEADS, :]
     steps = jnp.maximum(raw_steps, 0.0) + jnp.log1p(jnp.exp(-jnp.abs(raw_steps)))
-    decay = -steps * column(rate_ref[layer : layer + 1, :])
+    decay = -steps * small_ref[layer, HEADS : 2 * HEADS, :]
     steps = jnp.concatenate([steps[:, CHUNK * k : CHUNK * k + CHUNK] for k in range(chunks)], 0)
     decay = jnp.concatenate([decay[:, CHUNK * k : CHUNK * k + CHUNK] for k in range(chunks)], 0)
     first = decay.astype(BF16)
@@ -191,7 +221,7 @@
             joined[start + j] = jnp.where(ahead, states[j], mirror).astype(BF16)
 
     gain = jnp.transpose(
-        jnp.broadcast_to(gain_ref[layer : layer + 1, :], (CHUNK, INNER))
+        jnp.broadcast_to(small_ref[layer, 2 * HEADS : 2 * HEADS + 1, :], (CHUNK, INNER))
     )
     rounded = []
     for k in range(chunks):
@@ -221,10 +251,9 @@
         scale = lax.rsqrt(jnp.mean(gated * gated, axis=0, keepdims=True) + EPSILON)
         rounded.append((gated * scale * gain).astype(BF16))
 
-    out_copy.wait()
     results = []
     for k in range(chunks):
-        change = dot(rounded[k], out_w_ref[...], ((0,), (0,)))
+        change = dot(rounded[k], out_w_ref[layer], ((0,), (0,)))
         results.append((h[span(k)] + change).astype(BF16))
     if interleaved:
         perm = gather_matrix(leaving)
@@ -239,44 +268,19 @@
 
 
 def mix(x, layer, lines, interleaved, weights):
-    norm_gain, inner_weight, state_weight, step_weight, step_bias, decay_rate, out_gain, out_weight = weights
-    whole = lambda a: pl.BlockSpec(a.shape, lambda i: (0,) * a.ndim)
-    part = lambda a: pl.BlockSpec((1,) + a.shape[1:], lambda i: (layer, 0, 0))
-    step_weight = jnp.swapaxes(step_weight, 1, 2)
     return pl.pallas_call(
         functools.partial(layer_kernel, layer, lines, interleaved),
-        grid=(1,),
         out_shape=jax.ShapeDtypeStruct(x.shape, BF16),
-        in_specs=[
-            whole(x),
-            whole(norm_gain),
-            part(inner_weight),
-            part(state_weight),
-            part(step_weight),
-            whole(step_bias),
-            whole(decay_rate),
-            whole(out_gain),
-            pl.BlockSpec(memory_space=pltpu.HBM),
-        ],
-        out_specs=whole(x),
-        scratch_shapes=[pltpu.VMEM(out_weight.shape[1:], BF16), pltpu.SemaphoreType.DMA],
-        compiler_params=pltpu.CompilerParams(vmem_limit_bytes=40 * 1024 * 1024),
+        in_specs=[pl.BlockSpec(memory_space=pltpu.VMEM)] * 4,
+        out_specs=pl.BlockSpec(memory_space=pltpu.VMEM),
+        compiler_params=pltpu.CompilerParams(vmem_limit_bytes=32 * 1024 * 1024),
         name=f"mix_layer_{layer}",
-    )(
-        x,
-        norm_gain,
-        inner_weight,
-        state_weight,
-        step_weight,
-        step_bias,
-        decay_rate,
-        out_gain,
-        out_weight,
-    )
+    )(x, *weights)
 
 
 def on_device(gx, gy, field, *weights):
     nx, ny, width = field.shape
+    weights = prepare(*weights)
     lines = ny // gx
     sent = jnp.swapaxes(field, 0, 1).reshape(gx, lines * nx, width)
     taken = lax.all_to_all(sent, "gx", 0, 0, tiled=True).reshape(gx * nx * lines, width)

time: 72.2 us -> 66.8 us (0.925)
  blocking collectives: 57.8 us -> 32.1 us
  starting transfers between devices: 0 us -> 12.8 us
  waiting for transfers between devices: 0 us -> 7.14 us
    all_to_all x1 -> x0, blocking collectives: 25.5 us -> none  [on_device(): lax.all_to_all(sent, 'gx', 0, 0, tiled=True).reshape(gx * nx * lines, width)]
    all_to_all x0 -> x1, starting transfers between devices: none -> 12.8 us  [on_device(): lax.all_to_all(sent, 'gx', 0, 0, tiled=True).reshape(gx * nx * lines, width)]
    all_to_all x0 -> x1, waiting for transfers between devices: none -> 7.14 us  [on_device(): lax.all_to_all(sent, 'gx', 0, 0, tiled=True).reshape(gx * nx * lines, width)]
    unnamed x28 -> x18, local copies, waits for them, and re-layouts: 7.39 us -> 7.96 us
  transfers between devices with their start and end apart: 0 -> 1, of which waited for: 0 -> 1; matrix products, arithmetic and copies ran while one was open for 0% -> 0% of each run, Pallas kernels for 0% -> 1%
where the time goes in v4:
time: 66.8 us; the launch traced here: 66.4 us
  blocking collectives  32.1 us (48%)
  starting transfers between devices  12.8 us (19%)
  local copies, waits for them, and re-layouts  8.46 us (13%)
  waiting for transfers between devices  7.14 us (11%)
  Pallas kernels  5.85 us (9%)
    all_to_all x1, blocking collectives, on_device(): lax.all_to_all(stream.reshape(gx * nx, lines, width), ('gx', 'gy'), 0, 0,...  21.7 us
    all_to_all x1, starting transfers between devices, on_device(): lax.all_to_all(sent, 'gx', 0, 0, tiled=True).reshape(gx * nx * lines, width)  12.8 us
    all_to_all x1, blocking collectives, on_device(): return lax.all_to_all(stream.reshape(gy, ny, width), 'gy', 0, 0, tiled=True)  10.4 us
    unnamed x18, local copies, waits for them, and re-layouts  7.96 us
    all_to_all x1, waiting for transfers between devices, on_device(): lax.all_to_all(sent, 'gx', 0, 0, tiled=True).reshape(gx * nx * lines, width)  7.14 us
    pallas_call x2, Pallas kernels, mix(): pl.pallas_call(functools.partial(layer_kernel, layer, lines, interleaved)...  5.45 us
  transfers between devices with their start and end apart: 1, of which 1 were waited for; matrix products, arithmetic and copies ran while one was open for 0% of the time, Pallas kernels for 1%

profile of v4, /device:TPU:1, one launch (start us, length us, event | category | flops | bytes accessed | tf_op | source)
XLA Modules:
  0.0 66.4 jit_solution(11114687599658821070)
XLA Ops:
  0.0 0.0 copy-start
  0.0 1.9 %copy.13 = bf16[8,64,256]{2,0,1:T(8,128)(2,1)} copy(bf16[8,64,256]{2,1,0:T(8,128)(2,1)} %param.9) | data formatting | bytes 524288 | tf_op args[0]
  1.9 12.8 %all-to-all-start = ((bf16[32,16,256]{2,1,0:T(8,128)(2,1)}), bf16[32,16,256]{2,1,0:T(8,128)(2,1)S(1)}, u32[]{:S(2)}, u32[]{:S(2)}) async-start(bf16[32,16,256]{2,1,0:T(8,128)(2,1)} %bitcast.1), calls=%async_computation | async-start | bytes 524288 | tf_op jit(solution)/shard_map/all_to_all | solution.py:286
  14.7 0.0 copy-done
  14.7 0.0 copy-start.1
  14.7 1.0 %copy-done.1 = bf16[2,512,256]{2,1,0:T(8,128)(2,1)S(1)} copy-done((bf16[2,512,256]{2,1,0:T(8,128)(2,1)S(1)}, bf16[2,512,256]{2,1,0:T(8,128)(2,1)}, u32[]{:S(2)}) %copy-start.1) | copy-done | bytes 524312
  15.7 0.0 copy-start.2
  15.7 0.9 %copy-done.2 = bf16[2,256,128]{2,1,0:T(8,128)(2,1)S(1)} copy-done((bf16[2,256,128]{2,1,0:T(8,128)(2,1)S(1)}, bf16[2,256,128]{2,1,0:T(8,128)(2,1)}, u32[]{:S(2)}) %copy-start.2) | copy-done | bytes 131096
  16.6 0.0 copy-start.3
  16.6 0.7 %copy-done.3 = bf16[2,256,8]{1,2,0:T(8,128)(2,1)S(1)} copy-done((bf16[2,256,8]{1,2,0:T(8,128)(2,1)S(1)}, bf16[2,256,8]{1,2,0:T(8,128)(2,1)}, u32[]{:S(2)}) %copy-start.3) | copy-done | bytes 8216
  17.3 0.0 copy-start.4
  17.3 0.7 %copy-done.4 = f32[2,512]{1,0:T(2,128)S(1)} copy-done((f32[2,512]{1,0:T(2,128)S(1)}, f32[2,512]{1,0:T(2,128)}, u32[]{:S(2)}) %copy-start.4) | copy-done | bytes 4120
  18.0 0.0 copy-start.5
  18.0 0.7 %copy-done.5 = f32[2,256]{1,0:T(2,128)S(1)} copy-done((f32[2,256]{1,0:T(2,128)S(1)}, f32[2,256]{1,0:T(2,128)}, u32[]{:S(2)}) %copy-start.5) | copy-done | bytes 2072
  18.7 0.0 copy-start.6
  18.7 0.7 %copy-done.6 = f32[2,8]{1,0:T(2,128)S(1)} copy-done((f32[2,8]{1,0:T(2,128)S(1)}, f32[2,8]{1,0:T(2,128)}, u32[]{:S(2)}) %copy-start.6) | copy-done | bytes 88
  19.4 0.0 copy-start.7
  19.4 0.7 %copy-done.7 = f32[2,8]{1,0:T(2,128)S(1)} copy-done((f32[2,8]{1,0:T(2,128)S(1)}, f32[2,8]{1,0:T(2,128)}, u32[]{:S(2)}) %copy-start.7) | copy-done | bytes 88
  20.0 0.4 prepare_weights.1
  20.5 7.1 %all-to-all-done = bf16[32,16,256]{2,1,0:T(8,128)(2,1)S(1)} async-done(((bf16[32,16,256]{2,1,0:T(8,128)(2,1)}), bf16[32,16,256]{2,1,0:T(8,128)(2,1)S(1)}, u32[]{:S(2)}, u32[]{:S(2)}) %all-to-all-start) | async-done | bytes 262176 | tf_op jit(solution)/shard_map/all_to_all | solution.py:286
  27.6 2.9 %mix_layer_0.1 = bf16[512,256]{1,0:T(8,128)(2,1)S(1)} custom-call(bf16[512,256]{1,0:T(8,128)(2,1)S(1)} %bitcast.11, bf16[2,1168,256]{2,1,0:T(8,128)(2,1)S(1)} %get-tuple-element.8.weights_ref, bf16[2,512,256]{2,1,0:T(8,128)(2,1)S(1)} %get-tuple-element.9.out_w_ref, f32[2,24,512]{2,1,0:T(8,128)S(1)} %get-tuple-element.10.small_ref), custom_call_target="tpu_custom_call" | custom-call | tf_op jit(solution)/shard_map/mix_layer_0/pallas_call | solution.py:271
  30.5 0.1 reshape.20
  30.6 21.7 %all_to_all.15 = bf16[256,2,256]{2,1,0:T(2,128)(2,1)S(1)} all-to-all(bf16[256,2,256]{2,1,0:T(2,128)(2,1)S(1)} %reshape.20), channel_id=1, replica_groups=mesh['gx'=32,'gy'=8] {'gx','gy'}, dimensions={0} | all-to-all | bytes 524288 | tf_op jit(solution)/shard_map/all_to_all | solution.py:288
  52.4 0.3 copy.15
  52.6 0.1 reshape.22.x_ref
  52.7 2.6 %mix_layer_1.1 = bf16[512,256]{1,0:T(8,128)(2,1)S(1)} custom-call(bf16[512,256]{1,0:T(8,128)(2,1)S(1)} %reshape.22.x_ref, bf16[2,1168,256]{2,1,0:T(8,128)(2,1)S(1)} %get-tuple-element.8.weights_ref, bf16[2,512,256]{2,1,0:T(8,128)(2,1)S(1)} %get-tuple-element.9.out_w_ref, f32[2,24,512]{2,1,0:T(8,128)S(1)} %get-tuple-element.10.small_ref), custom_call_target="tpu_custom_call" | custom-call | tf_op jit(solution)/shard_map/mix_layer_1/pallas_call | solution.py:271
  55.3 10.4 %all_to_all.16 = bf16[8,64,256]{2,1,0:T(8,128)(2,1)S(1)} all-to-all(bf16[8,64,256]{2,1,0:T(8,128)(2,1)S(1)} %bitcast.12), channel_id=1, replica_groups=mesh['gx'=32,'gy'=8] {'gy'}, dimensions={0} | all-to-all | bytes 524288 | tf_op jit(solution)/shard_map/all_to_all | solution.py:293
  65.7 0.7 %copy.19 = bf16[8,64,256]{2,1,0:T(8,128)(2,1)} copy(bf16[8,64,256]{2,1,0:T(8,128)(2,1)S(1)} %all_to_all.16) | data formatting | bytes 524288
  (1 shorter events, 0.0 us)
Async XLA Ops:
  0.0 14.7 %copy-start = (bf16[2,256,1024]{2,1,0:T(8,128)(2,1)S(1)}, bf16[2,256,1024]{2,1,0:T(8,128)(2,1)}, u32[]{:S(2)}) copy-start(bf16[2,256,1024]{2,1,0:T(8,128)(2,1)} %inner_ref.1) | copy-start | bytes 3145732
  1.9 25.7 %all-to-all-start = ((bf16[32,16,256]{2,1,0:T(8,128)(2,1)}), bf16[32,16,256]{2,1,0:T(8,128)(2,1)S(1)}, u32[]{:S(2)}, u32[]{:S(2)}) async-start(bf16[32,16,256]{2,1,0:T(8,128)(2,1)} %bitcast.1), calls=%async_computation | async-start | bytes 524288 | tf_op jit(solution)/shard_map/all_to_all | solution.py:286
  14.7 1.0 %copy-start.1 = (bf16[2,512,256]{2,1,0:T(8,128)(2,1)S(1)}, bf16[2,512,256]{2,1,0:T(8,128)(2,1)}, u32[]{:S(2)}) copy-start(bf16[2,512,256]{2,1,0:T(8,128)(2,1)} %out_w_ref.1) | copy-start | bytes 1572868
  15.7 0.9 %copy-start.2 = (bf16[2,256,128]{2,1,0:T(8,128)(2,1)S(1)}, bf16[2,256,128]{2,1,0:T(8,128)(2,1)}, u32[]{:S(2)}) copy-start(bf16[2,256,128]{2,1,0:T(8,128)(2,1)} %state_ref.1) | copy-start | bytes 393220
  16.6 0.7 %copy-start.3 = (bf16[2,256,8]{1,2,0:T(8,128)(2,1)S(1)}, bf16[2,256,8]{1,2,0:T(8,128)(2,1)}, u32[]{:S(2)}) copy-start(bf16[2,256,8]{1,2,0:T(8,128)(2,1)} %param.13) | copy-start | bytes 24580
  17.3 0.7 %copy-start.4 = (f32[2,512]{1,0:T(2,128)S(1)}, f32[2,512]{1,0:T(2,128)}, u32[]{:S(2)}) copy-start(f32[2,512]{1,0:T(2,128)} %gain_ref.1) | copy-start | bytes 12292
  18.0 0.7 %copy-start.5 = (f32[2,256]{1,0:T(2,128)S(1)}, f32[2,256]{1,0:T(2,128)}, u32[]{:S(2)}) copy-start(f32[2,256]{1,0:T(2,128)} %norm_ref.1) | copy-start | bytes 6148
  18.7 0.7 %copy-start.6 = (f32[2,8]{1,0:T(2,128)S(1)}, f32[2,8]{1,0:T(2,128)}, u32[]{:S(2)}) copy-start(f32[2,8]{1,0:T(2,128)} %bias_ref.1) | copy-start | bytes 196
  19.4 0.7 %copy-start.7 = (f32[2,8]{1,0:T(2,128)S(1)}, f32[2,8]{1,0:T(2,128)}, u32[]{:S(2)}) copy-start(f32[2,8]{1,0:T(2,128)} %rate_ref.1) | copy-start | bytes 196

commit v5 on v4

--- a/solution.py
+++ b/solution.py
@@ -31,25 +31,17 @@
     return jnp.concatenate([below, jnp.ones((CHUNK, CHUNK), F32)], 1).astype(BF16)
 
 
-def gather_matrix(source):
-    i, j = positions(2 * CHUNK, 2 * CHUNK)
-    return jnp.where(source(i // CHUNK, i % CHUNK) == j, 1.0, 0.0).astype(BF16)
-
-
-def arriving(line, x):
-    return 16 * (x // 8) + 8 * line + x % 8
-
-
-def leaving(line, x):
-    return 2 * x + line
-
-
 def dot(a, b, dims=((1,), (0,))):
     return lax.dot_general(a, b, (dims, ((), ())), preferred_element_type=F32)
 
 
-def silu(v):
-    return 0.5 * v * (1.0 + jnp.tanh(0.5 * v))
+def silu_of_half(v):
+    return v + v * jnp.tanh(v)
+
+
+def rows16(row, rows):
+    piece = jnp.broadcast_to(row, (16, row.shape[1])).astype(BF16)
+    return jnp.concatenate([piece] * (rows // 16), 0)
 
 
 def column(row):
@@ -75,24 +67,22 @@
 ):
     base = 2 * INNER + 2 * ORDER
     for layer in range(2):
-        weights_ref[layer, : 2 * INNER, :] = jnp.transpose(inner_ref[layer])
+        weights_ref[layer, : 2 * INNER, :] = jnp.transpose(inner_ref[layer] * 0.5)
         weights_ref[layer, 2 * INNER : base, :] = jnp.transpose(state_ref[layer])
         weights_ref[layer, base:, :] = jnp.concatenate(
             [step_ref[layer], jnp.zeros_like(step_ref[layer])], 0
         )
-        out_ref[layer] = out_w_ref[layer]
         row = slice(layer, layer + 1)
+        gain = jnp.transpose(jnp.broadcast_to(gain_ref[row, :], (CHUNK, INNER)))
+        out_ref[layer] = (
+            out_w_ref[layer].astype(F32) * jnp.concatenate([gain, gain], 1)
+        ).astype(BF16)
         wide = (HEADS, INNER)
         small_ref[layer, :HEADS, :] = jnp.broadcast_to(column(bias_ref[row, :]), wide)
         small_ref[layer, HEADS : 2 * HEADS, :] = jnp.broadcast_to(column(rate_ref[row, :]), wide)
         norm = norm_ref[row, :]
-        small_ref[layer, 2 * HEADS :, :] = jnp.concatenate(
-            [
-                gain_ref[row, :],
-                jnp.concatenate([norm, norm], 1),
-                jnp.zeros((HEADS - 2, INNER), F32),
-            ],
-            0,
+        small_ref[layer, 2 * HEADS :, :] = jnp.broadcast_to(
+            jnp.concatenate([norm, norm], 1), wide
         )
 
 
@@ -115,28 +105,27 @@
 
 
 def layer_kernel(
-    layer, lines, interleaved, x_ref, weights_ref, out_w_ref, small_ref, o_ref
+    layer, lines, interleaved, x_ref, weights_ref, out_w_ref, small_ref, o_ref, mixed_ref
 ):
-    tokens = x_ref.shape[0]
+    tokens, width = x_ref.shape
     chunks = tokens // CHUNK
     per_line = chunks // lines
-    raw = x_ref[...]
+    h = x_ref[...].astype(F32)
     if interleaved:
-        perm = gather_matrix(arriving)
-        parts = [
-            dot(perm, raw[256 * a : 256 * a + 256]) for a in range(tokens // 256)
-        ]
         h = jnp.concatenate(
-            [p[CHUNK * l : CHUNK * l + CHUNK] for l in range(2) for p in parts], 0
+            [
+                h[8 * (lines * g + l) : 8 * (lines * g + l) + 8]
+                for l in range(lines)
+                for g in range(tokens // (8 * lines))
+            ],
+            0,
         )
-    else:
-        h = raw.astype(F32)
     scale = lax.rsqrt(jnp.mean(h * h, axis=1, keepdims=True) + EPSILON)
-    normed = (h * scale * small_ref[layer, 2 * HEADS + 1 : 2 * HEADS + 2, : h.shape[1]]).astype(BF16)
+    normed = (h * scale * small_ref[layer, 2 * HEADS : 2 * HEADS + 1, : h.shape[1]]).astype(BF16)
 
     projected = dot(weights_ref[layer], normed, ((1,), (1,)))
     gates = projected[:INNER]
-    inputs = silu(projected[INNER : 2 * INNER]).astype(BF16)
+    inputs = silu_of_half(projected[INNER : 2 * INNER]).astype(BF16)
     base = 2 * INNER
     enter = projected[base : base + ORDER].astype(BF16)
     leave = projected[base + ORDER : base + 2 * ORDER].astype(BF16)
@@ -169,6 +158,7 @@
 
     s_pos, t_pos = positions(CHUNK, CHUNK)
     double = jnp.where(s_pos == t_pos, 2.0, 1.0)
+    falling = jnp.where(s_pos < t_pos, -1.0, 1.0)
     ahead_half = t_pos < ORDER
 
     def span(k):
@@ -187,10 +177,22 @@
     carried_ahead = []
     carried_behind = []
     for k in range(chunks):
-        x = inputs[:, span(k)].astype(F32)
-        entered.append(by_head(x, entry, k).astype(BF16))
-        carried_ahead.append(by_head(x, entry_tail, k).astype(BF16))
-        carried_behind.append(by_head(x, entry_lead, k).astype(BF16))
+        x = inputs[:, span(k)]
+        for kept, factors in (
+            (entered, entry),
+            (carried_ahead, entry_tail),
+            (carried_behind, entry_lead),
+        ):
+            kept.append(
+                jnp.concatenate(
+                    [
+                        x[SIZE * h : SIZE * h + SIZE]
+                        * rows16(factors[HEADS * k + h : HEADS * k + h + 1], SIZE)
+                        for h in range(HEADS)
+                    ],
+                    0,
+                )
+            )
 
     empty = jnp.zeros((ORDER, CHUNK), BF16)
     joined = [None] * chunks
@@ -220,51 +222,45 @@
             ahead = jnp.concatenate([ahead_half] * (INNER // CHUNK), 0)
             joined[start + j] = jnp.where(ahead, states[j], mirror).astype(BF16)
 
-    gain = jnp.transpose(
-        jnp.broadcast_to(small_ref[layer, 2 * HEADS : 2 * HEADS + 1, :], (CHUNK, INNER))
-    )
     rounded = []
     for k in range(chunks):
         left = jnp.concatenate([entered[k], joined[k]], 1)
         leave_k = leave[:, span(k)]
-        scores = dot(enter[:, span(k)], leave_k, ((0,), (0,))) * double
-        leave_k = leave_k.astype(F32)
+        scores = (dot(enter[:, span(k)], leave_k, ((0,), (0,))) * double).astype(BF16)
         mixed = []
         for pair in range(HEADS // 2):
             rights = []
             for row in (HEADS * k + 2 * pair, HEADS * k + 2 * pair + 1):
                 gap = mid2_columns[:, row : row + 1] - mid2[row : row + 1]
-                mixing = (scores * jnp.exp2(-jnp.abs(gap))).astype(BF16)
+                mixing = scores * jnp.exp2(gap * falling).astype(BF16)
                 rights.append(
                     jnp.concatenate(
                         [
                             mixing,
-                            (leave_k * lead[row : row + 1]).astype(BF16),
-                            (leave_k * tail[row : row + 1]).astype(BF16),
+                            leave_k * rows16(lead[row : row + 1], ORDER),
+                            leave_k * rows16(tail[row : row + 1], ORDER),
                         ],
                         0,
                     )
                 )
             both = dot(left[CHUNK * pair : CHUNK * pair + CHUNK], jnp.concatenate(rights, 1))
             mixed += [both[:SIZE, :CHUNK], both[SIZE:, CHUNK:]]
-        gated = by_head(jnp.concatenate(mixed, 0), growth, k) * silu(gates[:, span(k)])
+        gated = by_head(jnp.concatenate(mixed, 0), growth, k) * silu_of_half(gates[:, span(k)])
         scale = lax.rsqrt(jnp.mean(gated * gated, axis=0, keepdims=True) + EPSILON)
-        rounded.append((gated * scale * gain).astype(BF16))
-
-    results = []
+        rounded.append((gated * scale).astype(BF16))
+
     for k in range(chunks):
-        change = dot(rounded[k], out_w_ref[layer], ((0,), (0,)))
-        results.append((h[span(k)] + change).astype(BF16))
+        result = h[span(k)] + dot(rounded[k], out_w_ref[layer], ((0,), (0,)))
+        if interleaved:
+            line, first_x = k // per_line, CHUNK * (k % per_line)
+            for part in range(width // 128):
+                first = part * tokens + lines * first_x + line
+                mixed_ref[pl.ds(first, CHUNK, stride=lines), :] = result[:, span(part)]
+        else:
+            o_ref[span(k), :] = result.astype(BF16)
     if interleaved:
-        perm = gather_matrix(leaving)
-        half = tokens // 256
-        for a in range(half):
-            o_ref[256 * a : 256 * a + 256, :] = dot(
-                perm, jnp.concatenate([results[a], results[half + a]], 0), ((0,), (0,))
-            ).astype(BF16)
-    else:
-        for k in range(chunks):
-            o_ref[span(k), :] = results[k]
+        for part in range(width // 128):
+            o_ref[:, span(part)] = mixed_ref[part * tokens : (part + 1) * tokens, :].astype(BF16)
 
 
 def mix(x, layer, lines, interleaved, weights):
@@ -273,6 +269,7 @@
         out_shape=jax.ShapeDtypeStruct(x.shape, BF16),
         in_specs=[pl.BlockSpec(memory_space=pltpu.VMEM)] * 4,
         out_specs=pl.BlockSpec(memory_space=pltpu.VMEM),
+        scratch_shapes=[pltpu.VMEM((x.size // 128, 128), F32)],
         compiler_params=pltpu.CompilerParams(vmem_limit_bytes=32 * 1024 * 1024),
         name=f"mix_layer_{layer}",
     )(x, *weights)

time: 66.8 us -> 66.3 us (level)
  no operation moved by 1% of the time
where the time goes in v5:
time: 66.3 us; the launch traced here: 65.9 us
  blocking collectives  32.3 us (49%)
  starting transfers between devices  12.8 us (19%)
  local copies, waits for them, and re-layouts  8.46 us (13%)
  waiting for transfers between devices  6.99 us (11%)
  Pallas kernels  5.36 us (8%)
    all_to_all x1, blocking collectives, on_device(): lax.all_to_all(stream.reshape(gx * nx, lines, width), ('gx', 'gy'), 0, 0,...  21.7 us
    all_to_all x1, starting transfers between devices, on_device(): lax.all_to_all(sent, 'gx', 0, 0, tiled=True).reshape(gx * nx * lines, width)  12.8 us
    all_to_all x1, blocking collectives, on_device(): return lax.all_to_all(stream.reshape(gy, ny, width), 'gy', 0, 0, tiled=True)  10.5 us
    unnamed x18, local copies, waits for them, and re-layouts  7.96 us
    all_to_all x1, waiting for transfers between devices, on_device(): lax.all_to_all(sent, 'gx', 0, 0, tiled=True).reshape(gx * nx * lines, width)  6.99 us
    pallas_call x2, Pallas kernels, mix(): pl.pallas_call(functools.partial(layer_kernel, layer, lines, interleaved)...  4.8 us
  transfers between devices with their start and end apart: 1, of which 1 were waited for; matrix products, arithmetic and copies ran while one was open for 0% of the time, Pallas kernels for 1%

profile of v5, /device:TPU:1, one launch (start us, length us, event | category | flops | bytes accessed | tf_op | source)
XLA Modules:
  0.0 65.9 jit_solution(1889479772877225994)
XLA Ops:
  0.0 0.0 copy-start
  0.0 1.9 %copy.13 = bf16[8,64,256]{2,0,1:T(8,128)(2,1)} copy(bf16[8,64,256]{2,1,0:T(8,128)(2,1)} %param.9) | data formatting | bytes 524288 | tf_op args[0]
  1.9 12.8 %all-to-all-start = ((bf16[32,16,256]{2,1,0:T(8,128)(2,1)}), bf16[32,16,256]{2,1,0:T(8,128)(2,1)S(1)}, u32[]{:S(2)}, u32[]{:S(2)}) async-start(bf16[32,16,256]{2,1,0:T(8,128)(2,1)} %bitcast.1), calls=%async_computation | async-start | bytes 524288 | tf_op jit(solution)/shard_map/all_to_all | solution.py:283
  14.7 0.0 copy-done
  14.7 0.0 copy-start.1
  14.7 1.0 %copy-done.1 = bf16[2,512,256]{2,1,0:T(8,128)(2,1)S(1)} copy-done((bf16[2,512,256]{2,1,0:T(8,128)(2,1)S(1)}, bf16[2,512,256]{2,1,0:T(8,128)(2,1)}, u32[]{:S(2)}) %copy-start.1) | copy-done | bytes 524312
  15.7 0.0 copy-start.2
  15.7 0.9 %copy-done.2 = bf16[2,256,128]{2,1,0:T(8,128)(2,1)S(1)} copy-done((bf16[2,256,128]{2,1,0:T(8,128)(2,1)S(1)}, bf16[2,256,128]{2,1,0:T(8,128)(2,1)}, u32[]{:S(2)}) %copy-start.2) | copy-done | bytes 131096
  16.6 0.0 copy-start.3
  16.6 0.7 %copy-done.3 = bf16[2,256,8]{1,2,0:T(8,128)(2,1)S(1)} copy-done((bf16[2,256,8]{1,2,0:T(8,128)(2,1)S(1)}, bf16[2,256,8]{1,2,0:T(8,128)(2,1)}, u32[]{:S(2)}) %copy-start.3) | copy-done | bytes 8216
  17.3 0.0 copy-start.4
  17.3 0.7 %copy-done.4 = f32[2,512]{1,0:T(2,128)S(1)} copy-done((f32[2,512]{1,0:T(2,128)S(1)}, f32[2,512]{1,0:T(2,128)}, u32[]{:S(2)}) %copy-start.4) | copy-done | bytes 4120
  18.0 0.0 copy-start.5
  18.0 0.7 %copy-done.5 = f32[2,256]{1,0:T(2,128)S(1)} copy-done((f32[2,256]{1,0:T(2,128)S(1)}, f32[2,256]{1,0:T(2,128)}, u32[]{:S(2)}) %copy-start.5) | copy-done | bytes 2072
  18.7 0.0 copy-start.6
  18.7 0.7 %copy-done.6 = f32[2,8]{1,0:T(2,128)S(1)} copy-done((f32[2,8]{1,0:T(2,128)S(1)}, f32[2,8]{1,0:T(2,128)}, u32[]{:S(2)}) %copy-start.6) | copy-done | bytes 88
  19.4 0.0 copy-start.7
  19.4 0.7 %copy-done.7 = f32[2,8]{1,0:T(2,128)S(1)} copy-done((f32[2,8]{1,0:T(2,128)S(1)}, f32[2,8]{1,0:T(2,128)}, u32[]{:S(2)}) %copy-start.7) | copy-done | bytes 88
  20.0 0.6 prepare_weights.1
  20.6 7.0 %all-to-all-done = bf16[32,16,256]{2,1,0:T(8,128)(2,1)S(1)} async-done(((bf16[32,16,256]{2,1,0:T(8,128)(2,1)}), bf16[32,16,256]{2,1,0:T(8,128)(2,1)S(1)}, u32[]{:S(2)}, u32[]{:S(2)}) %all-to-all-start) | async-done | bytes 262176 | tf_op jit(solution)/shard_map/all_to_all | solution.py:283
  27.6 2.4 %mix_layer_0.1 = bf16[512,256]{1,0:T(8,128)(2,1)S(1)} custom-call(bf16[512,256]{1,0:T(8,128)(2,1)S(1)} %bitcast.11, bf16[2,1168,256]{2,1,0:T(8,128)(2,1)S(1)} %get-tuple-element.8.weights_ref, bf16[2,512,256]{2,1,0:T(8,128)(2,1)S(1)} %get-tuple-element.9.out_w_ref, f32[2,24,512]{2,1,0:T(8,128)S(1)} %get-tuple-element.10.small_ref), custom_call_target="tpu_custom_call" | custom-call | tf_op jit(solution)/shard_map/mix_layer_0/pallas_call | solution.py:267
  30.0 0.1 reshape.20
  30.1 21.7 %all_to_all.15 = bf16[256,2,256]{2,1,0:T(2,128)(2,1)S(1)} all-to-all(bf16[256,2,256]{2,1,0:T(2,128)(2,1)S(1)} %reshape.20), channel_id=1, replica_groups=mesh['gx'=32,'gy'=8] {'gx','gy'}, dimensions={0} | all-to-all | bytes 524288 | tf_op jit(solution)/shard_map/all_to_all | solution.py:285
  51.9 0.3 copy.15
  52.2 0.1 reshape.22.x_ref
  52.3 2.4 %mix_layer_1.1 = bf16[512,256]{1,0:T(8,128)(2,1)S(1)} custom-call(bf16[512,256]{1,0:T(8,128)(2,1)S(1)} %reshape.22.x_ref, bf16[2,1168,256]{2,1,0:T(8,128)(2,1)S(1)} %get-tuple-element.8.weights_ref, bf16[2,512,256]{2,1,0:T(8,128)(2,1)S(1)} %get-tuple-element.9.out_w_ref, f32[2,24,512]{2,1,0:T(8,128)S(1)} %get-tuple-element.10.small_ref), custom_call_target="tpu_custom_call" | custom-call | tf_op jit(solution)/shard_map/mix_layer_1/pallas_call | solution.py:267
  54.7 10.5 %all_to_all.16 = bf16[8,64,256]{2,1,0:T(8,128)(2,1)S(1)} all-to-all(bf16[8,64,256]{2,1,0:T(8,128)(2,1)S(1)} %bitcast.12), channel_id=1, replica_groups=mesh['gx'=32,'gy'=8] {'gy'}, dimensions={0} | all-to-all | bytes 524288 | tf_op jit(solution)/shard_map/all_to_all | solution.py:290
  65.2 0.7 %copy.19 = bf16[8,64,256]{2,1,0:T(8,128)(2,1)} copy(bf16[8,64,256]{2,1,0:T(8,128)(2,1)S(1)} %all_to_all.16) | data formatting | bytes 524288
  (1 shorter events, 0.0 us)
Async XLA Ops:
  0.0 14.7 %copy-start = (bf16[2,256,1024]{2,1,0:T(8,128)(2,1)S(1)}, bf16[2,256,1024]{2,1,0:T(8,128)(2,1)}, u32[]{:S(2)}) copy-start(bf16[2,256,1024]{2,1,0:T(8,128)(2,1)} %inner_ref.1) | copy-start | bytes 3145732
  1.9 25.7 %all-to-all-start = ((bf16[32,16,256]{2,1,0:T(8,128)(2,1)}), bf16[32,16,256]{2,1,0:T(8,128)(2,1)S(1)}, u32[]{:S(2)}, u32[]{:S(2)}) async-start(bf16[32,16,256]{2,1,0:T(8,128)(2,1)} %bitcast.1), calls=%async_computation | async-start | bytes 524288 | tf_op jit(solution)/shard_map/all_to_all | solution.py:283
  14.7 1.0 %copy-start.1 = (bf16[2,512,256]{2,1,0:T(8,128)(2,1)S(1)}, bf16[2,512,256]{2,1,0:T(8,128)(2,1)}, u32[]{:S(2)}) copy-start(bf16[2,512,256]{2,1,0:T(8,128)(2,1)} %out_w_ref.1) | copy-start | bytes 1572868
  15.7 0.9 %copy-start.2 = (bf16[2,256,128]{2,1,0:T(8,128)(2,1)S(1)}, bf16[2,256,128]{2,1,0:T(8,128)(2,1)}, u32[]{:S(2)}) copy-start(bf16[2,256,128]{2,1,0:T(8,128)(2,1)} %state_ref.1) | copy-start | bytes 393220
  16.6 0.7 %copy-start.3 = (bf16[2,256,8]{1,2,0:T(8,128)(2,1)S(1)}, bf16[2,256,8]{1,2,0:T(8,128)(2,1)}, u32[]{:S(2)}) copy-start(bf16[2,256,8]{1,2,0:T(8,128)(2,1)} %param.13) | copy-start | bytes 24580
  17.3 0.7 %copy-start.4 = (f32[2,512]{1,0:T(2,128)S(1)}, f32[2,512]{1,0:T(2,128)}, u32[]{:S(2)}) copy-start(f32[2,512]{1,0:T(2,128)} %gain_ref.1) | copy-start | bytes 12292
  18.0 0.7 %copy-start.5 = (f32[2,256]{1,0:T(2,128)S(1)}, f32[2,256]{1,0:T(2,128)}, u32[]{:S(2)}) copy-start(f32[2,256]{1,0:T(2,128)} %norm_ref.1) | copy-start | bytes 6148
  18.7 0.7 %copy-start.6 = (f32[2,8]{1,0:T(2,128)S(1)}, f32[2,8]{1,0:T(2,128)}, u32[]{:S(2)}) copy-start(f32[2,8]{1,0:T(2,128)} %bias_ref.1) | copy-start | bytes 196
  19.4 0.7 %copy-start.7 = (f32[2,8]{1,0:T(2,128)S(1)}, f32[2,8]{1,0:T(2,128)}, u32[]{:S(2)}) copy-start(f32[2,8]{1,0:T(2,128)} %rate_ref.1) | copy-start | bytes 196

commit v6 on v5

--- a/solution.py
+++ b/solution.py
@@ -50,6 +50,55 @@
         jnp.int32, (n, n), 1
     )
     return jnp.sum(jnp.where(square, jnp.broadcast_to(row, (n, n)), 0.0), 1, keepdims=True)
+
+
+def spread_kernel(field_ref, o_ref, taken, mixed, staged, in_sems, out_sems):
+    nx, ny, width = field_ref.shape
+    groups = in_sems.shape[0]
+    size = ny // groups
+    arriving = []
+    for g in range(groups):
+        part = pl.ds(size * g, size)
+        arriving.append(
+            pltpu.make_async_copy(field_ref.at[:, part, :], taken.at[:, part, :], in_sems.at[g])
+        )
+        arriving[-1].start()
+    leaving = []
+    for g in range(groups):
+        arriving[g].wait()
+        rows = slice(nx * size * g, nx * size * (g + 1))
+        for half in range(width // 128):
+            lanes = slice(128 * half, 128 * half + 128)
+            first = nx * ny * half
+            for x in range(nx):
+                plane = taken[x, size * g : size * g + size, lanes].astype(F32)
+                mixed[pl.ds(first + nx * size * g + x, size, stride=nx), :] = plane
+            staged[rows, lanes] = mixed[first + rows.start : first + rows.stop, :].astype(BF16)
+        part = pl.ds(nx * size * g, nx * size)
+        leaving.append(pltpu.make_async_copy(staged.at[part], o_ref.at[part], out_sems.at[g]))
+        leaving[-1].start()
+    for copy in leaving:
+        copy.wait()
+
+
+def spread(field):
+    nx, ny, width = field.shape
+    groups = 4
+    return pl.pallas_call(
+        spread_kernel,
+        out_shape=jax.ShapeDtypeStruct((ny * nx, width), BF16),
+        in_specs=[pl.BlockSpec(memory_space=pl.ANY)],
+        out_specs=pl.BlockSpec(memory_space=pl.ANY),
+        scratch_shapes=[
+            pltpu.VMEM(field.shape, BF16),
+            pltpu.VMEM((ny * nx * width // 128, 128), F32),
+            pltpu.VMEM((ny * nx, width), BF16),
+            pltpu.SemaphoreType.DMA((groups,)),
+            pltpu.SemaphoreType.DMA((groups,)),
+        ],
+        compiler_params=pltpu.CompilerParams(vmem_limit_bytes=62 * 1024 * 1024),
+        name="spread_field",
+    )(field)
 
 
 def prepare_kernel(
@@ -65,13 +114,15 @@
     out_ref,
     small_ref,
 ):
-    base = 2 * INNER + 2 * ORDER
+    base = 2 * HEADS + 2 * ORDER
     for layer in range(2):
-        weights_ref[layer, : 2 * INNER, :] = jnp.transpose(inner_ref[layer] * 0.5)
-        weights_ref[layer, 2 * INNER : base, :] = jnp.transpose(state_ref[layer])
-        weights_ref[layer, base:, :] = jnp.concatenate(
+        weights_ref[layer, : 2 * HEADS, :] = jnp.concatenate(
             [step_ref[layer], jnp.zeros_like(step_ref[layer])], 0
         )
+        weights_ref[layer, 2 * HEADS : base, :] = jnp.transpose(state_ref[layer])
+        inner = jnp.transpose(inner_ref[layer] * 0.5)
+        weights_ref[layer, base : base + INNER, :] = inner[INNER:]
+        weights_ref[layer, base + INNER :, :] = inner[:INNER]
         row = slice(layer, layer + 1)
         gain = jnp.transpose(jnp.broadcast_to(gain_ref[row, :], (CHUNK, INNER)))
         out_ref[layer] = (
@@ -105,13 +156,29 @@
 
 
 def layer_kernel(
-    layer, lines, interleaved, x_ref, weights_ref, out_w_ref, small_ref, o_ref, mixed_ref
+    layer, lines, grid, x_ref, weights_ref, out_w_ref, small_ref, o_ref, mixed_ref, sorted_ref
 ):
+    interleaved = lines > 1
     tokens, width = x_ref.shape
     chunks = tokens // CHUNK
     per_line = chunks // lines
     h = x_ref[...].astype(F32)
-    if interleaved:
+    if not interleaved:
+        gx, gy = grid
+        pair = tokens // (gx * gy)
+        for part in range(width // 128):
+            first = part * tokens
+            mixed_ref[first : first + tokens, :] = h[:, 128 * part : 128 * part + 128]
+            for b in range(gy):
+                for l in range(pair):
+                    source = pl.ds(first + b * pair + l, gx, stride=gy * pair)
+                    target = pl.ds(first + b * gx * pair + l, gx, stride=pair)
+                    sorted_ref[target, :] = mixed_ref[source, :]
+        h = jnp.concatenate(
+            [sorted_ref[part * tokens : part * tokens + tokens, :] for part in range(width // 128)],
+            1,
+        )
+    else:
         h = jnp.concatenate(
             [
                 h[8 * (lines * g + l) : 8 * (lines * g + l) + 8]
@@ -124,12 +191,13 @@
     normed = (h * scale * small_ref[layer, 2 * HEADS : 2 * HEADS + 1, : h.shape[1]]).astype(BF16)
 
     projected = dot(weights_ref[layer], normed, ((1,), (1,)))
-    gates = projected[:INNER]
-    inputs = silu_of_half(projected[INNER : 2 * INNER]).astype(BF16)
-    base = 2 * INNER
+    raw_steps = projected[:HEADS]
+    base = 2 * HEADS
     enter = projected[base : base + ORDER].astype(BF16)
     leave = projected[base + ORDER : base + 2 * ORDER].astype(BF16)
-    raw_steps = projected[base + 2 * ORDER : base + 2 * ORDER + HEADS]
+    base += 2 * ORDER
+    inputs = silu_of_half(projected[base : base + INNER]).astype(BF16)
+    gates = projected[base + INNER :]
     raw_steps = raw_steps + small_ref[layer, :HEADS, :]
     steps = jnp.maximum(raw_steps, 0.0) + jnp.log1p(jnp.exp(-jnp.abs(raw_steps)))
     decay = -steps * small_ref[layer, HEADS : 2 * HEADS, :]
@@ -263,13 +331,13 @@
             o_ref[:, span(part)] = mixed_ref[part * tokens : (part + 1) * tokens, :].astype(BF16)
 
 
-def mix(x, layer, lines, interleaved, weights):
+def mix(x, layer, lines, grid, weights):
     return pl.pallas_call(
-        functools.partial(layer_kernel, layer, lines, interleaved),
+        functools.partial(layer_kernel, layer, lines, grid),
         out_shape=jax.ShapeDtypeStruct(x.shape, BF16),
         in_specs=[pl.BlockSpec(memory_space=pltpu.VMEM)] * 4,
         out_specs=pl.BlockSpec(memory_space=pltpu.VMEM),
-        scratch_shapes=[pltpu.VMEM((x.size // 128, 128), F32)],
+        scratch_shapes=[pltpu.VMEM((x.size // 128, 128), F32)] * 2,
         compiler_params=pltpu.CompilerParams(vmem_limit_bytes=32 * 1024 * 1024),
         name=f"mix_layer_{layer}",
     )(x, *weights)
@@ -277,16 +345,16 @@
 
 def on_device(gx, gy, field, *weights):
     nx, ny, width = field.shape
+    lines = ny // gx
+    tokens = nx * ny
     weights = prepare(*weights)
-    lines = ny // gx
-    sent = jnp.swapaxes(field, 0, 1).reshape(gx, lines * nx, width)
-    taken = lax.all_to_all(sent, "gx", 0, 0, tiled=True).reshape(gx * nx * lines, width)
-    stream = mix(taken, 0, lines, True, weights)
+    sent = spread(field).reshape(gx, lines * nx, width)
+    taken = lax.all_to_all(sent, "gx", 0, 0, tiled=True).reshape(tokens, width)
+    stream = mix(taken, 0, lines, (gx, gy), weights)
     taken = lax.all_to_all(
         stream.reshape(gx * nx, lines, width), ("gx", "gy"), 0, 0, tiled=True
     )
-    taken = jnp.swapaxes(taken.reshape(gx, gy, lines, width), 0, 1)
-    stream = mix(taken.reshape(gy * gx * lines, width), 1, 1, False, weights)
+    stream = mix(taken.reshape(tokens, width), 1, 1, (gx, gy), weights)
     return lax.all_to_all(stream.reshape(gy, ny, width), "gy", 0, 0, tiled=True)
 
 

time: 66.3 us -> 65.8 us (level)
  local copies, waits for them, and re-layouts: 8.46 us -> 6.27 us
  Pallas kernels: 5.36 us -> 7.02 us
    unnamed x18 -> x17, local copies, waits for them, and re-layouts: 7.96 us -> 6.07 us
    pallas_call x2 -> x3, Pallas kernels: 4.8 us -> 6.46 us  [the longest x2 4.71 us: mix(): pl.pallas_call(functools.partial(layer_kernel, layer, lines, grid), out_s...]
where the time goes in v6:
time: 65.8 us; the launch traced here: 65.4 us
  blocking collectives  32.3 us (49%)
  starting transfers between devices  12.8 us (19%)
  Pallas kernels  7.02 us (11%)
  waiting for transfers between devices  6.99 us (11%)
  local copies, waits for them, and re-layouts  6.27 us (10%)
    all_to_all x1, blocking collectives, on_device(): lax.all_to_all(stream.reshape(gx * nx, lines, width), ('gx', 'gy'), 0, 0,...  21.8 us
    all_to_all x1, starting transfers between devices, on_device(): taken = lax.all_to_all(sent, 'gx', 0, 0, tiled=True).reshape(tokens, width)  12.8 us
    all_to_all x1, blocking collectives, on_device(): return lax.all_to_all(stream.reshape(gy, ny, width), 'gy', 0, 0, tiled=True)  10.5 us
    all_to_all x1, waiting for transfers between devices, on_device(): taken = lax.all_to_all(sent, 'gx', 0, 0, tiled=True).reshape(tokens, width)  6.99 us
    unnamed x17, local copies, waits for them, and re-layouts  6.07 us
    pallas_call x2, Pallas kernels, mix(): pl.pallas_call(functools.partial(layer_kernel, layer, lines, grid), out_s...  4.71 us
    pallas_call x1, Pallas kernels, spread(): pl.pallas_call(spread_kernel, out_shape=jax.ShapeDtypeStruct((ny * nx, wi...  1.75 us
  transfers between devices with their start and end apart: 1, of which 1 were waited for; matrix products, arithmetic and copies ran while one was open for 0% of the time, Pallas kernels for 1%

profile of v6, /device:TPU:1, one launch (start us, length us, event | category | flops | bytes accessed | tf_op | source)
XLA Modules:
  0.0 65.4 jit_solution(409907662679301708)
XLA Ops:
  0.0 0.0 copy-start
  0.0 1.8 %spread_field.1 = bf16[512,256]{1,0:T(8,128)(2,1)} custom-call(bf16[8,64,256]{2,1,0:T(8,128)(2,1)} %field_ref.1), custom_call_target="tpu_custom_call" | custom-call | tf_op jit(solution)/shard_map/spread_field/pallas_call | solution.py:87
  1.8 12.8 %all-to-all-start = ((bf16[32,16,256]{2,1,0:T(8,128)(2,1)}), bf16[32,16,256]{2,1,0:T(8,128)(2,1)S(1)}, u32[]{:S(2)}, u32[]{:S(2)}) async-start(bf16[32,16,256]{2,1,0:T(8,128)(2,1)} %bitcast.7), calls=%async_computation | async-start | bytes 524288 | tf_op jit(solution)/shard_map/all_to_all | solution.py:352
  14.5 0.0 copy-done
  14.5 0.0 copy-start.1
  14.6 1.0 %copy-done.1 = bf16[2,512,256]{2,1,0:T(8,128)(2,1)S(1)} copy-done((bf16[2,512,256]{2,1,0:T(8,128)(2,1)S(1)}, bf16[2,512,256]{2,1,0:T(8,128)(2,1)}, u32[]{:S(2)}) %copy-start.1) | copy-done | bytes 524312
  15.6 0.0 copy-start.2
  15.6 0.9 %copy-done.2 = bf16[2,256,128]{2,1,0:T(8,128)(2,1)S(1)} copy-done((bf16[2,256,128]{2,1,0:T(8,128)(2,1)S(1)}, bf16[2,256,128]{2,1,0:T(8,128)(2,1)}, u32[]{:S(2)}) %copy-start.2) | copy-done | bytes 131096
  16.5 0.0 copy-start.3
  16.5 0.7 %copy-done.3 = bf16[2,256,8]{1,2,0:T(8,128)(2,1)S(1)} copy-done((bf16[2,256,8]{1,2,0:T(8,128)(2,1)S(1)}, bf16[2,256,8]{1,2,0:T(8,128)(2,1)}, u32[]{:S(2)}) %copy-start.3) | copy-done | bytes 8216
  17.2 0.0 copy-start.4
  17.2 0.7 %copy-done.4 = f32[2,512]{1,0:T(2,128)S(1)} copy-done((f32[2,512]{1,0:T(2,128)S(1)}, f32[2,512]{1,0:T(2,128)}, u32[]{:S(2)}) %copy-start.4) | copy-done | bytes 4120
  17.9 0.0 copy-start.5
  17.9 0.7 %copy-done.5 = f32[2,256]{1,0:T(2,128)S(1)} copy-done((f32[2,256]{1,0:T(2,128)S(1)}, f32[2,256]{1,0:T(2,128)}, u32[]{:S(2)}) %copy-start.5) | copy-done | bytes 2072
  18.6 0.0 copy-start.6
  18.6 0.7 %copy-done.6 = f32[2,8]{1,0:T(2,128)S(1)} copy-done((f32[2,8]{1,0:T(2,128)S(1)}, f32[2,8]{1,0:T(2,128)}, u32[]{:S(2)}) %copy-start.6) | copy-done | bytes 88
  19.2 0.0 copy-start.7
  19.2 0.7 %copy-done.7 = f32[2,8]{1,0:T(2,128)S(1)} copy-done((f32[2,8]{1,0:T(2,128)S(1)}, f32[2,8]{1,0:T(2,128)}, u32[]{:S(2)}) %copy-start.7) | copy-done | bytes 88
  19.9 0.6 prepare_weights.1
  20.5 7.0 %all-to-all-done = bf16[32,16,256]{2,1,0:T(8,128)(2,1)S(1)} async-done(((bf16[32,16,256]{2,1,0:T(8,128)(2,1)}), bf16[32,16,256]{2,1,0:T(8,128)(2,1)S(1)}, u32[]{:S(2)}, u32[]{:S(2)}) %all-to-all-start) | async-done | bytes 262176 | tf_op jit(solution)/shard_map/all_to_all | solution.py:352
  27.5 2.3 %mix_layer_0.1 = bf16[512,256]{1,0:T(8,128)(2,1)S(1)} custom-call(bf16[512,256]{1,0:T(8,128)(2,1)S(1)} %bitcast.4, bf16[2,1168,256]{2,1,0:T(8,128)(2,1)S(1)} %get-tuple-element.8.weights_ref, bf16[2,512,256]{2,1,0:T(8,128)(2,1)S(1)} %get-tuple-element.9.out_w_ref, f32[2,24,512]{2,1,0:T(8,128)S(1)} %get-tuple-element.10.small_ref), custom_call_target="tpu_custom_call" | custom-call | tf_op jit(solution)/shard_map/mix_layer_0/pallas_call | solution.py:335
  29.8 0.1 reshape.17
  29.9 21.8 %all_to_all.15 = bf16[256,2,256]{2,1,0:T(2,128)(2,1)S(1)} all-to-all(bf16[256,2,256]{2,1,0:T(2,128)(2,1)S(1)} %reshape.17), channel_id=1, replica_groups=mesh['gx'=32,'gy'=8] {'gx','gy'}, dimensions={0} | all-to-all | bytes 524288 | tf_op jit(solution)/shard_map/all_to_all | solution.py:354
  51.6 0.1 reshape.18.x_ref
  51.7 2.4 %mix_layer_1.1 = bf16[512,256]{1,0:T(8,128)(2,1)S(1)} custom-call(bf16[512,256]{1,0:T(8,128)(2,1)S(1)} %reshape.18.x_ref, bf16[2,1168,256]{2,1,0:T(8,128)(2,1)S(1)} %get-tuple-element.8.weights_ref, bf16[2,512,256]{2,1,0:T(8,128)(2,1)S(1)} %get-tuple-element.9.out_w_ref, f32[2,24,512]{2,1,0:T(8,128)S(1)} %get-tuple-element.10.small_ref), custom_call_target="tpu_custom_call" | custom-call | tf_op jit(solution)/shard_map/mix_layer_1/pallas_call | solution.py:335
  54.2 10.5 %all_to_all.16 = bf16[8,64,256]{2,1,0:T(8,128)(2,1)S(1)} all-to-all(bf16[8,64,256]{2,1,0:T(8,128)(2,1)S(1)} %bitcast.5), channel_id=1, replica_groups=mesh['gx'=32,'gy'=8] {'gy'}, dimensions={0} | all-to-all | bytes 524288 | tf_op jit(solution)/shard_map/all_to_all | solution.py:358
  64.7 0.7 %copy.11 = bf16[8,64,256]{2,1,0:T(8,128)(2,1)} copy(bf16[8,64,256]{2,1,0:T(8,128)(2,1)S(1)} %all_to_all.16) | data formatting | bytes 524288
Async XLA Ops:
  0.0 14.5 %copy-start = (bf16[2,256,1024]{2,1,0:T(8,128)(2,1)S(1)}, bf16[2,256,1024]{2,1,0:T(8,128)(2,1)}, u32[]{:S(2)}) copy-start(bf16[2,256,1024]{2,1,0:T(8,128)(2,1)} %inner_ref.1) | copy-start | bytes 3145732
  1.8 25.7 %all-to-all-start = ((bf16[32,16,256]{2,1,0:T(8,128)(2,1)}), bf16[32,16,256]{2,1,0:T(8,128)(2,1)S(1)}, u32[]{:S(2)}, u32[]{:S(2)}) async-start(bf16[32,16,256]{2,1,0:T(8,128)(2,1)} %bitcast.7), calls=%async_computation | async-start | bytes 524288 | tf_op jit(solution)/shard_map/all_to_all | solution.py:352
  14.5 1.0 %copy-start.1 = (bf16[2,512,256]{2,1,0:T(8,128)(2,1)S(1)}, bf16[2,512,256]{2,1,0:T(8,128)(2,1)}, u32[]{:S(2)}) copy-start(bf16[2,512,256]{2,1,0:T(8,128)(2,1)} %out_w_ref.1) | copy-start | bytes 1572868
  15.6 0.9 %copy-start.2 = (bf16[2,256,128]{2,1,0:T(8,128)(2,1)S(1)}, bf16[2,256,128]{2,1,0:T(8,128)(2,1)}, u32[]{:S(2)}) copy-start(bf16[2,256,128]{2,1,0:T(8,128)(2,1)} %state_ref.1) | copy-start | bytes 393220
  16.5 0.7 %copy-start.3 = (bf16[2,256,8]{1,2,0:T(8,128)(2,1)S(1)}, bf16[2,256,8]{1,2,0:T(8,128)(2,1)}, u32[]{:S(2)}) copy-start(bf16[2,256,8]{1,2,0:T(8,128)(2,1)} %param.13) | copy-start | bytes 24580
  17.2 0.7 %copy-start.4 = (f32[2,512]{1,0:T(2,128)S(1)}, f32[2,512]{1,0:T(2,128)}, u32[]{:S(2)}) copy-start(f32[2,512]{1,0:T(2,128)} %gain_ref.1) | copy-start | bytes 12292
  17.9 0.7 %copy-start.5 = (f32[2,256]{1,0:T(2,128)S(1)}, f32[2,256]{1,0:T(2,128)}, u32[]{:S(2)}) copy-start(f32[2,256]{1,0:T(2,128)} %norm_ref.1) | copy-start | bytes 6148
  18.6 0.7 %copy-start.6 = (f32[2,8]{1,0:T(2,128)S(1)}, f32[2,8]{1,0:T(2,128)}, u32[]{:S(2)}) copy-start(f32[2,8]{1,0:T(2,128)} %bias_ref.1) | copy-start | bytes 196
  19.2 0.7 %copy-start.7 = (f32[2,8]{1,0:T(2,128)S(1)}, f32[2,8]{1,0:T(2,128)}, u32[]{:S(2)}) copy-start(f32[2,8]{1,0:T(2,128)} %rate_ref.1) | copy-start | bytes 196

commit v7 on v6

--- a/solution.py
+++ b/solution.py
@@ -159,24 +159,23 @@
     layer, lines, grid, x_ref, weights_ref, out_w_ref, small_ref, o_ref, mixed_ref, sorted_ref
 ):
     interleaved = lines > 1
-    tokens, width = x_ref.shape
+    width = weights_ref.shape[2]
+    parts = width // 128
+    tokens = x_ref.size // width
     chunks = tokens // CHUNK
     per_line = chunks // lines
     h = x_ref[...].astype(F32)
     if not interleaved:
         gx, gy = grid
         pair = tokens // (gx * gy)
-        for part in range(width // 128):
-            first = part * tokens
-            mixed_ref[first : first + tokens, :] = h[:, 128 * part : 128 * part + 128]
-            for b in range(gy):
-                for l in range(pair):
-                    source = pl.ds(first + b * pair + l, gx, stride=gy * pair)
-                    target = pl.ds(first + b * gx * pair + l, gx, stride=pair)
-                    sorted_ref[target, :] = mixed_ref[source, :]
+        mixed_ref[...] = h
+        for part in range(parts):
+            for l in range(pair):
+                found = mixed_ref[pl.ds(l * parts + part, gx * gy, stride=pair * parts), :]
+                found = jnp.swapaxes(found.reshape(gx, gy, 128), 0, 1).reshape(gx * gy, 128)
+                sorted_ref[pl.ds(part * tokens + l, gx * gy, stride=pair), :] = found
         h = jnp.concatenate(
-            [sorted_ref[part * tokens : part * tokens + tokens, :] for part in range(width // 128)],
-            1,
+            [sorted_ref[part * tokens : part * tokens + tokens, :] for part in range(parts)], 1
         )
     else:
         h = jnp.concatenate(
@@ -190,14 +189,14 @@
     scale = lax.rsqrt(jnp.mean(h * h, axis=1, keepdims=True) + EPSILON)
     normed = (h * scale * small_ref[layer, 2 * HEADS : 2 * HEADS + 1, : h.shape[1]]).astype(BF16)
 
-    projected = dot(weights_ref[layer], normed, ((1,), (1,)))
+    rows = weights_ref.shape[1] - INNER
+    projected = dot(weights_ref[layer, :rows, :], normed, ((1,), (1,)))
     raw_steps = projected[:HEADS]
     base = 2 * HEADS
     enter = projected[base : base + ORDER].astype(BF16)
     leave = projected[base + ORDER : base + 2 * ORDER].astype(BF16)
     base += 2 * ORDER
     inputs = silu_of_half(projected[base : base + INNER]).astype(BF16)
-    gates = projected[base + INNER :]
     raw_steps = raw_steps + small_ref[layer, :HEADS, :]
     steps = jnp.maximum(raw_steps, 0.0) + jnp.log1p(jnp.exp(-jnp.abs(raw_steps)))
     decay = -steps * small_ref[layer, HEADS : 2 * HEADS, :]
@@ -208,6 +207,7 @@
     second = rest.astype(BF16)
     third = (rest - second.astype(F32)).astype(BF16)
     summed = dot(jnp.concatenate([first, second, third], 0), sum_matrix())
+    gates = dot(weights_ref[layer, rows:, :], normed, ((1,), (1,)))
     n = HEADS * chunks
     summed = summed[:n] + summed[n : 2 * n] + summed[2 * n :]
     mid = summed[:, :CHUNK]
@@ -321,20 +321,19 @@
         result = h[span(k)] + dot(rounded[k], out_w_ref[layer], ((0,), (0,)))
         if interleaved:
             line, first_x = k // per_line, CHUNK * (k % per_line)
-            for part in range(width // 128):
-                first = part * tokens + lines * first_x + line
-                mixed_ref[pl.ds(first, CHUNK, stride=lines), :] = result[:, span(part)]
+            for part in range(parts):
+                target = pl.ds((lines * first_x + line) * parts + part, CHUNK, stride=lines * parts)
+                mixed_ref[target, :] = result[:, span(part)]
         else:
             o_ref[span(k), :] = result.astype(BF16)
     if interleaved:
-        for part in range(width // 128):
-            o_ref[:, span(part)] = mixed_ref[part * tokens : (part + 1) * tokens, :].astype(BF16)
-
-
-def mix(x, layer, lines, grid, weights):
+        o_ref[...] = mixed_ref[...].astype(BF16)
+
+
+def mix(x, layer, lines, grid, shape, weights):
     return pl.pallas_call(
         functools.partial(layer_kernel, layer, lines, grid),
-        out_shape=jax.ShapeDtypeStruct(x.shape, BF16),
+        out_shape=jax.ShapeDtypeStruct(shape, BF16),
         in_specs=[pl.BlockSpec(memory_space=pltpu.VMEM)] * 4,
         out_specs=pl.BlockSpec(memory_space=pltpu.VMEM),
         scratch_shapes=[pltpu.VMEM((x.size // 128, 128), F32)] * 2,
@@ -350,11 +349,11 @@
     weights = prepare(*weights)
     sent = spread(field).reshape(gx, lines * nx, width)
     taken = lax.all_to_all(sent, "gx", 0, 0, tiled=True).reshape(tokens, width)
-    stream = mix(taken, 0, lines, (gx, gy), weights)
+    stream = mix(taken, 0, lines, (gx, gy), (2 * tokens, width // 2), weights)
     taken = lax.all_to_all(
-        stream.reshape(gx * nx, lines, width), ("gx", "gy"), 0, 0, tiled=True
-    )
-    stream = mix(taken.reshape(tokens, width), 1, 1, (gx, gy), weights)
+        stream.reshape(gx * nx, -1, width // 2), ("gx", "gy"), 0, 0, tiled=True
+    )
+    stream = mix(taken.reshape(stream.shape), 1, 1, (gx, gy), (tokens, width), weights)
     return lax.all_to_all(stream.reshape(gy, ny, width), "gy", 0, 0, tiled=True)
 
 

time: 65.8 us -> 65.4 us (level)
  no operation moved by 1% of the time
where the time goes in v7:
time: 65.4 us; the launch traced here: 64.9 us
  blocking collectives  32.3 us (49%)
  starting transfers between devices  12.8 us (20%)
  waiting for transfers between devices  6.99 us (11%)
  Pallas kernels  6.8 us (10%)
  local copies, waits for them, and re-layouts  6.07 us (9%)
    all_to_all x1, blocking collectives, on_device(): lax.all_to_all(stream.reshape(gx * nx, -1, width // 2), ('gx', 'gy'), 0,...  21.8 us
    all_to_all x1, starting transfers between devices, on_device(): taken = lax.all_to_all(sent, 'gx', 0, 0, tiled=True).reshape(tokens, width)  12.8 us
    all_to_all x1, blocking collectives, on_device(): return lax.all_to_all(stream.reshape(gy, ny, width), 'gy', 0, 0, tiled=True)  10.5 us
    all_to_all x1, waiting for transfers between devices, on_device(): taken = lax.all_to_all(sent, 'gx', 0, 0, tiled=True).reshape(tokens, width)  6.99 us
    unnamed x17, local copies, waits for them, and re-layouts  6.07 us
    pallas_call x2, Pallas kernels, mix(): pl.pallas_call(functools.partial(layer_kernel, layer, lines, grid), out_s...  4.49 us
    pallas_call x1, Pallas kernels, spread(): pl.pallas_call(spread_kernel, out_shape=jax.ShapeDtypeStruct((ny * nx, wi...  1.75 us
  transfers between devices with their start and end apart: 1, of which 1 were waited for; matrix products, arithmetic and copies ran while one was open for 0% of the time, Pallas kernels for 1%

profile of v7, /device:TPU:1, one launch (start us, length us, event | category | flops | bytes accessed | tf_op | source)
XLA Modules:
  0.0 64.9 jit_solution(2553403302060803988)
XLA Ops:
  0.0 0.0 copy-start
  0.0 1.8 %spread_field.1 = bf16[512,256]{1,0:T(8,128)(2,1)} custom-call(bf16[8,64,256]{2,1,0:T(8,128)(2,1)} %field_ref.1), custom_call_target="tpu_custom_call" | custom-call | tf_op jit(solution)/shard_map/spread_field/pallas_call | solution.py:87
  1.8 12.8 %all-to-all-start = ((bf16[32,16,256]{2,1,0:T(8,128)(2,1)}), bf16[32,16,256]{2,1,0:T(8,128)(2,1)S(1)}, u32[]{:S(2)}, u32[]{:S(2)}) async-start(bf16[32,16,256]{2,1,0:T(8,128)(2,1)} %bitcast.11), calls=%async_computation | async-start | bytes 524288 | tf_op jit(solution)/shard_map/all_to_all | solution.py:351
  14.5 0.0 copy-done
  14.5 0.0 copy-start.1
  14.6 1.0 %copy-done.1 = bf16[2,512,256]{2,1,0:T(8,128)(2,1)S(1)} copy-done((bf16[2,512,256]{2,1,0:T(8,128)(2,1)S(1)}, bf16[2,512,256]{2,1,0:T(8,128)(2,1)}, u32[]{:S(2)}) %copy-start.1) | copy-done | bytes 524312
  15.6 0.0 copy-start.2
  15.6 0.9 %copy-done.2 = bf16[2,256,128]{2,1,0:T(8,128)(2,1)S(1)} copy-done((bf16[2,256,128]{2,1,0:T(8,128)(2,1)S(1)}, bf16[2,256,128]{2,1,0:T(8,128)(2,1)}, u32[]{:S(2)}) %copy-start.2) | copy-done | bytes 131096
  16.5 0.0 copy-start.3
  16.5 0.7 %copy-done.3 = bf16[2,256,8]{1,2,0:T(8,128)(2,1)S(1)} copy-done((bf16[2,256,8]{1,2,0:T(8,128)(2,1)S(1)}, bf16[2,256,8]{1,2,0:T(8,128)(2,1)}, u32[]{:S(2)}) %copy-start.3) | copy-done | bytes 8216
  17.2 0.0 copy-start.4
  17.2 0.7 %copy-done.4 = f32[2,512]{1,0:T(2,128)S(1)} copy-done((f32[2,512]{1,0:T(2,128)S(1)}, f32[2,512]{1,0:T(2,128)}, u32[]{:S(2)}) %copy-start.4) | copy-done | bytes 4120
  17.9 0.0 copy-start.5
  17.9 0.7 %copy-done.5 = f32[2,256]{1,0:T(2,128)S(1)} copy-done((f32[2,256]{1,0:T(2,128)S(1)}, f32[2,256]{1,0:T(2,128)}, u32[]{:S(2)}) %copy-start.5) | copy-done | bytes 2072
  18.6 0.0 copy-start.6
  18.6 0.7 %copy-done.6 = f32[2,8]{1,0:T(2,128)S(1)} copy-done((f32[2,8]{1,0:T(2,128)S(1)}, f32[2,8]{1,0:T(2,128)}, u32[]{:S(2)}) %copy-start.6) | copy-done | bytes 88
  19.2 0.0 copy-start.7
  19.2 0.7 %copy-done.7 = f32[2,8]{1,0:T(2,128)S(1)} copy-done((f32[2,8]{1,0:T(2,128)S(1)}, f32[2,8]{1,0:T(2,128)}, u32[]{:S(2)}) %copy-start.7) | copy-done | bytes 88
  19.9 0.6 prepare_weights.1
  20.5 7.0 %all-to-all-done = bf16[32,16,256]{2,1,0:T(8,128)(2,1)S(1)} async-done(((bf16[32,16,256]{2,1,0:T(8,128)(2,1)}), bf16[32,16,256]{2,1,0:T(8,128)(2,1)S(1)}, u32[]{:S(2)}, u32[]{:S(2)}) %all-to-all-start) | async-done | bytes 262176 | tf_op jit(solution)/shard_map/all_to_all | solution.py:351
  27.5 2.2 %mix_layer_0.1 = bf16[1024,128]{1,0:T(8,128)(2,1)S(1)} custom-call(bf16[512,256]{1,0:T(8,128)(2,1)S(1)} %bitcast.6, bf16[2,1168,256]{2,1,0:T(8,128)(2,1)S(1)} %get-tuple-element.8.weights_ref, bf16[2,512,256]{2,1,0:T(8,128)(2,1)S(1)} %get-tuple-element.9.out_w_ref, f32[2,24,512]{2,1,0:T(8,128)S(1)} %get-tuple-element.10.small_ref), custom_call_target="tpu_custom_call" | custom-call | tf_op jit(solution)/shard_map/mix_layer_0/pallas_call | solution.py:334
  29.7 21.8 %all_to_all.15 = bf16[256,4,128]{2,1,0:T(4,128)(2,1)S(1)} all-to-all(bf16[256,4,128]{2,1,0:T(4,128)(2,1)S(1)} %bitcast.9), channel_id=1, replica_groups=mesh['gx'=32,'gy'=8] {'gx','gy'}, dimensions={0} | all-to-all | bytes 524288 | tf_op jit(solution)/shard_map/all_to_all | solution.py:353
  51.4 2.3 %mix_layer_1.1 = bf16[512,256]{1,0:T(8,128)(2,1)S(1)} custom-call(bf16[1024,128]{1,0:T(8,128)(2,1)S(1)} %bitcast.7, bf16[2,1168,256]{2,1,0:T(8,128)(2,1)S(1)} %get-tuple-element.8.weights_ref, bf16[2,512,256]{2,1,0:T(8,128)(2,1)S(1)} %get-tuple-element.9.out_w_ref, f32[2,24,512]{2,1,0:T(8,128)S(1)} %get-tuple-element.10.small_ref), custom_call_target="tpu_custom_call" | custom-call | tf_op jit(solution)/shard_map/mix_layer_1/pallas_call | solution.py:334
  53.7 10.5 %all_to_all.16 = bf16[8,64,256]{2,1,0:T(8,128)(2,1)S(1)} all-to-all(bf16[8,64,256]{2,1,0:T(8,128)(2,1)S(1)} %bitcast.8), channel_id=1, replica_groups=mesh['gx'=32,'gy'=8] {'gy'}, dimensions={0} | all-to-all | bytes 524288 | tf_op jit(solution)/shard_map/all_to_all | solution.py:357
  64.2 0.7 %copy.11 = bf16[8,64,256]{2,1,0:T(8,128)(2,1)} copy(bf16[8,64,256]{2,1,0:T(8,128)(2,1)S(1)} %all_to_all.16) | data formatting | bytes 524288
Async XLA Ops:
  0.0 14.5 %copy-start = (bf16[2,256,1024]{2,1,0:T(8,128)(2,1)S(1)}, bf16[2,256,1024]{2,1,0:T(8,128)(2,1)}, u32[]{:S(2)}) copy-start(bf16[2,256,1024]{2,1,0:T(8,128)(2,1)} %inner_ref.1) | copy-start | bytes 3145732
  1.8 25.7 %all-to-all-start = ((bf16[32,16,256]{2,1,0:T(8,128)(2,1)}), bf16[32,16,256]{2,1,0:T(8,128)(2,1)S(1)}, u32[]{:S(2)}, u32[]{:S(2)}) async-start(bf16[32,16,256]{2,1,0:T(8,128)(2,1)} %bitcast.11), calls=%async_computation | async-start | bytes 524288 | tf_op jit(solution)/shard_map/all_to_all | solution.py:351
  14.5 1.0 %copy-start.1 = (bf16[2,512,256]{2,1,0:T(8,128)(2,1)S(1)}, bf16[2,512,256]{2,1,0:T(8,128)(2,1)}, u32[]{:S(2)}) copy-start(bf16[2,512,256]{2,1,0:T(8,128)(2,1)} %out_w_ref.1) | copy-start | bytes 1572868
  15.6 0.9 %copy-start.2 = (bf16[2,256,128]{2,1,0:T(8,128)(2,1)S(1)}, bf16[2,256,128]{2,1,0:T(8,128)(2,1)}, u32[]{:S(2)}) copy-start(bf16[2,256,128]{2,1,0:T(8,128)(2,1)} %state_ref.1) | copy-start | bytes 393220
  16.5 0.7 %copy-start.3 = (bf16[2,256,8]{1,2,0:T(8,128)(2,1)S(1)}, bf16[2,256,8]{1,2,0:T(8,128)(2,1)}, u32[]{:S(2)}) copy-start(bf16[2,256,8]{1,2,0:T(8,128)(2,1)} %param.13) | copy-start | bytes 24580
  17.2 0.7 %copy-start.4 = (f32[2,512]{1,0:T(2,128)S(1)}, f32[2,512]{1,0:T(2,128)}, u32[]{:S(2)}) copy-start(f32[2,512]{1,0:T(2,128)} %gain_ref.1) | copy-start | bytes 12292
  17.9 0.7 %copy-start.5 = (f32[2,256]{1,0:T(2,128)S(1)}, f32[2,256]{1,0:T(2,128)}, u32[]{:S(2)}) copy-start(f32[2,256]{1,0:T(2,128)} %norm_ref.1) | copy-start | bytes 6148
  18.6 0.7 %copy-start.6 = (f32[2,8]{1,0:T(2,128)S(1)}, f32[2,8]{1,0:T(2,128)}, u32[]{:S(2)}) copy-start(f32[2,8]{1,0:T(2,128)} %bias_ref.1) | copy-start | bytes 196
  19.2 0.7 %copy-start.7 = (f32[2,8]{1,0:T(2,128)S(1)}, f32[2,8]{1,0:T(2,128)}, u32[]{:S(2)}) copy-start(f32[2,8]{1,0:T(2,128)} %rate_ref.1) | copy-start | bytes 196

commit v8 on v7

--- a/solution.py
+++ b/solution.py
@@ -37,6 +37,10 @@
 
 def silu_of_half(v):
     return v + v * jnp.tanh(v)
+
+
+def backwards(v):
+    return jnp.concatenate([v[i : i + 1] for i in reversed(range(v.shape[0]))], 0)
 
 
 def rows16(row, rows):
@@ -172,7 +176,8 @@
         for part in range(parts):
             for l in range(pair):
                 found = mixed_ref[pl.ds(l * parts + part, gx * gy, stride=pair * parts), :]
-                found = jnp.swapaxes(found.reshape(gx, gy, 128), 0, 1).reshape(gx * gy, 128)
+                found = backwards(found.reshape(gx, gy, 128))
+                found = backwards(jnp.swapaxes(found, 0, 1)).reshape(gx * gy, 128)
                 sorted_ref[pl.ds(part * tokens + l, gx * gy, stride=pair), :] = found
         h = jnp.concatenate(
             [sorted_ref[part * tokens : part * tokens + tokens, :] for part in range(parts)], 1
@@ -182,7 +187,7 @@
             [
                 h[8 * (lines * g + l) : 8 * (lines * g + l) + 8]
                 for l in range(lines)
-                for g in range(tokens // (8 * lines))
+                for g in reversed(range(tokens // (8 * lines)))
             ],
             0,
         )
@@ -291,6 +296,7 @@
             joined[start + j] = jnp.where(ahead, states[j], mirror).astype(BF16)
 
     rounded = []
+    scales = []
     for k in range(chunks):
         left = jnp.concatenate([entered[k], joined[k]], 1)
         leave_k = leave[:, span(k)]
@@ -314,18 +320,24 @@
             both = dot(left[CHUNK * pair : CHUNK * pair + CHUNK], jnp.concatenate(rights, 1))
             mixed += [both[:SIZE, :CHUNK], both[SIZE:, CHUNK:]]
         gated = by_head(jnp.concatenate(mixed, 0), growth, k) * silu_of_half(gates[:, span(k)])
+        rounded.append(gated.astype(BF16))
         scale = lax.rsqrt(jnp.mean(gated * gated, axis=0, keepdims=True) + EPSILON)
-        rounded.append((gated * scale).astype(BF16))
+        scales.append(jnp.transpose(jnp.broadcast_to(scale, (CHUNK, CHUNK))))
 
     for k in range(chunks):
-        result = h[span(k)] + dot(rounded[k], out_w_ref[layer], ((0,), (0,)))
+        change = dot(rounded[k], out_w_ref[layer], ((0,), (0,)))
+        result = h[span(k)] + change * jnp.concatenate([scales[k]] * parts, 1)
         if interleaved:
             line, first_x = k // per_line, CHUNK * (k % per_line)
             for part in range(parts):
                 target = pl.ds((lines * first_x + line) * parts + part, CHUNK, stride=lines * parts)
                 mixed_ref[target, :] = result[:, span(part)]
         else:
-            o_ref[span(k), :] = result.astype(BF16)
+            result = result.astype(BF16)
+            size = tokens // gy
+            for b in range(CHUNK // size):
+                first = tokens - size * (k * (CHUNK // size) + b + 1)
+                o_ref[first : first + size, :] = result[size * b : size * b + size]
     if interleaved:
         o_ref[...] = mixed_ref[...].astype(BF16)
 
@@ -347,14 +359,25 @@
     lines = ny // gx
     tokens = nx * ny
     weights = prepare(*weights)
+    falling_x = [list(reversed(range(gx)))]
+    falling_y = [list(reversed(range(gy)))]
     sent = spread(field).reshape(gx, lines * nx, width)
-    taken = lax.all_to_all(sent, "gx", 0, 0, tiled=True).reshape(tokens, width)
+    taken = lax.all_to_all(sent, "gx", 0, 0, tiled=True, axis_index_groups=falling_x)
+    taken = taken.reshape(tokens, width)
     stream = mix(taken, 0, lines, (gx, gy), (2 * tokens, width // 2), weights)
+    owners = [[gy * (x // gy) + gy - 1 - x % gy for x in range(gx * nx)]]
     taken = lax.all_to_all(
-        stream.reshape(gx * nx, -1, width // 2), ("gx", "gy"), 0, 0, tiled=True
+        stream.reshape(gx * nx, -1, width // 2),
+        ("gx", "gy"),
+        0,
+        0,
+        tiled=True,
+        axis_index_groups=owners,
     )
     stream = mix(taken.reshape(stream.shape), 1, 1, (gx, gy), (tokens, width), weights)
-    return lax.all_to_all(stream.reshape(gy, ny, width), "gy", 0, 0, tiled=True)
+    return lax.all_to_all(
+        stream.reshape(gy, ny, width), "gy", 0, 0, tiled=True, axis_index_groups=falling_y
+    )
 
 
 def solution(mesh):

time: 65.4 us -> 64.4 us (0.985)
  waiting for transfers between devices: 6.99 us -> 2.62 us
  blocking collectives: 32.3 us -> 35.8 us
    all_to_all x1, blocking collectives: 21.8 us -> 26.9 us  [on_device(): lax.all_to_all(stream.reshape(gx * nx, -1, width // 2), ('gx', 'gy'), 0,...]
    all_to_all x1, waiting for transfers between devices: 6.99 us -> 2.62 us  [on_device(): lax.all_to_all(sent, 'gx', 0, 0, tiled=True, axis_index_groups=falling_x)]
    all_to_all x1, blocking collectives: 10.5 us -> 8.9 us  [on_device(): lax.all_to_all(stream.reshape(gy, ny, width), 'gy', 0, 0, tiled=True, axi...]
where the time goes in v8:
time: 64.4 us; the launch traced here: 64 us
  blocking collectives  35.8 us (56%)
  starting transfers between devices  12.8 us (20%)
  Pallas kernels  6.67 us (10%)
  local copies, waits for them, and re-layouts  6.07 us (9%)
  waiting for transfers between devices  2.62 us (4%)
    all_to_all x1, blocking collectives, on_device(): lax.all_to_all(stream.reshape(gx * nx, -1, width // 2), ('gx', 'gy'), 0,...  26.9 us
    all_to_all x1, starting transfers between devices, on_device(): lax.all_to_all(sent, 'gx', 0, 0, tiled=True, axis_index_groups=falling_x)  12.8 us
    all_to_all x1, blocking collectives, on_device(): lax.all_to_all(stream.reshape(gy, ny, width), 'gy', 0, 0, tiled=True, axi...  8.9 us
    unnamed x17, local copies, waits for them, and re-layouts  6.07 us
    pallas_call x2, Pallas kernels, mix(): pl.pallas_call(functools.partial(layer_kernel, layer, lines, grid), out_s...  4.37 us
    all_to_all x1, waiting for transfers between devices, on_device(): lax.all_to_all(sent, 'gx', 0, 0, tiled=True, axis_index_groups=falling_x)  2.62 us
    pallas_call x1, Pallas kernels, spread(): pl.pallas_call(spread_kernel, out_shape=jax.ShapeDtypeStruct((ny * nx, wi...  1.75 us
  transfers between devices with their start and end apart: 1, of which 1 were waited for; matrix products, arithmetic and copies ran while one was open for 0% of the time, Pallas kernels for 1%

profile of v8, /device:TPU:1, one launch (start us, length us, event | category | flops | bytes accessed | tf_op | source)
XLA Modules:
  0.0 64.0 jit_solution(17344730818429263786)
XLA Ops:
  0.0 0.0 copy-start
  0.0 1.8 %spread_field.1 = bf16[512,256]{1,0:T(8,128)(2,1)} custom-call(bf16[8,64,256]{2,1,0:T(8,128)(2,1)} %field_ref.1), custom_call_target="tpu_custom_call" | custom-call | tf_op jit(solution)/shard_map/spread_field/pallas_call | solution.py:91
  1.8 12.8 %all-to-all-start = ((bf16[32,16,256]{2,1,0:T(8,128)(2,1)}), bf16[32,16,256]{2,1,0:T(8,128)(2,1)S(1)}, u32[]{:S(2)}, u32[]{:S(2)}) async-start(bf16[32,16,256]{2,1,0:T(8,128)(2,1)} %bitcast.11), calls=%async_computation | async-start | bytes 524288 | tf_op jit(solution)/shard_map/all_to_all | solution.py:365
  14.5 0.0 copy-done
  14.6 0.0 copy-start.1
  14.6 1.0 %copy-done.1 = bf16[2,512,256]{2,1,0:T(8,128)(2,1)S(1)} copy-done((bf16[2,512,256]{2,1,0:T(8,128)(2,1)S(1)}, bf16[2,512,256]{2,1,0:T(8,128)(2,1)}, u32[]{:S(2)}) %copy-start.1) | copy-done | bytes 524312
  15.6 0.0 copy-start.2
  15.6 0.9 %copy-done.2 = bf16[2,256,128]{2,1,0:T(8,128)(2,1)S(1)} copy-done((bf16[2,256,128]{2,1,0:T(8,128)(2,1)S(1)}, bf16[2,256,128]{2,1,0:T(8,128)(2,1)}, u32[]{:S(2)}) %copy-start.2) | copy-done | bytes 131096
  16.5 0.0 copy-start.3
  16.5 0.7 %copy-done.3 = bf16[2,256,8]{1,2,0:T(8,128)(2,1)S(1)} copy-done((bf16[2,256,8]{1,2,0:T(8,128)(2,1)S(1)}, bf16[2,256,8]{1,2,0:T(8,128)(2,1)}, u32[]{:S(2)}) %copy-start.3) | copy-done | bytes 8216
  17.2 0.0 copy-start.4
  17.2 0.7 %copy-done.4 = f32[2,512]{1,0:T(2,128)S(1)} copy-done((f32[2,512]{1,0:T(2,128)S(1)}, f32[2,512]{1,0:T(2,128)}, u32[]{:S(2)}) %copy-start.4) | copy-done | bytes 4120
  17.9 0.0 copy-start.5
  17.9 0.7 %copy-done.5 = f32[2,256]{1,0:T(2,128)S(1)} copy-done((f32[2,256]{1,0:T(2,128)S(1)}, f32[2,256]{1,0:T(2,128)}, u32[]{:S(2)}) %copy-start.5) | copy-done | bytes 2072
  18.6 0.0 copy-start.6
  18.6 0.7 %copy-done.6 = f32[2,8]{1,0:T(2,128)S(1)} copy-done((f32[2,8]{1,0:T(2,128)S(1)}, f32[2,8]{1,0:T(2,128)}, u32[]{:S(2)}) %copy-start.6) | copy-done | bytes 88
  19.2 0.0 copy-start.7
  19.2 0.7 %copy-done.7 = f32[2,8]{1,0:T(2,128)S(1)} copy-done((f32[2,8]{1,0:T(2,128)S(1)}, f32[2,8]{1,0:T(2,128)}, u32[]{:S(2)}) %copy-start.7) | copy-done | bytes 88
  19.9 0.6 prepare_weights.1
  20.5 2.6 %all-to-all-done = bf16[32,16,256]{2,1,0:T(8,128)(2,1)S(1)} async-done(((bf16[32,16,256]{2,1,0:T(8,128)(2,1)}), bf16[32,16,256]{2,1,0:T(8,128)(2,1)S(1)}, u32[]{:S(2)}, u32[]{:S(2)}) %all-to-all-start) | async-done | bytes 262176 | tf_op jit(solution)/shard_map/all_to_all | solution.py:365
  23.1 2.1 %mix_layer_0.1 = bf16[1024,128]{1,0:T(8,128)(2,1)S(1)} custom-call(bf16[512,256]{1,0:T(8,128)(2,1)S(1)} %bitcast.6, bf16[2,1168,256]{2,1,0:T(8,128)(2,1)S(1)} %get-tuple-element.8.weights_ref, bf16[2,512,256]{2,1,0:T(8,128)(2,1)S(1)} %get-tuple-element.9.out_w_ref, f32[2,24,512]{2,1,0:T(8,128)S(1)} %get-tuple-element.10.small_ref), custom_call_target="tpu_custom_call" | custom-call | tf_op jit(solution)/shard_map/mix_layer_0/pallas_call | solution.py:346
  25.2 26.9 %all_to_all.15 = bf16[256,4,128]{2,1,0:T(4,128)(2,1)S(1)} all-to-all(bf16[256,4,128]{2,1,0:T(4,128)(2,1)S(1)} %bitcast.9), channel_id=1, replica_groups={{7,6,5,4,3,2,1,0,15,14,13,12,11,10,9,8,23,22,21,20,19,18,17,16,31,30,29..., dimensions={0} | all-to-all | bytes 524288 | tf_op jit(solution)/shard_map/all_to_all | solution.py:369
  52.1 2.3 %mix_layer_1.1 = bf16[512,256]{1,0:T(8,128)(2,1)S(1)} custom-call(bf16[1024,128]{1,0:T(8,128)(2,1)S(1)} %bitcast.7, bf16[2,1168,256]{2,1,0:T(8,128)(2,1)S(1)} %get-tuple-element.8.weights_ref, bf16[2,512,256]{2,1,0:T(8,128)(2,1)S(1)} %get-tuple-element.9.out_w_ref, f32[2,24,512]{2,1,0:T(8,128)S(1)} %get-tuple-element.10.small_ref), custom_call_target="tpu_custom_call" | custom-call | tf_op jit(solution)/shard_map/mix_layer_1/pallas_call | solution.py:346
  54.4 8.9 %all_to_all.16 = bf16[8,64,256]{2,1,0:T(8,128)(2,1)S(1)} all-to-all(bf16[8,64,256]{2,1,0:T(8,128)(2,1)S(1)} %bitcast.8), channel_id=1, replica_groups={{7,6,5,4,3,2,1,0},{15,14,13,12,11,10,9,8},{23,22,21,20,19,18,17,16},{31..., dimensions={0} | all-to-all | bytes 524288 | tf_op jit(solution)/shard_map/all_to_all | solution.py:378
  63.3 0.7 %copy.11 = bf16[8,64,256]{2,1,0:T(8,128)(2,1)} copy(bf16[8,64,256]{2,1,0:T(8,128)(2,1)S(1)} %all_to_all.16) | data formatting | bytes 524288
Async XLA Ops:
  0.0 14.5 %copy-start = (bf16[2,256,1024]{2,1,0:T(8,128)(2,1)S(1)}, bf16[2,256,1024]{2,1,0:T(8,128)(2,1)}, u32[]{:S(2)}) copy-start(bf16[2,256,1024]{2,1,0:T(8,128)(2,1)} %inner_ref.1) | copy-start | bytes 3145732
  1.8 21.3 %all-to-all-start = ((bf16[32,16,256]{2,1,0:T(8,128)(2,1)}), bf16[32,16,256]{2,1,0:T(8,128)(2,1)S(1)}, u32[]{:S(2)}, u32[]{:S(2)}) async-start(bf16[32,16,256]{2,1,0:T(8,128)(2,1)} %bitcast.11), calls=%async_computation | async-start | bytes 524288 | tf_op jit(solution)/shard_map/all_to_all | solution.py:365
  14.6 1.0 %copy-start.1 = (bf16[2,512,256]{2,1,0:T(8,128)(2,1)S(1)}, bf16[2,512,256]{2,1,0:T(8,128)(2,1)}, u32[]{:S(2)}) copy-start(bf16[2,512,256]{2,1,0:T(8,128)(2,1)} %out_w_ref.1) | copy-start | bytes 1572868
  15.6 0.9 %copy-start.2 = (bf16[2,256,128]{2,1,0:T(8,128)(2,1)S(1)}, bf16[2,256,128]{2,1,0:T(8,128)(2,1)}, u32[]{:S(2)}) copy-start(bf16[2,256,128]{2,1,0:T(8,128)(2,1)} %state_ref.1) | copy-start | bytes 393220
  16.5 0.7 %copy-start.3 = (bf16[2,256,8]{1,2,0:T(8,128)(2,1)S(1)}, bf16[2,256,8]{1,2,0:T(8,128)(2,1)}, u32[]{:S(2)}) copy-start(bf16[2,256,8]{1,2,0:T(8,128)(2,1)} %param.13) | copy-start | bytes 24580
  17.2 0.7 %copy-start.4 = (f32[2,512]{1,0:T(2,128)S(1)}, f32[2,512]{1,0:T(2,128)}, u32[]{:S(2)}) copy-start(f32[2,512]{1,0:T(2,128)} %gain_ref.1) | copy-start | bytes 12292
  17.9 0.7 %copy-start.5 = (f32[2,256]{1,0:T(2,128)S(1)}, f32[2,256]{1,0:T(2,128)}, u32[]{:S(2)}) copy-start(f32[2,256]{1,0:T(2,128)} %norm_ref.1) | copy-start | bytes 6148
  18.6 0.7 %copy-start.6 = (f32[2,8]{1,0:T(2,128)S(1)}, f32[2,8]{1,0:T(2,128)}, u32[]{:S(2)}) copy-start(f32[2,8]{1,0:T(2,128)} %bias_ref.1) | copy-start | bytes 196
  19.2 0.7 %copy-start.7 = (f32[2,8]{1,0:T(2,128)S(1)}, f32[2,8]{1,0:T(2,128)}, u32[]{:S(2)}) copy-start(f32[2,8]{1,0:T(2,128)} %rate_ref.1) | copy-start | bytes 196

commit v9 on v8

--- a/solution.py
+++ b/solution.py
@@ -168,16 +168,16 @@
     tokens = x_ref.size // width
     chunks = tokens // CHUNK
     per_line = chunks // lines
+    gx, gy = grid
     h = x_ref[...].astype(F32)
     if not interleaved:
-        gx, gy = grid
         pair = tokens // (gx * gy)
         mixed_ref[...] = h
         for part in range(parts):
             for l in range(pair):
                 found = mixed_ref[pl.ds(l * parts + part, gx * gy, stride=pair * parts), :]
-                found = backwards(found.reshape(gx, gy, 128))
-                found = backwards(jnp.swapaxes(found, 0, 1)).reshape(gx * gy, 128)
+                found = jnp.swapaxes(found.reshape(gx, gy, 128), 0, 1)
+                found = backwards(found).reshape(gx * gy, 128)
                 sorted_ref[pl.ds(part * tokens + l, gx * gy, stride=pair), :] = found
         h = jnp.concatenate(
             [sorted_ref[part * tokens : part * tokens + tokens, :] for part in range(parts)], 1
@@ -329,9 +329,12 @@
         result = h[span(k)] + change * jnp.concatenate([scales[k]] * parts, 1)
         if interleaved:
             line, first_x = k // per_line, CHUNK * (k % per_line)
-            for part in range(parts):
-                target = pl.ds((lines * first_x + line) * parts + part, CHUNK, stride=lines * parts)
-                mixed_ref[target, :] = result[:, span(part)]
+            size = tokens // (lines * gx)
+            for i in range(CHUNK // size):
+                x = size * (gx - 1 - (first_x // size + i))
+                for part in range(parts):
+                    target = pl.ds((lines * x + line) * parts + part, size, stride=lines * parts)
+                    mixed_ref[target, :] = result[size * i : size * i + size, span(part)]
         else:
             result = result.astype(BF16)
             size = tokens // gy
@@ -365,7 +368,7 @@
     taken = lax.all_to_all(sent, "gx", 0, 0, tiled=True, axis_index_groups=falling_x)
     taken = taken.reshape(tokens, width)
     stream = mix(taken, 0, lines, (gx, gy), (2 * tokens, width // 2), weights)
-    owners = [[gy * (x // gy) + gy - 1 - x % gy for x in range(gx * nx)]]
+    owners = [list(reversed(range(gx * gy)))]
     taken = lax.all_to_all(
         stream.reshape(gx * nx, -1, width // 2),
         ("gx", "gy"),

time: 64.4 us -> 63.8 us (level)
  blocking collectives: 35.8 us -> 34.9 us
where the time goes in v9:
time: 63.8 us; the launch traced here: 63.1 us
  blocking collectives  34.9 us (55%)
  starting transfers between devices  12.8 us (20%)
  Pallas kernels  6.66 us (10%)
  local copies, waits for them, and re-layouts  6.07 us (10%)
  waiting for transfers between devices  2.62 us (4%)
    all_to_all x1, blocking collectives, on_device(): lax.all_to_all(stream.reshape(gx * nx, -1, width // 2), ('gx', 'gy'), 0,...  26.4 us
    all_to_all x1, starting transfers between devices, on_device(): lax.all_to_all(sent, 'gx', 0, 0, tiled=True, axis_index_groups=falling_x)  12.8 us
    all_to_all x1, blocking collectives, on_device(): lax.all_to_all(stream.reshape(gy, ny, width), 'gy', 0, 0, tiled=True, axi...  8.49 us
    unnamed x17, local copies, waits for them, and re-layouts  6.07 us
    pallas_call x2, Pallas kernels, mix(): pl.pallas_call(functools.partial(layer_kernel, layer, lines, grid), out_s...  4.35 us
    all_to_all x1, waiting for transfers between devices, on_device(): lax.all_to_all(sent, 'gx', 0, 0, tiled=True, axis_index_groups=falling_x)  2.62 us
    pallas_call x1, Pallas kernels, spread(): pl.pallas_call(spread_kernel, out_shape=jax.ShapeDtypeStruct((ny * nx, wi...  1.75 us
  transfers between devices with their start and end apart: 1, of which 1 were waited for; matrix products, arithmetic and copies ran while one was open for 0% of the time, Pallas kernels for 1%

profile of v9, /device:TPU:1, one launch (start us, length us, event | category | flops | bytes accessed | tf_op | source)
XLA Modules:
  0.0 63.1 jit_solution(11049733362701410031)
XLA Ops:
  0.0 0.0 copy-start
  0.0 1.8 %spread_field.1 = bf16[512,256]{1,0:T(8,128)(2,1)} custom-call(bf16[8,64,256]{2,1,0:T(8,128)(2,1)} %field_ref.1), custom_call_target="tpu_custom_call" | custom-call | tf_op jit(solution)/shard_map/spread_field/pallas_call | solution.py:91
  1.8 12.8 %all-to-all-start = ((bf16[32,16,256]{2,1,0:T(8,128)(2,1)}), bf16[32,16,256]{2,1,0:T(8,128)(2,1)S(1)}, u32[]{:S(2)}, u32[]{:S(2)}) async-start(bf16[32,16,256]{2,1,0:T(8,128)(2,1)} %bitcast.11), calls=%async_computation | async-start | bytes 524288 | tf_op jit(solution)/shard_map/all_to_all | solution.py:368
  14.5 0.0 copy-done
  14.6 0.0 copy-start.1
  14.6 1.0 %copy-done.1 = bf16[2,512,256]{2,1,0:T(8,128)(2,1)S(1)} copy-done((bf16[2,512,256]{2,1,0:T(8,128)(2,1)S(1)}, bf16[2,512,256]{2,1,0:T(8,128)(2,1)}, u32[]{:S(2)}) %copy-start.1) | copy-done | bytes 524312
  15.6 0.0 copy-start.2
  15.6 0.9 %copy-done.2 = bf16[2,256,128]{2,1,0:T(8,128)(2,1)S(1)} copy-done((bf16[2,256,128]{2,1,0:T(8,128)(2,1)S(1)}, bf16[2,256,128]{2,1,0:T(8,128)(2,1)}, u32[]{:S(2)}) %copy-start.2) | copy-done | bytes 131096
  16.5 0.0 copy-start.3
  16.5 0.7 %copy-done.3 = bf16[2,256,8]{1,2,0:T(8,128)(2,1)S(1)} copy-done((bf16[2,256,8]{1,2,0:T(8,128)(2,1)S(1)}, bf16[2,256,8]{1,2,0:T(8,128)(2,1)}, u32[]{:S(2)}) %copy-start.3) | copy-done | bytes 8216
  17.2 0.0 copy-start.4
  17.2 0.7 %copy-done.4 = f32[2,512]{1,0:T(2,128)S(1)} copy-done((f32[2,512]{1,0:T(2,128)S(1)}, f32[2,512]{1,0:T(2,128)}, u32[]{:S(2)}) %copy-start.4) | copy-done | bytes 4120
  17.9 0.0 copy-start.5
  17.9 0.7 %copy-done.5 = f32[2,256]{1,0:T(2,128)S(1)} copy-done((f32[2,256]{1,0:T(2,128)S(1)}, f32[2,256]{1,0:T(2,128)}, u32[]{:S(2)}) %copy-start.5) | copy-done | bytes 2072
  18.6 0.0 copy-start.6
  18.6 0.7 %copy-done.6 = f32[2,8]{1,0:T(2,128)S(1)} copy-done((f32[2,8]{1,0:T(2,128)S(1)}, f32[2,8]{1,0:T(2,128)}, u32[]{:S(2)}) %copy-start.6) | copy-done | bytes 88
  19.2 0.0 copy-start.7
  19.2 0.7 %copy-done.7 = f32[2,8]{1,0:T(2,128)S(1)} copy-done((f32[2,8]{1,0:T(2,128)S(1)}, f32[2,8]{1,0:T(2,128)}, u32[]{:S(2)}) %copy-start.7) | copy-done | bytes 88
  19.9 0.6 prepare_weights.1
  20.5 2.6 %all-to-all-done = bf16[32,16,256]{2,1,0:T(8,128)(2,1)S(1)} async-done(((bf16[32,16,256]{2,1,0:T(8,128)(2,1)}), bf16[32,16,256]{2,1,0:T(8,128)(2,1)S(1)}, u32[]{:S(2)}, u32[]{:S(2)}) %all-to-all-start) | async-done | bytes 262176 | tf_op jit(solution)/shard_map/all_to_all | solution.py:368
  23.1 2.1 %mix_layer_0.1 = bf16[1024,128]{1,0:T(8,128)(2,1)S(1)} custom-call(bf16[512,256]{1,0:T(8,128)(2,1)S(1)} %bitcast.6, bf16[2,1168,256]{2,1,0:T(8,128)(2,1)S(1)} %get-tuple-element.8.weights_ref, bf16[2,512,256]{2,1,0:T(8,128)(2,1)S(1)} %get-tuple-element.9.out_w_ref, f32[2,24,512]{2,1,0:T(8,128)S(1)} %get-tuple-element.10.small_ref), custom_call_target="tpu_custom_call" | custom-call | tf_op jit(solution)/shard_map/mix_layer_0/pallas_call | solution.py:349
  25.2 26.4 %all_to_all.15 = bf16[256,4,128]{2,1,0:T(4,128)(2,1)S(1)} all-to-all(bf16[256,4,128]{2,1,0:T(4,128)(2,1)S(1)} %bitcast.9), channel_id=1, replica_groups={{255,254,253,252,251,250,249,248,247,246,245,244,243,242,241,240,239,23..., dimensions={0} | all-to-all | bytes 524288 | tf_op jit(solution)/shard_map/all_to_all | solution.py:372
  51.6 2.3 %mix_layer_1.1 = bf16[512,256]{1,0:T(8,128)(2,1)S(1)} custom-call(bf16[1024,128]{1,0:T(8,128)(2,1)S(1)} %bitcast.7, bf16[2,1168,256]{2,1,0:T(8,128)(2,1)S(1)} %get-tuple-element.8.weights_ref, bf16[2,512,256]{2,1,0:T(8,128)(2,1)S(1)} %get-tuple-element.9.out_w_ref, f32[2,24,512]{2,1,0:T(8,128)S(1)} %get-tuple-element.10.small_ref), custom_call_target="tpu_custom_call" | custom-call | tf_op jit(solution)/shard_map/mix_layer_1/pallas_call | solution.py:349
  53.9 8.5 %all_to_all.16 = bf16[8,64,256]{2,1,0:T(8,128)(2,1)S(1)} all-to-all(bf16[8,64,256]{2,1,0:T(8,128)(2,1)S(1)} %bitcast.8), channel_id=1, replica_groups={{7,6,5,4,3,2,1,0},{15,14,13,12,11,10,9,8},{23,22,21,20,19,18,17,16},{31..., dimensions={0} | all-to-all | bytes 524288 | tf_op jit(solution)/shard_map/all_to_all | solution.py:381
  62.4 0.7 %copy.11 = bf16[8,64,256]{2,1,0:T(8,128)(2,1)} copy(bf16[8,64,256]{2,1,0:T(8,128)(2,1)S(1)} %all_to_all.16) | data formatting | bytes 524288
Async XLA Ops:
  0.0 14.5 %copy-start = (bf16[2,256,1024]{2,1,0:T(8,128)(2,1)S(1)}, bf16[2,256,1024]{2,1,0:T(8,128)(2,1)}, u32[]{:S(2)}) copy-start(bf16[2,256,1024]{2,1,0:T(8,128)(2,1)} %inner_ref.1) | copy-start | bytes 3145732
  1.8 21.3 %all-to-all-start = ((bf16[32,16,256]{2,1,0:T(8,128)(2,1)}), bf16[32,16,256]{2,1,0:T(8,128)(2,1)S(1)}, u32[]{:S(2)}, u32[]{:S(2)}) async-start(bf16[32,16,256]{2,1,0:T(8,128)(2,1)} %bitcast.11), calls=%async_computation | async-start | bytes 524288 | tf_op jit(solution)/shard_map/all_to_all | solution.py:368
  14.6 1.0 %copy-start.1 = (bf16[2,512,256]{2,1,0:T(8,128)(2,1)S(1)}, bf16[2,512,256]{2,1,0:T(8,128)(2,1)}, u32[]{:S(2)}) copy-start(bf16[2,512,256]{2,1,0:T(8,128)(2,1)} %out_w_ref.1) | copy-start | bytes 1572868
  15.6 0.9 %copy-start.2 = (bf16[2,256,128]{2,1,0:T(8,128)(2,1)S(1)}, bf16[2,256,128]{2,1,0:T(8,128)(2,1)}, u32[]{:S(2)}) copy-start(bf16[2,256,128]{2,1,0:T(8,128)(2,1)} %state_ref.1) | copy-start | bytes 393220
  16.5 0.7 %copy-start.3 = (bf16[2,256,8]{1,2,0:T(8,128)(2,1)S(1)}, bf16[2,256,8]{1,2,0:T(8,128)(2,1)}, u32[]{:S(2)}) copy-start(bf16[2,256,8]{1,2,0:T(8,128)(2,1)} %param.13) | copy-start | bytes 24580
  17.2 0.7 %copy-start.4 = (f32[2,512]{1,0:T(2,128)S(1)}, f32[2,512]{1,0:T(2,128)}, u32[]{:S(2)}) copy-start(f32[2,512]{1,0:T(2,128)} %gain_ref.1) | copy-start | bytes 12292
  17.9 0.7 %copy-start.5 = (f32[2,256]{1,0:T(2,128)S(1)}, f32[2,256]{1,0:T(2,128)}, u32[]{:S(2)}) copy-start(f32[2,256]{1,0:T(2,128)} %norm_ref.1) | copy-start | bytes 6148
  18.6 0.7 %copy-start.6 = (f32[2,8]{1,0:T(2,128)S(1)}, f32[2,8]{1,0:T(2,128)}, u32[]{:S(2)}) copy-start(f32[2,8]{1,0:T(2,128)} %bias_ref.1) | copy-start | bytes 196
  19.2 0.7 %copy-start.7 = (f32[2,8]{1,0:T(2,128)S(1)}, f32[2,8]{1,0:T(2,128)}, u32[]{:S(2)}) copy-start(f32[2,8]{1,0:T(2,128)} %rate_ref.1) | copy-start | bytes 196

commit v10 on v9

--- a/solution.py
+++ b/solution.py
@@ -231,7 +231,7 @@
 
     s_pos, t_pos = positions(CHUNK, CHUNK)
     double = jnp.where(s_pos == t_pos, 2.0, 1.0)
-    falling = jnp.where(s_pos < t_pos, -1.0, 1.0)
+    falling = jnp.where(s_pos < t_pos, -1.0, 1.0).astype(BF16)
     ahead_half = t_pos < ORDER
 
     def span(k):
@@ -306,7 +306,7 @@
             rights = []
             for row in (HEADS * k + 2 * pair, HEADS * k + 2 * pair + 1):
                 gap = mid2_columns[:, row : row + 1] - mid2[row : row + 1]
-                mixing = scores * jnp.exp2(gap * falling).astype(BF16)
+                mixing = scores * jnp.exp2(gap.astype(BF16) * falling)
                 rights.append(
                     jnp.concatenate(
                         [

time: 63.8 us -> 63.7 us (level)
  no operation moved by 1% of the time
where the time goes in v10:
time: 63.7 us; the launch traced here: 63.1 us
  blocking collectives  34.9 us (55%)
  starting transfers between devices  12.8 us (20%)
  Pallas kernels  6.63 us (10%)
  local copies, waits for them, and re-layouts  6.07 us (10%)
  waiting for transfers between devices  2.62 us (4%)
    all_to_all x1, blocking collectives, on_device(): lax.all_to_all(stream.reshape(gx * nx, -1, width // 2), ('gx', 'gy'), 0,...  26.4 us
    all_to_all x1, starting transfers between devices, on_device(): lax.all_to_all(sent, 'gx', 0, 0, tiled=True, axis_index_groups=falling_x)  12.8 us
    all_to_all x1, blocking collectives, on_device(): lax.all_to_all(stream.reshape(gy, ny, width), 'gy', 0, 0, tiled=True, axi...  8.49 us
    unnamed x17, local copies, waits for them, and re-layouts  6.07 us
    pallas_call x2, Pallas kernels, mix(): pl.pallas_call(functools.partial(layer_kernel, layer, lines, grid), out_s...  4.32 us
    all_to_all x1, waiting for transfers between devices, on_device(): lax.all_to_all(sent, 'gx', 0, 0, tiled=True, axis_index_groups=falling_x)  2.62 us
    pallas_call x1, Pallas kernels, spread(): pl.pallas_call(spread_kernel, out_shape=jax.ShapeDtypeStruct((ny * nx, wi...  1.75 us
  transfers between devices with their start and end apart: 1, of which 1 were waited for; matrix products, arithmetic and copies ran while one was open for 0% of the time, Pallas kernels for 1%

profile of v10, /device:TPU:1, one launch (start us, length us, event | category | flops | bytes accessed | tf_op | source)
XLA Modules:
  0.0 63.1 jit_solution(16739498095661838082)
XLA Ops:
  0.0 0.0 copy-start
  0.0 1.8 %spread_field.1 = bf16[512,256]{1,0:T(8,128)(2,1)} custom-call(bf16[8,64,256]{2,1,0:T(8,128)(2,1)} %field_ref.1), custom_call_target="tpu_custom_call" | custom-call | tf_op jit(solution)/shard_map/spread_field/pallas_call | solution.py:91
  1.8 12.8 %all-to-all-start = ((bf16[32,16,256]{2,1,0:T(8,128)(2,1)}), bf16[32,16,256]{2,1,0:T(8,128)(2,1)S(1)}, u32[]{:S(2)}, u32[]{:S(2)}) async-start(bf16[32,16,256]{2,1,0:T(8,128)(2,1)} %bitcast.11), calls=%async_computation | async-start | bytes 524288 | tf_op jit(solution)/shard_map/all_to_all | solution.py:368
  14.5 0.0 copy-done
  14.6 0.0 copy-start.1
  14.6 1.0 %copy-done.1 = bf16[2,512,256]{2,1,0:T(8,128)(2,1)S(1)} copy-done((bf16[2,512,256]{2,1,0:T(8,128)(2,1)S(1)}, bf16[2,512,256]{2,1,0:T(8,128)(2,1)}, u32[]{:S(2)}) %copy-start.1) | copy-done | bytes 524312
  15.6 0.0 copy-start.2
  15.6 0.9 %copy-done.2 = bf16[2,256,128]{2,1,0:T(8,128)(2,1)S(1)} copy-done((bf16[2,256,128]{2,1,0:T(8,128)(2,1)S(1)}, bf16[2,256,128]{2,1,0:T(8,128)(2,1)}, u32[]{:S(2)}) %copy-start.2) | copy-done | bytes 131096
  16.5 0.0 copy-start.3
  16.5 0.7 %copy-done.3 = bf16[2,256,8]{1,2,0:T(8,128)(2,1)S(1)} copy-done((bf16[2,256,8]{1,2,0:T(8,128)(2,1)S(1)}, bf16[2,256,8]{1,2,0:T(8,128)(2,1)}, u32[]{:S(2)}) %copy-start.3) | copy-done | bytes 8216
  17.2 0.0 copy-start.4
  17.2 0.7 %copy-done.4 = f32[2,512]{1,0:T(2,128)S(1)} copy-done((f32[2,512]{1,0:T(2,128)S(1)}, f32[2,512]{1,0:T(2,128)}, u32[]{:S(2)}) %copy-start.4) | copy-done | bytes 4120
  17.9 0.0 copy-start.5
  17.9 0.7 %copy-done.5 = f32[2,256]{1,0:T(2,128)S(1)} copy-done((f32[2,256]{1,0:T(2,128)S(1)}, f32[2,256]{1,0:T(2,128)}, u32[]{:S(2)}) %copy-start.5) | copy-done | bytes 2072
  18.6 0.0 copy-start.6
  18.6 0.7 %copy-done.6 = f32[2,8]{1,0:T(2,128)S(1)} copy-done((f32[2,8]{1,0:T(2,128)S(1)}, f32[2,8]{1,0:T(2,128)}, u32[]{:S(2)}) %copy-start.6) | copy-done | bytes 88
  19.2 0.0 copy-start.7
  19.2 0.7 %copy-done.7 = f32[2,8]{1,0:T(2,128)S(1)} copy-done((f32[2,8]{1,0:T(2,128)S(1)}, f32[2,8]{1,0:T(2,128)}, u32[]{:S(2)}) %copy-start.7) | copy-done | bytes 88
  19.9 0.6 prepare_weights.1
  20.5 2.6 %all-to-all-done = bf16[32,16,256]{2,1,0:T(8,128)(2,1)S(1)} async-done(((bf16[32,16,256]{2,1,0:T(8,128)(2,1)}), bf16[32,16,256]{2,1,0:T(8,128)(2,1)S(1)}, u32[]{:S(2)}, u32[]{:S(2)}) %all-to-all-start) | async-done | bytes 262176 | tf_op jit(solution)/shard_map/all_to_all | solution.py:368
  23.1 2.1 %mix_layer_0.1 = bf16[1024,128]{1,0:T(8,128)(2,1)S(1)} custom-call(bf16[512,256]{1,0:T(8,128)(2,1)S(1)} %bitcast.6, bf16[2,1168,256]{2,1,0:T(8,128)(2,1)S(1)} %get-tuple-element.8.weights_ref, bf16[2,512,256]{2,1,0:T(8,128)(2,1)S(1)} %get-tuple-element.9.out_w_ref, f32[2,24,512]{2,1,0:T(8,128)S(1)} %get-tuple-element.10.small_ref), custom_call_target="tpu_custom_call" | custom-call | tf_op jit(solution)/shard_map/mix_layer_0/pallas_call | solution.py:349
  25.2 26.4 %all_to_all.15 = bf16[256,4,128]{2,1,0:T(4,128)(2,1)S(1)} all-to-all(bf16[256,4,128]{2,1,0:T(4,128)(2,1)S(1)} %bitcast.9), channel_id=1, replica_groups={{255,254,253,252,251,250,249,248,247,246,245,244,243,242,241,240,239,23..., dimensions={0} | all-to-all | bytes 524288 | tf_op jit(solution)/shard_map/all_to_all | solution.py:372
  51.6 2.2 %mix_layer_1.1 = bf16[512,256]{1,0:T(8,128)(2,1)S(1)} custom-call(bf16[1024,128]{1,0:T(8,128)(2,1)S(1)} %bitcast.7, bf16[2,1168,256]{2,1,0:T(8,128)(2,1)S(1)} %get-tuple-element.8.weights_ref, bf16[2,512,256]{2,1,0:T(8,128)(2,1)S(1)} %get-tuple-element.9.out_w_ref, f32[2,24,512]{2,1,0:T(8,128)S(1)} %get-tuple-element.10.small_ref), custom_call_target="tpu_custom_call" | custom-call | tf_op jit(solution)/shard_map/mix_layer_1/pallas_call | solution.py:349
  53.9 8.5 %all_to_all.16 = bf16[8,64,256]{2,1,0:T(8,128)(2,1)S(1)} all-to-all(bf16[8,64,256]{2,1,0:T(8,128)(2,1)S(1)} %bitcast.8), channel_id=1, replica_groups={{7,6,5,4,3,2,1,0},{15,14,13,12,11,10,9,8},{23,22,21,20,19,18,17,16},{31..., dimensions={0} | all-to-all | bytes 524288 | tf_op jit(solution)/shard_map/all_to_all | solution.py:381
  62.4 0.7 %copy.11 = bf16[8,64,256]{2,1,0:T(8,128)(2,1)} copy(bf16[8,64,256]{2,1,0:T(8,128)(2,1)S(1)} %all_to_all.16) | data formatting | bytes 524288
Async XLA Ops:
  0.0 14.5 %copy-start = (bf16[2,256,1024]{2,1,0:T(8,128)(2,1)S(1)}, bf16[2,256,1024]{2,1,0:T(8,128)(2,1)}, u32[]{:S(2)}) copy-start(bf16[2,256,1024]{2,1,0:T(8,128)(2,1)} %inner_ref.1) | copy-start | bytes 3145732
  1.8 21.3 %all-to-all-start = ((bf16[32,16,256]{2,1,0:T(8,128)(2,1)}), bf16[32,16,256]{2,1,0:T(8,128)(2,1)S(1)}, u32[]{:S(2)}, u32[]{:S(2)}) async-start(bf16[32,16,256]{2,1,0:T(8,128)(2,1)} %bitcast.11), calls=%async_computation | async-start | bytes 524288 | tf_op jit(solution)/shard_map/all_to_all | solution.py:368
  14.6 1.0 %copy-start.1 = (bf16[2,512,256]{2,1,0:T(8,128)(2,1)S(1)}, bf16[2,512,256]{2,1,0:T(8,128)(2,1)}, u32[]{:S(2)}) copy-start(bf16[2,512,256]{2,1,0:T(8,128)(2,1)} %out_w_ref.1) | copy-start | bytes 1572868
  15.6 0.9 %copy-start.2 = (bf16[2,256,128]{2,1,0:T(8,128)(2,1)S(1)}, bf16[2,256,128]{2,1,0:T(8,128)(2,1)}, u32[]{:S(2)}) copy-start(bf16[2,256,128]{2,1,0:T(8,128)(2,1)} %state_ref.1) | copy-start | bytes 393220
  16.5 0.7 %copy-start.3 = (bf16[2,256,8]{1,2,0:T(8,128)(2,1)S(1)}, bf16[2,256,8]{1,2,0:T(8,128)(2,1)}, u32[]{:S(2)}) copy-start(bf16[2,256,8]{1,2,0:T(8,128)(2,1)} %param.13) | copy-start | bytes 24580
  17.2 0.7 %copy-start.4 = (f32[2,512]{1,0:T(2,128)S(1)}, f32[2,512]{1,0:T(2,128)}, u32[]{:S(2)}) copy-start(f32[2,512]{1,0:T(2,128)} %gain_ref.1) | copy-start | bytes 12292
  17.9 0.7 %copy-start.5 = (f32[2,256]{1,0:T(2,128)S(1)}, f32[2,256]{1,0:T(2,128)}, u32[]{:S(2)}) copy-start(f32[2,256]{1,0:T(2,128)} %norm_ref.1) | copy-start | bytes 6148
  18.6 0.7 %copy-start.6 = (f32[2,8]{1,0:T(2,128)S(1)}, f32[2,8]{1,0:T(2,128)}, u32[]{:S(2)}) copy-start(f32[2,8]{1,0:T(2,128)} %bias_ref.1) | copy-start | bytes 196
  19.2 0.7 %copy-start.7 = (f32[2,8]{1,0:T(2,128)S(1)}, f32[2,8]{1,0:T(2,128)}, u32[]{:S(2)}) copy-start(f32[2,8]{1,0:T(2,128)} %rate_ref.1) | copy-start | bytes 196
